TPU v7x, 32 devices: a whole 2x2x4 slice. The times are simulated.
32 devices in a mesh: cfg: 2 (over x), space: 8 (over z, y), diag: 2 (over core).
Axes of the slice: x: 2, y: 2, z: 4, core: 2. Of those that a mesh axis runs over, the one named last changes fastest.
Arguments:
- eigvecs: bfloat16 [8, 2, 3, 128, 16, 256], P('cfg', None, None, None, ('space', 'diag')), parts along dimension 0, may hold values from -6 to 6
- gauge_links: float32 [8, 3, 2, 3, 3, 16, 256], P('cfg', None, None, None, None, ('space', 'diag')), parts along dimension 0, may hold values from -6 to 6
- momenta: int32 [4, 3], replicated, may hold values from -2 to 2
- spin_mix: float32 [16, 4, 4], replicated, may hold values from -4 to 4
- perambulators: bfloat16 [64, 4, 2, 128, 512], P(('cfg', 'space', 'diag')), parts along dimension 0, may hold values from -0.375 to 0.375
- contraction_list: int32 [32, 3], P(('space', 'diag')), may hold values from 0 to 63, as said below
Outputs:
- diagrams: bfloat16 [64, 4, 2, 128, 512], P(('cfg', 'space', 'diag')), parts along dimension 0
There are 2 independent parts, one for each index of `cfg`. A program takes and returns all parts, laid end to end along the dimension named above; an argument that names none is the same for every part. Nothing has to cross between parts.
Inputs may be any that keep to these rules, and one draw needn't show every extreme that they name: `contraction_list`: row j is one diagram. Column 0 is an elemental item below 64, column 1 a spin structure below 16, column 2 a perambulator q with q // 2 == j // 2; each aligned group of 2 rows names each of its 2 perambulators exactly once.
All inputs are finite; a program needn't handle non-finite values.
Results may differ from a plain program's by a relative error of at most 0.0064.
Values may be sent and summed in bfloat16 or wider, within the bound.
No kernel may reach another device: no remote copies, remote signals or barrier semaphores. Data moves between devices by JAX's collectives and lax.ppermute only.
A program may use at most 128 MiB of HBM per device.

v0:
```python
import functools
import math

import jax
import jax.numpy as jnp
from jax import lax
from jax.experimental import pallas as pl
from jax.experimental.pallas import tpu as pltpu
from jax.sharding import PartitionSpec as P

NCOL = 3
NMOM = 4
NDISP = 4
LX = 16
LY = 16
LANES = 128
ROWS = 16
SITES = ("space", "diag")
MIB = 1024 * 1024
PLANE_LIMIT = 20 * MIB


def shifted(value, axis, by):
    size = lax.axis_size(axis)
    return lax.ppermute(value, axis, [(i, (i + by) % size) for i in range(size)])


def in_hbm(value):
    return pltpu.with_memory_space_constraint(value, pltpu.HBM)


def exchanged(value, mask):
    size = lax.axis_size(SITES)
    return lax.ppermute(value, SITES, [(i, i ^ mask) for i in range(size)])


def gathered(rows, early, late):
    bits = lax.axis_size(SITES).bit_length() - 1
    value = rows[None]
    for low in range(0, bits, 2):
        if low == 2:
            value, late = lax.optimization_barrier((value, late))
        arrived = [exchanged(value, step << low) for step in reversed(range(1, 1 << min(2, bits - low)))]
        if low == 0:
            arrived, early = lax.optimization_barrier((arrived, early))
        value = jnp.concatenate([value] + arrived[::-1])
    return value, early, late


def diagonal(value):
    size = value.shape[0]
    same = lax.broadcasted_iota(jnp.int32, value.shape, 0) == lax.broadcasted_iota(jnp.int32, value.shape, 1)
    return jnp.sum(jnp.where(same, value, 0.0), 0, keepdims=True).reshape(1, size)


def rounded(real, imag, left=None):
    planes = [value.astype(jnp.bfloat16) for value in (real, imag)]
    lost = [diagonal(value - plane.astype(jnp.float32)) for value, plane in zip((real, imag), planes)]
    tile = jnp.concatenate(lost + [jnp.zeros((ROWS - 2, real.shape[1]), jnp.float32)], 0)
    if left is not None:
        tile = tile + left
    return planes, tile.astype(jnp.bfloat16)


def store_rounded(ref, index, real, imag, left=None):
    nvec = real.shape[0]
    planes, tile = rounded(real, imag, left)
    ref[(*index, pl.ds(0, nvec))] = planes[0]
    ref[(*index, pl.ds(nvec, nvec))] = planes[1]
    ref[(*index, pl.ds(2 * nvec, ROWS))] = tile


def restored(total):
    nvec = total.shape[1]
    shape = (nvec, nvec)
    same = lax.broadcasted_iota(jnp.int32, shape, 0) == lax.broadcasted_iota(jnp.int32, shape, 1)
    return [
        total[part * nvec : (part + 1) * nvec] + jnp.where(same, total[2 * nvec + part : 2 * nvec + part + 1], 0.0)
        for part in range(2)
    ]


def color_product(matrix, real, imag, adjoint):
    rows = []
    for row in range(NCOL):
        real_part = imag_part = None
        for col in range(NCOL):
            if adjoint:
                mreal, mimag = matrix[0][col][row], matrix[1][col][row]
                one = mreal * real[col] + mimag * imag[col]
                two = mreal * imag[col] - mimag * real[col]
            else:
                mreal, mimag = matrix[0][row][col], matrix[1][row][col]
                one = mreal * real[col] - mimag * imag[col]
                two = mreal * imag[col] + mimag * real[col]
            real_part = one if real_part is None else real_part + one
            imag_part = two if imag_part is None else imag_part + two
        rows.append((real_part, imag_part))
    return rows


def color_loop(link, nvec, width, load, store, adjoint):
    height = math.gcd(nvec, 2 * ROWS)
    for lane in range(0, width, LANES):
        lanes = pl.ds(lane, LANES)
        matrix = [
            [[link(part, row, col, lanes) for col in range(NCOL)] for row in range(NCOL)] for part in range(2)
        ]
        for start in range(0, nvec, height):
            rows = pl.ds(start, height)
            real = [load(0, color, rows, lanes) for color in range(NCOL)]
            imag = [load(1, color, rows, lanes) for color in range(NCOL)]
            for color, (one, two) in enumerate(color_product(matrix, real, imag, adjoint)):
                store(0, color, rows, lanes, one)
                store(1, color, rows, lanes, two)


def fill_tables(position, total_z, plane, momenta_ref, phase_ref, turn_ref):
    width = phase_ref.shape[-1]
    flat = lax.broadcasted_iota(jnp.int32, (1, width), 1)
    xcoord = (flat % LX).astype(jnp.float32)
    ycoord = (flat % plane // LX).astype(jnp.float32)
    zcoord = (position * (width // plane) + flat // plane).astype(jnp.float32)
    for moment in range(NMOM):
        along_x = momenta_ref[moment, 0].astype(jnp.float32)
        along_y = momenta_ref[moment, 1].astype(jnp.float32)
        along_z = momenta_ref[moment, 2].astype(jnp.float32)
        angle = (
            2.0 * math.pi * (along_x * xcoord / LX + along_y * ycoord / LY + along_z * zcoord / total_z)
        )
        phase_ref[moment, 0] = jnp.cos(angle)
        phase_ref[moment, 1] = jnp.sin(angle)
        turn = jnp.full((1, turn_ref.shape[-1]), 2.0 * math.pi / total_z, jnp.float32) * along_z
        turn_ref[moment, 0] = jnp.cos(turn)
        turn_ref[moment, 1] = jnp.sin(turn)


def fill_moves(move_ref):
    width = move_ref.shape[-1]
    source = lax.broadcasted_iota(jnp.int32, (width, width), 0)
    site = lax.broadcasted_iota(jnp.int32, (width, width), 1)
    xcoord = site % LX
    ycoord = site // LX % LY
    for sign, by in enumerate((1, -1)):
        along_x = site - xcoord + (xcoord + LX + by) % LX
        along_y = site + ((ycoord + LY + by) % LY - ycoord) * LX
        move_ref[0, sign] = (source == along_x).astype(jnp.float32).astype(jnp.bfloat16)
        move_ref[1, sign] = (source == along_y).astype(jnp.float32).astype(jnp.bfloat16)


def plane_kernel(
    total_z, plane, scale,
    position_ref, momenta_in, vector_in, link_in,
    item_ref, own_ref, phase_ref, turn_ref,
    momenta_ref, vector_ref, link_ref,
    ahead_x_ref, ahead_y_ref, behind_x_ref, behind_y_ref, adjoint_x_ref, adjoint_y_ref,
    phased_ref, still_ref, moved_x_ref, moved_y_ref, move_ref, momenta_sem, sems,
):
    now = pl.program_id(0)
    slices, _, _, nvec, width = vector_ref.shape

    def copies(index):
        return (
            pltpu.make_async_copy(vector_in.at[index], vector_ref.at[index], sems.at[0, index]),
            pltpu.make_async_copy(link_in.at[index], link_ref.at[index], sems.at[1, index]),
        )

    @pl.when(now == 0)
    def _():
        moments = pltpu.make_async_copy(momenta_in, momenta_ref, momenta_sem)
        moments.start()
        for index in range(slices):
            for copy in copies(index):
                copy.start()
        fill_moves(move_ref)
        moments.wait()
        fill_tables(position_ref[0], total_z, plane, momenta_ref, phase_ref, turn_ref)

    for copy in copies(now):
        copy.wait()

    def linker(direction):
        return lambda part, row, col, lanes: link_ref[now, direction, part, row, col, :, lanes]

    def vector(part, color, rows, lanes):
        return vector_ref[now, part, color, rows, lanes].astype(jnp.float32)

    def gram(moved_ref, disp):
        product = lax.dot_general(
            phased_ref[...], moved_ref[...], (((1,), (1,)), ((), ())), preferred_element_type=jnp.float32
        )
        for moment in range(NMOM):
            start = 2 * moment * nvec
            upper = product[start : start + nvec]
            lower = product[start + nvec : start + 2 * nvec]
            factor = scale if disp == 0 else 0.5 * scale
            real = factor * (upper[:, :nvec] + lower[:, nvec:])
            imag = factor * (upper[:, nvec:] - lower[:, :nvec])
            store_rounded(item_ref, (0, moment, disp), real, imag)

    flat = vector_ref[now].reshape(2 * NCOL * nvec, width)
    for direction, ahead_ref in enumerate((ahead_x_ref, ahead_y_ref)):
        ahead_ref[...] = jnp.dot(
            flat, move_ref[direction, 0], preferred_element_type=jnp.float32
        ).reshape(ahead_ref.shape)

    for color in range(NCOL):
        span = pl.ds(color * width, width)
        for part in range(2):
            still_ref[pl.ds(part * nvec, nvec), span] = vector_ref[now, part, color]
        for start in range(0, nvec, ROWS):
            real = vector_ref[now, 0, color, pl.ds(start, ROWS), :].astype(jnp.float32)
            imag = vector_ref[now, 1, color, pl.ds(start, ROWS), :].astype(jnp.float32)
            for moment in range(NMOM):
                cosine = phase_ref[moment, 0]
                sine = phase_ref[moment, 1]
                first = 2 * moment * nvec + start
                phased_ref[pl.ds(first, ROWS), span] = (cosine * real - sine * imag).astype(jnp.bfloat16)
                phased_ref[pl.ds(first + nvec, ROWS), span] = (sine * real + cosine * imag).astype(jnp.bfloat16)
    gram(still_ref, 0)

    for direction, (adjoint_ref, behind_ref) in enumerate(
        ((adjoint_x_ref, behind_x_ref), (adjoint_y_ref, behind_y_ref))
    ):

        def adjoint(part, color, rows, lanes, value):
            adjoint_ref[part, color, rows, lanes] = value.astype(jnp.bfloat16)

        color_loop(linker(direction), nvec, width, vector, adjoint, True)
        behind_ref[...] = jnp.dot(
            adjoint_ref[...].reshape(2 * NCOL * nvec, width),
            move_ref[direction, 1],
            preferred_element_type=jnp.float32,
        ).reshape(behind_ref.shape)

    for direction, (ahead_ref, behind_ref, moved_ref) in enumerate(
        ((ahead_x_ref, behind_x_ref, moved_x_ref), (ahead_y_ref, behind_y_ref, moved_y_ref))
    ):

        def ahead(part, color, rows, lanes):
            return ahead_ref[part, color, rows, lanes]

        def forward(part, color, rows, lanes, value):
            moved_ref[
                pl.ds(part * nvec + rows.start, rows.size), pl.ds(color * width + lanes.start, lanes.size)
            ] = (value - behind_ref[part, color, rows, lanes]).astype(jnp.bfloat16)

        color_loop(linker(direction), nvec, width, ahead, forward, False)
        gram(moved_ref, direction + 1)

    def own(part, color, rows, lanes, value):
        own_ref[0, part, color, rows, lanes] = value

    color_loop(linker(2), nvec, width, vector, own, True)


def plane_items(position, momenta, vectors, links, total_z, plane, scale):
    slices, _, _, nvec, width = vectors.shape
    color_block = (2, NCOL, nvec, width)
    return pl.pallas_call(
        functools.partial(plane_kernel, total_z, plane, scale),
        grid=(slices,),
        in_specs=[pl.BlockSpec(memory_space=pltpu.SMEM)] + [pl.BlockSpec(memory_space=pltpu.HBM)] * 3,
        out_specs=[
            pl.BlockSpec((1, NMOM, NDISP - 1, 2 * nvec + ROWS, nvec), lambda t: (t, 0, 0, 0, 0)),
            pl.BlockSpec((1,) + color_block, lambda t: (t, 0, 0, 0, 0)),
            pl.BlockSpec((NMOM, 2, 1, width), lambda t: (0, 0, 0, 0)),
            pl.BlockSpec((NMOM, 2, 1, nvec), lambda t: (0, 0, 0, 0)),
        ],
        out_shape=[
            jax.ShapeDtypeStruct((slices, NMOM, NDISP - 1, 2 * nvec + ROWS, nvec), jnp.bfloat16),
            jax.ShapeDtypeStruct(vectors.shape, jnp.float32),
            jax.ShapeDtypeStruct((NMOM, 2, 1, width), jnp.float32),
            jax.ShapeDtypeStruct((NMOM, 2, 1, nvec), jnp.float32),
        ],
        scratch_shapes=[
            pltpu.SMEM(momenta.shape, jnp.int32),
            pltpu.VMEM(vectors.shape, jnp.bfloat16),
            pltpu.VMEM(links.shape, jnp.float32),
        ]
        + [pltpu.VMEM(color_block, jnp.float32)] * 4
        + [pltpu.VMEM(color_block, jnp.bfloat16)] * 2
        + [pltpu.VMEM((NMOM * 2 * nvec, NCOL * width), jnp.bfloat16)]
        + [pltpu.VMEM((2 * nvec, NCOL * width), jnp.bfloat16)] * 3
        + [
            pltpu.VMEM((2, 2, width, width), jnp.bfloat16),
            pltpu.SemaphoreType.DMA,
            pltpu.SemaphoreType.DMA((2, slices)),
        ],
        compiler_params=pltpu.CompilerParams(vmem_limit_bytes=PLANE_LIMIT),
        cost_estimate=pl.CostEstimate(
            flops=slices * 16 * NMOM * nvec * nvec * NCOL * width,
            bytes_accessed=6 * vectors.size + 4 * links.size,
            transcendentals=0,
        ),
        name="plane_items",
    )(position, in_hbm(momenta), in_hbm(vectors), in_hbm(links))


def layer_kernel(
    core, scale, rows_ref, item_ref, own_ref, ahead_ref, phase_ref, turn_ref, out_ref, lhs_ref, listed_ref
):
    nvec, width = own_ref.shape[3:]
    total = out_ref.shape[0]
    sites = rows_ref.shape[0] // 2

    def parts_of(place):
        item = rows_ref[2 * lax.rem(place, sites) + core, lax.div(place, sites), 0]
        rest = lax.rem(item, NMOM * NDISP)
        return lax.div(item, NMOM * NDISP), lax.div(rest, NDISP), lax.rem(rest, NDISP)

    def bond(place, lhs):
        slice_index, moment, _ = parts_of(place)
        cosine = phase_ref[moment, 0]
        sine = phase_ref[moment, 1]
        for color in range(NCOL):
            span = pl.ds(color * width, width)
            for part in range(2):
                value = own_ref[slice_index, part, color]
                lhs[pl.ds(part * nvec, nvec), span] = (cosine * value).astype(jnp.bfloat16)
                lhs[pl.ds((2 + part) * nvec, nvec), span] = (sine * value).astype(jnp.bfloat16)
        rhs = jnp.concatenate(
            [
                jnp.concatenate([ahead_ref[slice_index, part, color] for color in range(NCOL)], 1)
                for part in range(2)
            ],
            0,
        )
        gram = lax.dot_general(lhs[...], rhs, (((1,), (1,)), ((), ())), preferred_element_type=jnp.float32)
        block = [
            [gram[i * nvec : (i + 1) * nvec, j * nvec : (j + 1) * nvec] for j in range(2)] for i in range(4)
        ]
        cos_real = block[0][0] + block[1][1]
        cos_imag = block[0][1] - block[1][0]
        sin_real = block[2][0] + block[3][1]
        sin_imag = block[2][1] - block[3][0]
        half = 0.5 * scale
        turn_cos = half * turn_ref[moment, 0]
        turn_sin = half * turn_ref[moment, 1]
        back_real = cos_real - sin_imag
        back_imag = cos_imag + sin_real
        real = half * (cos_real + sin_imag) - (turn_cos * back_real - turn_sin * back_imag).T
        imag = half * (cos_imag - sin_real) + (turn_cos * back_imag + turn_sin * back_real).T
        return real, imag

    found = jnp.int32(0)
    for place in range(total):
        slice_index, moment, disp = parts_of(jnp.int32(place))
        out_ref[place] = item_ref[slice_index, moment, jnp.minimum(disp, NDISP - 2)]
        listed_ref[found] = place
        found = found + (disp == NDISP - 1).astype(jnp.int32)

    @pl.loop(0, lax.div(found + 1, 2))
    def _(pair):
        both = [listed_ref[2 * pair], listed_ref[jnp.minimum(2 * pair + 1, found - 1)]]
        results = [bond(place, lhs_ref.at[index]) for index, place in enumerate(both)]
        for place, (real, imag) in zip(both, results):
            store_rounded(out_ref, (place,), real, imag)


def layer_items(core, rows, item, own, ahead, phase, turn, scale):
    slices, _, _, nvec, width = own.shape
    devices, slots, _ = rows.shape
    total = slots * devices // 2
    whole = pl.BlockSpec(memory_space=pltpu.VMEM)
    return pl.pallas_call(
        functools.partial(layer_kernel, core, scale),
        in_specs=[pl.BlockSpec(memory_space=pltpu.SMEM)] + [whole] * 5,
        out_specs=whole,
        out_shape=jax.ShapeDtypeStruct((total, 2 * nvec + ROWS, nvec), jnp.bfloat16),
        scratch_shapes=[
            pltpu.VMEM((2, 4 * nvec, NCOL * width), jnp.bfloat16),
            pltpu.SMEM((total,), jnp.int32),
        ],
        compiler_params=pltpu.CompilerParams(vmem_limit_bytes=8 * MIB),
        cost_estimate=pl.CostEstimate(
            flops=total * 4 * nvec * nvec * NCOL * width,
            bytes_accessed=2 * own.size,
            transcendentals=0,
        ),
        name="layer_items",
    )(rows, item, own, ahead, phase, turn)


def add_kernel(places, *refs):
    for out_ref, entries in zip(refs[len(refs) - len(places) :], places):
        for index, entry in enumerate(entries):
            total = sum(refs[number][at].astype(jnp.float32) for number, at in entry)
            nvec = total.shape[1]
            if out_ref.dtype == jnp.float32:
                out_ref[index] = total
            else:
                left = total[2 * nvec :]
                store_rounded(out_ref, (index,), total[:nvec], total[nvec : 2 * nvec], left)


def added(groups):
    arrays = []

    def number(array):
        found = [place for place, other in enumerate(arrays) if other is array]
        if not found:
            arrays.append(array)
        return found[0] if found else len(arrays) - 1

    places = [[[(number(array), at) for array, at in entry] for entry in entries] for entries, _ in groups]
    tail = arrays[0].shape[1:]
    whole = pl.BlockSpec(memory_space=pltpu.VMEM)
    size = sum(len(entry) for entries in places for entry in entries) * math.prod(tail)
    return pl.pallas_call(
        functools.partial(add_kernel, places),
        in_specs=[whole] * len(arrays),
        out_specs=[whole] * len(groups),
        out_shape=[jax.ShapeDtypeStruct((len(entries),) + tail, dtype) for entries, dtype in groups],
        compiler_params=pltpu.CompilerParams(vmem_limit_bytes=8 * MIB),
        cost_estimate=pl.CostEstimate(flops=size, bytes_accessed=4 * size, transcendentals=0),
        name="added",
    )(*arrays)


class Chain:
    def __init__(self, entries, order):
        self.entries = entries
        self.order = order

    def chunks(self, step):
        far = [r for r in self.entries if r >> (self.order[step] - 1) & 1]
        if step + 1 == len(self.order):
            return [far]
        split = [[], []]
        for r in far:
            split[r >> (self.order[step + 1] - 1) & 1].append(r)
        return [split[1], split[0]]

    def send(self, step, far):
        bit = self.order[step]
        near = [r ^ (1 << (bit - 1)) for r in far]
        groups = [([self.entries[r] for r in far], jnp.bfloat16)]
        last = step + 1 == len(self.order)
        if step == 0 or last:
            kept = [self.entries[r] if step == 0 else self.entries[r][:2] for r in near]
            groups.append((kept, jnp.float32))
        outs = added(groups)
        arrived = exchanged(outs[0], 1 << bit)
        for at, r in enumerate(near):
            if step == 0:
                self.entries[r] = [(outs[1], at)]
            elif last:
                self.entries[r][:2] = [(outs[1], at)]
            self.entries[r].append((arrived, at))
        for r in far:
            del self.entries[r]


def mix_kernel(slot_ref, structure_ref, weight_ref, tau_ref, out_ref):
    spins, _, nvec, width = tau_ref.shape[1:]
    base = structure_ref[pl.program_id(0)] * spins * spins
    weight = [[weight_ref[base + r * spins + s] for s in range(spins)] for r in range(spins)]

    @pl.loop(0, 2 * nvec // ROWS)
    def _(index):
        part = index // (nvec // ROWS)
        rows = pl.ds(pl.multiple_of(index % (nvec // ROWS) * ROWS, ROWS), ROWS)
        tau = [tau_ref[0, s, part, rows, :].astype(jnp.float32) for s in range(spins)]
        for r in range(spins):
            mixed = weight[r][0] * tau[0]
            for s in range(1, spins):
                mixed = mixed + weight[r][s] * tau[s]
            out_ref[0, r, part, rows, :] = mixed.astype(jnp.bfloat16)


def mixed_perambulators(slots, structures, weights, perambulators):
    block = (1,) + perambulators.shape[1:]
    count = slots.shape[0]
    return pl.pallas_call(
        mix_kernel,
        grid_spec=pltpu.PrefetchScalarGridSpec(
            num_scalar_prefetch=3,
            grid=(count,),
            in_specs=[pl.BlockSpec(block, lambda j, slot, *_: (slot[j], 0, 0, 0, 0))],
            out_specs=pl.BlockSpec(block, lambda j, *_: (j, 0, 0, 0, 0)),
        ),
        out_shape=jax.ShapeDtypeStruct((count,) + perambulators.shape[1:], jnp.bfloat16),
        compiler_params=pltpu.CompilerParams(vmem_limit_bytes=8 * MIB),
        cost_estimate=pl.CostEstimate(
            flops=8 * perambulators.size, bytes_accessed=4 * perambulators.size, transcendentals=0
        ),
        name="mixed_perambulators",
    )(slots, structures, weights, in_hbm(perambulators))


def diagram_kernel(places, *refs):
    tau_ref, out_ref, block_ref, sems = refs[-4:]
    count, spins, _, nvec, width = tau_ref.shape

    def copy(index, r):
        return pltpu.make_async_copy(block_ref.at[index, r], out_ref.at[index, r], sems.at[index, r])

    for index, entry in enumerate(places):
        real, imag = restored(sum(refs[number][at].astype(jnp.float32) for number, at in entry))
        square = jnp.concatenate(
            [jnp.concatenate([real, -imag], 1), jnp.concatenate([imag, real], 1)], 0
        ).astype(jnp.bfloat16)
        for r in range(spins):
            tau = tau_ref[index, r].reshape(2 * nvec, width)
            block = jnp.dot(square, tau, preferred_element_type=jnp.float32)
            block_ref[index, r] = block.astype(jnp.bfloat16).reshape(2, nvec, width)
            copy(index, r).start()
    for index in range(count):
        for r in range(spins):
            copy(index, r).wait()


def diagrams(entries, tau):
    count, spins, _, nvec, width = tau.shape
    whole = pl.BlockSpec(memory_space=pltpu.VMEM)
    arrays = [array for entry in entries for array, _ in entry]
    places = []
    for entry in entries:
        start = sum(len(one) for one in places)
        places.append([(start + number, at) for number, (_, at) in enumerate(entry)])
    return pl.pallas_call(
        functools.partial(diagram_kernel, places),
        in_specs=[whole] * (len(arrays) + 1),
        out_specs=pl.BlockSpec(memory_space=pltpu.HBM),
        out_shape=jax.ShapeDtypeStruct(tau.shape, jnp.bfloat16),
        scratch_shapes=[
            pltpu.VMEM(tau.shape, jnp.bfloat16),
            pltpu.SemaphoreType.DMA((count, spins)),
        ],
        compiler_params=pltpu.CompilerParams(vmem_limit_bytes=8 * MIB),
        cost_estimate=pl.CostEstimate(
            flops=8 * nvec * nvec * width * spins * count, bytes_accessed=4 * tau.size, transcendentals=0
        ),
        name="diagrams",
    )(*arrays, tau)


def body(eigvecs, gauge_links, momenta, spin_mix, perambulators, contraction_list):
    slices, _, _, nvec, depth, plane = eigvecs.shape
    devices = lax.axis_size(SITES)
    position = lax.axis_index(SITES)
    bits = devices.bit_length() - 1
    total_z = depth * devices
    width = depth * plane
    scale = 1.0 / math.sqrt(NCOL * plane * total_z)
    place = position.reshape(1)
    rows, after, place = gathered(contraction_list, eigvecs, place)
    upper = shifted(after[:, :, :, :, :1, :], SITES, -1)
    vectors = eigvecs.reshape(slices, 2, NCOL, nvec, width)
    links = gauge_links.reshape(slices, 3, 2, NCOL, NCOL, 1, width)
    item, own, phase, turn = plane_items(place, momenta, vectors, links, total_z, plane, scale)
    chosen = contraction_list[:, 2] - position * perambulators.shape[0]
    tau = mixed_perambulators(chosen, contraction_list[:, 1], spin_mix.reshape(-1), perambulators)
    ahead = jnp.concatenate([eigvecs[:, :, :, :, 1:, :], upper], 4).reshape(vectors.shape)
    send = layer_items(1, rows, item, own, ahead, phase, turn, scale)
    keep = layer_items(0, rows, item, own, ahead, phase, turn, scale)
    slots = range(contraction_list.shape[0])
    other = exchanged(send, 1)
    sites = devices // 2
    chains = [
        Chain(
            {r: [(keep, slot * sites + r), (other, slot * sites + r)] for r in range(sites)},
            [2, 1, *range(3, bits)] if slot % 2 else [1, bits - 1, *range(2, bits - 1)],
        )
        for slot in slots
    ]
    for step in range(bits - 1):
        messages = [chain.chunks(step) for chain in chains]
        for part in range(len(messages[0])):
            for chain, far in zip(chains, messages):
                chain.send(step, far[part])
    return diagrams([chain.entries[0] for chain in chains], tau)


def solution(mesh):
    placed = (
        P("cfg", None, None, None, ("space", "diag"), None),
        P("cfg", None, None, None, None, ("space", "diag"), None),
        P(),
        P(),
        P(("cfg", "space", "diag"), None, None, None, None),
        P(("space", "diag"), None),
    )
    return jax.shard_map(
        body,
        mesh=mesh,
        in_specs=placed,
        out_specs=P(("cfg", "space", "diag"), None, None, None, None),
        check_vma=False,
    )
```

profile of v0, /device:TPU:0, one launch (start us, length us, event | category | flops | bytes accessed | tf_op | source)
XLA Modules:
  0.0 59.0 jit_solution(13790267298853444304)
XLA Ops:
  0.0 2.4 %collective-permute-start = (s32[1,2,3]{2,1,0:T(2,128)}, s32[1,2,3]{2,1,0:T(2,128)S(1)}, u32[]{:S(2)}, u32[]{:S(2)}) collective-permute-start(s32[1,2,3]{2,1,0:T(2,128)} %bitcast.7), channel_id=1, source_target_pairs={{0,3},{1,2},{2,1},{3,0},{4,7},{5,6},{6,5},{7,4},{8,11},{9,10},{10,... | collective-permute-start | bytes 80 | tf_op jit(solution)/shard_map/ppermute | solution.py:34
  2.4 0.6 %collective-permute-start.1 = (s32[1,2,3]{2,1,0:T(2,128)}, s32[1,2,3]{2,1,0:T(2,128)S(1)}, u32[]{:S(2)}, u32[]{:S(2)}) collective-permute-start(s32[1,2,3]{2,1,0:T(2,128)} %bitcast.8), channel_id=1, source_target_pairs={{0,2},{1,3},{2,0},{3,1},{4,6},{5,7},{6,4},{7,5},{8,10},{9,11},{10,... | collective-permute-start | bytes 80 | tf_op jit(solution)/shard_map/ppermute | solution.py:34
  3.1 0.8 %collective-permute-done = s32[1,2,3]{2,1,0:T(2,128)S(1)} collective-permute-done((s32[1,2,3]{2,1,0:T(2,128)}, s32[1,2,3]{2,1,0:T(2,128)S(1)}, u32[]{:S(2)}, u32[]{:S(2)}) %collective-permute-start) | collective-permute-done | bytes 56 | tf_op jit(solution)/shard_map/ppermute | solution.py:34
  3.9 2.3 %collective-permute-done.1 = s32[1,2,3]{2,1,0:T(2,128)S(1)} collective-permute-done((s32[1,2,3]{2,1,0:T(2,128)}, s32[1,2,3]{2,1,0:T(2,128)S(1)}, u32[]{:S(2)}, u32[]{:S(2)}) %collective-permute-start.1) | collective-permute-done | bytes 56 | tf_op jit(solution)/shard_map/ppermute | solution.py:34
  6.2 2.7 %collective-permute-start.6 = (bf16[4,2,3,128,1,256]{5,3,2,1,0,4:T(8,128)(2,1)}, bf16[4,2,3,128,1,256]{5,3,2,1,0,4:T(8,128)(2,1)S(1)}, u32[]{:S(2)}, u32[]{:S(2)}) collective-permute-start(bf16[4,2,3,128,1,256]{5,3,2,1,0,4:T(8,128)(2,1)} %bitcast.11), channel_id=1, source_target_pairs={{0,15},{1,0},{2,1},{3,2},{4,3},{5,4},{6,5},{7,6},{8,7},{9,8},{10,9... | collective-permute-start | bytes 4718600 | tf_op jit(solution)/shard_map/ppermute | solution.py:25
  8.9 0.7 %pad_add_fusion = s32[4,2,3]{2,1,0:T(2,128)S(1)} fusion(s32[1,2,3]{2,1,0:T(2,128)S(1)} %collective-permute-done, s32[1,2,3]{2,1,0:T(2,128)S(1)} %collective-permute-done.1, s32[1,2,3]{2,1,0:T(2,128)S(1)} %collective-permute-done.2, s32[1,2,3]{2,1,0:T(2,128)} %bitcast.10), kind=kLoop, calls=%fused_computation.4 | loop fusion | flops 72 | bytes 192 | tf_op jit(solution)/shard_map/concatenate | solution.py:46
  9.6 1.4 %collective-permute-start.4 = (s32[4,2,3]{2,1,0:T(2,128)S(1)}, s32[4,2,3]{2,1,0:T(2,128)S(1)}, u32[]{:S(2)}, u32[]{:S(2)}) collective-permute-start(s32[4,2,3]{2,1,0:T(2,128)S(1)} %pad_add_fusion), channel_id=1, source_target_pairs={{0,8},{1,9},{2,10},{3,11},{4,12},{5,13},{6,14},{7,15},{8,0},{9,1},... | collective-permute-start | bytes 296 | tf_op jit(solution)/shard_map/ppermute | solution.py:34
  11.0 3.0 %collective-permute-start.5 = (s32[4,2,3]{2,1,0:T(2,128)S(1)}, s32[4,2,3]{2,1,0:T(2,128)S(1)}, u32[]{:S(2)}, u32[]{:S(2)}) collective-permute-start(s32[4,2,3]{2,1,0:T(2,128)S(1)} %pad_add_fusion), channel_id=1, source_target_pairs={{0,12},{1,13},{2,14},{3,15},{4,8},{5,9},{6,10},{7,11},{8,4},{9,5},... | collective-permute-start | bytes 296 | tf_op jit(solution)/shard_map/ppermute | solution.py:34
  14.0 15.1 %plane_items.1 = (bf16[4,4,3,272,128]{4,3,2,1,0:T(8,128)(2,1)S(1)}, f32[4,2,3,128,256]{4,3,2,1,0:T(8,128)S(1)}, f32[4,2,1,256]{3,2,1,0:T(1,128)S(1)}, f32[4,2,1,128]{3,2,1,0:T(1,128)S(1)}) custom-call(s32[1]{0:T(128)} %bitcast.1.position_ref, s32[4,3]{1,0:T(4,128)} %momenta_in.1, bf16[4,2,3,128,256]{4,3,2,1,0:T(8,128)(2,1)} %bitcast.12, ...), custom_call_target="tpu_custom_call" | custom-call | flops 3221225472 | bytes 4939776 | tf_op jit(solution)/shard_map/plane_items/pallas_call | solution.py:260
  29.2 3.3 %layer_items.3 = bf16[16,272,128]{2,1,0:T(8,128)(2,1)S(1)} custom-call(s32[16,2,3]{2,1,0:T(2,128)S(1)} %constant_dynamic-update-slice_fusion.rows_ref, bf16[4,4,3,272,128]{4,3,2,1,0:T(8,128)(2,1)S(1)} %get-tuple-element.32.item_ref, f32[4,2,3,128,256]{4,3,2,1,0:T(8,128)S(1)} %get-tuple-element.33.own_ref, bf16[4,2,3,128,256]{4,3,2,1,0:T(8,128)(2,1)S(1)} %bitcast.5, ...), custom_call_target="tpu_custom_call" | custom-call | flops 805306368 | bytes 1572864 | tf_op jit(solution)/shard_map/layer_items/pallas_call | solution.py:366
  32.6 1.7 %layer_items.2.refs_0_ = bf16[16,272,128]{2,1,0:T(8,128)(2,1)S(1)} custom-call(s32[16,2,3]{2,1,0:T(2,128)S(1)} %constant_dynamic-update-slice_fusion.rows_ref, bf16[4,4,3,272,128]{4,3,2,1,0:T(8,128)(2,1)S(1)} %get-tuple-element.32.item_ref, f32[4,2,3,128,256]{4,3,2,1,0:T(8,128)S(1)} %get-tuple-element.33.own_ref, bf16[4,2,3,128,256]{4,3,2,1,0:T(8,128)(2,1)S(1)} %bitcast.6, ...), custom_call_target="tpu_custom_call" | custom-call | flops 805306368 | bytes 1572864 | tf_op jit(solution)/shard_map/layer_items/pallas_call | solution.py:366
  34.3 1.0 %collective-permute-done.7.refs_1_ = bf16[16,272,128]{2,1,0:T(8,128)(2,1)S(1)} collective-permute-done((bf16[16,272,128]{2,1,0:T(8,128)(2,1)S(1)}, bf16[16,272,128]{2,1,0:T(8,128)(2,1)S(1)}, u32[]{:S(2)}, u32[]{:S(2)}) %collective-permute-start.7) | collective-permute-done | bytes 1114144 | tf_op jit(solution)/shard_map/ppermute | solution.py:34
  35.6 0.6 %collective-permute-start.14 = (bf16[2,272,128]{2,1,0:T(8,128)(2,1)S(1)}, bf16[2,272,128]{2,1,0:T(8,128)(2,1)S(1)}, u32[]{:S(2)}, u32[]{:S(2)}) collective-permute-start(bf16[2,272,128]{2,1,0:T(8,128)(2,1)S(1)} %get-tuple-element.46), channel_id=1, source_target_pairs={{0,4},{1,5},{2,6},{3,7},{4,0},{5,1},{6,2},{7,3},{8,12},{9,13},{10,... | collective-permute-start | bytes 417800 | tf_op jit(solution)/shard_map/ppermute | solution.py:34
  36.4 2.1 %collective-permute-start.8 = (bf16[2,272,128]{2,1,0:T(8,128)(2,1)S(1)}, bf16[2,272,128]{2,1,0:T(8,128)(2,1)S(1)}, u32[]{:S(2)}, u32[]{:S(2)}) collective-permute-start(bf16[2,272,128]{2,1,0:T(8,128)(2,1)S(1)} %get-tuple-element.38), channel_id=1, source_target_pairs={{0,2},{1,3},{2,0},{3,1},{4,6},{5,7},{6,4},{7,5},{8,10},{9,11},{10,... | collective-permute-start | bytes 417800 | tf_op jit(solution)/shard_map/ppermute | solution.py:34
  38.6 1.5 %collective-permute-start.13 = (bf16[2,272,128]{2,1,0:T(8,128)(2,1)S(1)}, bf16[2,272,128]{2,1,0:T(8,128)(2,1)S(1)}, u32[]{:S(2)}, u32[]{:S(2)}) collective-permute-start(bf16[2,272,128]{2,1,0:T(8,128)(2,1)S(1)} %get-tuple-element.44), channel_id=1, source_target_pairs={{0,4},{1,5},{2,6},{3,7},{4,0},{5,1},{6,2},{7,3},{8,12},{9,13},{10,... | collective-permute-start | bytes 417800 | tf_op jit(solution)/shard_map/ppermute | solution.py:34
  40.1 1.9 %collective-permute-done.9.refs_1_ = bf16[2,272,128]{2,1,0:T(8,128)(2,1)S(1)} collective-permute-done((bf16[2,272,128]{2,1,0:T(8,128)(2,1)S(1)}, bf16[2,272,128]{2,1,0:T(8,128)(2,1)S(1)}, u32[]{:S(2)}, u32[]{:S(2)}) %collective-permute-start.9) | collective-permute-done | bytes 139296 | tf_op jit(solution)/shard_map/ppermute | solution.py:34
  42.0 1.6 %collective-permute-start.10 = (bf16[1,272,128]{2,1,0:T(8,128)(2,1)S(1)}, bf16[1,272,128]{2,1,0:T(8,128)(2,1)S(1)}, u32[]{:S(2)}, u32[]{:S(2)}) collective-permute-start(bf16[1,272,128]{2,1,0:T(8,128)(2,1)S(1)} %added.12), channel_id=1, source_target_pairs={{0,8},{1,9},{2,10},{3,11},{4,12},{5,13},{6,14},{7,15},{8,0},{9,1},... | collective-permute-start | bytes 208904 | tf_op jit(solution)/shard_map/ppermute | solution.py:34
  43.7 0.6 %collective-permute-start.15 = (bf16[1,272,128]{2,1,0:T(8,128)(2,1)S(1)}, bf16[1,272,128]{2,1,0:T(8,128)(2,1)S(1)}, u32[]{:S(2)}, u32[]{:S(2)}) collective-permute-start(bf16[1,272,128]{2,1,0:T(8,128)(2,1)S(1)} %added.17), channel_id=1, source_target_pairs={{0,2},{1,3},{2,0},{3,1},{4,6},{5,7},{6,4},{7,5},{8,10},{9,11},{10,... | collective-permute-start | bytes 208904 | tf_op jit(solution)/shard_map/ppermute | solution.py:34
  44.6 1.6 %collective-permute-start.11 = (bf16[1,272,128]{2,1,0:T(8,128)(2,1)S(1)}, bf16[1,272,128]{2,1,0:T(8,128)(2,1)S(1)}, u32[]{:S(2)}, u32[]{:S(2)}) collective-permute-start(bf16[1,272,128]{2,1,0:T(8,128)(2,1)S(1)} %added.14), channel_id=1, source_target_pairs={{0,8},{1,9},{2,10},{3,11},{4,12},{5,13},{6,14},{7,15},{8,0},{9,1},... | collective-permute-start | bytes 208904 | tf_op jit(solution)/shard_map/ppermute | solution.py:34
  46.3 1.3 %collective-permute-start.16 = (bf16[1,272,128]{2,1,0:T(8,128)(2,1)S(1)}, bf16[1,272,128]{2,1,0:T(8,128)(2,1)S(1)}, u32[]{:S(2)}, u32[]{:S(2)}) collective-permute-start(bf16[1,272,128]{2,1,0:T(8,128)(2,1)S(1)} %added.19), channel_id=1, source_target_pairs={{0,2},{1,3},{2,0},{3,1},{4,6},{5,7},{6,4},{7,5},{8,10},{9,11},{10,... | collective-permute-start | bytes 208904 | tf_op jit(solution)/shard_map/ppermute | solution.py:34
  47.6 3.0 %collective-permute-done.10.refs_2_ = bf16[1,272,128]{2,1,0:T(8,128)(2,1)S(1)} collective-permute-done((bf16[1,272,128]{2,1,0:T(8,128)(2,1)S(1)}, bf16[1,272,128]{2,1,0:T(8,128)(2,1)S(1)}, u32[]{:S(2)}, u32[]{:S(2)}) %collective-permute-start.10) | collective-permute-done | bytes 69664 | tf_op jit(solution)/shard_map/ppermute | solution.py:34
  50.9 2.8 %collective-permute-start.17 = (bf16[1,272,128]{2,1,0:T(8,128)(2,1)S(1)}, bf16[1,272,128]{2,1,0:T(8,128)(2,1)S(1)}, u32[]{:S(2)}, u32[]{:S(2)}) collective-permute-start(bf16[1,272,128]{2,1,0:T(8,128)(2,1)S(1)} %get-tuple-element.48), channel_id=1, source_target_pairs={{0,8},{1,9},{2,10},{3,11},{4,12},{5,13},{6,14},{7,15},{8,0},{9,1},... | collective-permute-start | bytes 208904 | tf_op jit(solution)/shard_map/ppermute | solution.py:34
  53.9 3.4 %mixed_perambulators.1.refs_6_ = bf16[2,4,2,128,512]{4,3,2,1,0:T(8,128)(2,1)S(1)} custom-call(s32[2]{0:T(128)S(1)} %get-tuple-element.50.slot_ref, s32[2]{0:T(128)S(1)} %get-tuple-element.49.structure_ref, f32[256]{0:T(256)S(1)} %reshape.17.weight_ref, bf16[2,4,2,128,512]{4,3,2,1,0:T(8,128)(2,1)} %tau_ref.1), custom_call_target="tpu_custom_call" | custom-call | flops 8388608 | bytes 4194304 | tf_op jit(solution)/shard_map/mixed_perambulators/pallas_call | solution.py:475
  57.4 1.6 %diagrams.1 = bf16[2,4,2,128,512]{4,3,2,1,0:T(8,128)(2,1)} custom-call(f32[1,272,128]{2,1,0:T(8,128)S(1)} %get-tuple-element.41.refs_0_, bf16[1,272,128]{2,1,0:T(8,128)(2,1)S(1)} %collective-permute-done.11.refs_1_, bf16[1,272,128]{2,1,0:T(8,128)(2,1)S(1)} %collective-permute-done.12.refs_2_, f32[1,272,128]{2,1,0:T(8,128)S(1)} %get-tuple-element.47.refs_3_, ...), custom_call_target="tpu_custom_call" | custom-call | flops 536870912 | bytes 4194304 | tf_op jit(solution)/shard_map/diagrams/pallas_call | solution.py:522
  (39 shorter events, 1.6 us)
Async XLA Ops:
  0.0 3.9 %collective-permute-start = (s32[1,2,3]{2,1,0:T(2,128)}, s32[1,2,3]{2,1,0:T(2,128)S(1)}, u32[]{:S(2)}, u32[]{:S(2)}) collective-permute-start(s32[1,2,3]{2,1,0:T(2,128)} %bitcast.7), channel_id=1, source_target_pairs={{0,3},{1,2},{2,1},{3,0},{4,7},{5,6},{6,5},{7,4},{8,11},{9,10},{10,... | collective-permute-start | bytes 80 | tf_op jit(solution)/shard_map/ppermute | solution.py:34
  2.4 3.8 %collective-permute-start.1 = (s32[1,2,3]{2,1,0:T(2,128)}, s32[1,2,3]{2,1,0:T(2,128)S(1)}, u32[]{:S(2)}, u32[]{:S(2)}) collective-permute-start(s32[1,2,3]{2,1,0:T(2,128)} %bitcast.8), channel_id=1, source_target_pairs={{0,2},{1,3},{2,0},{3,1},{4,6},{5,7},{6,4},{7,5},{8,10},{9,11},{10,... | collective-permute-start | bytes 80 | tf_op jit(solution)/shard_map/ppermute | solution.py:34
  3.0 3.2 %collective-permute-start.2 = (s32[1,2,3]{2,1,0:T(2,128)}, s32[1,2,3]{2,1,0:T(2,128)S(1)}, u32[]{:S(2)}, u32[]{:S(2)}) collective-permute-start(s32[1,2,3]{2,1,0:T(2,128)} %bitcast.9), channel_id=1, source_target_pairs={{0,1},{1,0},{2,3},{3,2},{4,5},{5,4},{6,7},{7,6},{8,9},{9,8},{10,11... | collective-permute-start | bytes 80 | tf_op jit(solution)/shard_map/ppermute | solution.py:34
  6.2 23.0 %collective-permute-start.6 = (bf16[4,2,3,128,1,256]{5,3,2,1,0,4:T(8,128)(2,1)}, bf16[4,2,3,128,1,256]{5,3,2,1,0,4:T(8,128)(2,1)S(1)}, u32[]{:S(2)}, u32[]{:S(2)}) collective-permute-start(bf16[4,2,3,128,1,256]{5,3,2,1,0,4:T(8,128)(2,1)} %bitcast.11), channel_id=1, source_target_pairs={{0,15},{1,0},{2,1},{3,2},{4,3},{5,4},{6,5},{7,6},{8,7},{9,8},{10,9... | collective-permute-start | bytes 4718600 | tf_op jit(solution)/shard_map/ppermute | solution.py:25
  9.6 19.5 %collective-permute-start.3 = (s32[4,2,3]{2,1,0:T(2,128)S(1)}, s32[4,2,3]{2,1,0:T(2,128)S(1)}, u32[]{:S(2)}, u32[]{:S(2)}) collective-permute-start(s32[4,2,3]{2,1,0:T(2,128)S(1)} %pad_add_fusion), channel_id=1, source_target_pairs={{0,4},{1,5},{2,6},{3,7},{4,0},{5,1},{6,2},{7,3},{8,12},{9,13},{10,... | collective-permute-start | bytes 296 | tf_op jit(solution)/shard_map/ppermute | solution.py:34
  9.6 19.6 %collective-permute-start.4 = (s32[4,2,3]{2,1,0:T(2,128)S(1)}, s32[4,2,3]{2,1,0:T(2,128)S(1)}, u32[]{:S(2)}, u32[]{:S(2)}) collective-permute-start(s32[4,2,3]{2,1,0:T(2,128)S(1)} %pad_add_fusion), channel_id=1, source_target_pairs={{0,8},{1,9},{2,10},{3,11},{4,12},{5,13},{6,14},{7,15},{8,0},{9,1},... | collective-permute-start | bytes 296 | tf_op jit(solution)/shard_map/ppermute | solution.py:34
  11.0 18.2 %collective-permute-start.5 = (s32[4,2,3]{2,1,0:T(2,128)S(1)}, s32[4,2,3]{2,1,0:T(2,128)S(1)}, u32[]{:S(2)}, u32[]{:S(2)}) collective-permute-start(s32[4,2,3]{2,1,0:T(2,128)S(1)} %pad_add_fusion), channel_id=1, source_target_pairs={{0,12},{1,13},{2,14},{3,15},{4,8},{5,9},{6,10},{7,11},{8,4},{9,5},... | collective-permute-start | bytes 296 | tf_op jit(solution)/shard_map/ppermute | solution.py:34
  32.5 2.8 %collective-permute-start.7 = (bf16[16,272,128]{2,1,0:T(8,128)(2,1)S(1)}, bf16[16,272,128]{2,1,0:T(8,128)(2,1)S(1)}, u32[]{:S(2)}, u32[]{:S(2)}) collective-permute-start(bf16[16,272,128]{2,1,0:T(8,128)(2,1)S(1)} %layer_items.3), channel_id=1, source_target_pairs={{0,1},{1,0},{2,3},{3,2},{4,5},{5,4},{6,7},{7,6},{8,9},{9,8},{10,11... | collective-permute-start | bytes 3342344 | tf_op jit(solution)/shard_map/ppermute | solution.py:34
  35.4 6.5 %collective-permute-start.9 = (bf16[2,272,128]{2,1,0:T(8,128)(2,1)S(1)}, bf16[2,272,128]{2,1,0:T(8,128)(2,1)S(1)}, u32[]{:S(2)}, u32[]{:S(2)}) collective-permute-start(bf16[2,272,128]{2,1,0:T(8,128)(2,1)S(1)} %get-tuple-element.40), channel_id=1, source_target_pairs={{0,2},{1,3},{2,0},{3,1},{4,6},{5,7},{6,4},{7,5},{8,10},{9,11},{10,... | collective-permute-start | bytes 417800 | tf_op jit(solution)/shard_map/ppermute | solution.py:34
  35.6 8.1 %collective-permute-start.14 = (bf16[2,272,128]{2,1,0:T(8,128)(2,1)S(1)}, bf16[2,272,128]{2,1,0:T(8,128)(2,1)S(1)}, u32[]{:S(2)}, u32[]{:S(2)}) collective-permute-start(bf16[2,272,128]{2,1,0:T(8,128)(2,1)S(1)} %get-tuple-element.46), channel_id=1, source_target_pairs={{0,4},{1,5},{2,6},{3,7},{4,0},{5,1},{6,2},{7,3},{8,12},{9,13},{10,... | collective-permute-start | bytes 417800 | tf_op jit(solution)/shard_map/ppermute | solution.py:34
  36.3 8.0 %copy-start.1 = (f32[16,4,4]{0,2,1:T(4,128)S(1)}, f32[16,4,4]{0,2,1:T(4,128)}, u32[]{:S(2)}) copy-start(f32[16,4,4]{0,2,1:T(4,128)} %param.9) | copy-start | bytes 3076
  36.4 17.4 %copy-start = (s32[2,3]{1,0:T(2,128)S(1)}, s32[2,3]{1,0:T(2,128)}, u32[]{:S(2)}) copy-start(s32[2,3]{1,0:T(2,128)} %param.11) | copy-start | bytes 76
  36.4 10.0 %collective-permute-start.8 = (bf16[2,272,128]{2,1,0:T(8,128)(2,1)S(1)}, bf16[2,272,128]{2,1,0:T(8,128)(2,1)S(1)}, u32[]{:S(2)}, u32[]{:S(2)}) collective-permute-start(bf16[2,272,128]{2,1,0:T(8,128)(2,1)S(1)} %get-tuple-element.38), channel_id=1, source_target_pairs={{0,2},{1,3},{2,0},{3,1},{4,6},{5,7},{6,4},{7,5},{8,10},{9,11},{10,... | collective-permute-start | bytes 417800 | tf_op jit(solution)/shard_map/ppermute | solution.py:34
  38.6 12.2 %collective-permute-start.13 = (bf16[2,272,128]{2,1,0:T(8,128)(2,1)S(1)}, bf16[2,272,128]{2,1,0:T(8,128)(2,1)S(1)}, u32[]{:S(2)}, u32[]{:S(2)}) collective-permute-start(bf16[2,272,128]{2,1,0:T(8,128)(2,1)S(1)} %get-tuple-element.44), channel_id=1, source_target_pairs={{0,4},{1,5},{2,6},{3,7},{4,0},{5,1},{6,2},{7,3},{8,12},{9,13},{10,... | collective-permute-start | bytes 417800 | tf_op jit(solution)/shard_map/ppermute | solution.py:34
  42.0 8.6 %collective-permute-start.10 = (bf16[1,272,128]{2,1,0:T(8,128)(2,1)S(1)}, bf16[1,272,128]{2,1,0:T(8,128)(2,1)S(1)}, u32[]{:S(2)}, u32[]{:S(2)}) collective-permute-start(bf16[1,272,128]{2,1,0:T(8,128)(2,1)S(1)} %added.12), channel_id=1, source_target_pairs={{0,8},{1,9},{2,10},{3,11},{4,12},{5,13},{6,14},{7,15},{8,0},{9,1},... | collective-permute-start | bytes 208904 | tf_op jit(solution)/shard_map/ppermute | solution.py:34
  43.7 7.1 %collective-permute-start.15 = (bf16[1,272,128]{2,1,0:T(8,128)(2,1)S(1)}, bf16[1,272,128]{2,1,0:T(8,128)(2,1)S(1)}, u32[]{:S(2)}, u32[]{:S(2)}) collective-permute-start(bf16[1,272,128]{2,1,0:T(8,128)(2,1)S(1)} %added.17), channel_id=1, source_target_pairs={{0,2},{1,3},{2,0},{3,1},{4,6},{5,7},{6,4},{7,5},{8,10},{9,11},{10,... | collective-permute-start | bytes 208904 | tf_op jit(solution)/shard_map/ppermute | solution.py:34
  44.6 12.7 %collective-permute-start.11 = (bf16[1,272,128]{2,1,0:T(8,128)(2,1)S(1)}, bf16[1,272,128]{2,1,0:T(8,128)(2,1)S(1)}, u32[]{:S(2)}, u32[]{:S(2)}) collective-permute-start(bf16[1,272,128]{2,1,0:T(8,128)(2,1)S(1)} %added.14), channel_id=1, source_target_pairs={{0,8},{1,9},{2,10},{3,11},{4,12},{5,13},{6,14},{7,15},{8,0},{9,1},... | collective-permute-start | bytes 208904 | tf_op jit(solution)/shard_map/ppermute | solution.py:34
  46.3 11.0 %collective-permute-start.16 = (bf16[1,272,128]{2,1,0:T(8,128)(2,1)S(1)}, bf16[1,272,128]{2,1,0:T(8,128)(2,1)S(1)}, u32[]{:S(2)}, u32[]{:S(2)}) collective-permute-start(bf16[1,272,128]{2,1,0:T(8,128)(2,1)S(1)} %added.19), channel_id=1, source_target_pairs={{0,2},{1,3},{2,0},{3,1},{4,6},{5,7},{6,4},{7,5},{8,10},{9,11},{10,... | collective-permute-start | bytes 208904 | tf_op jit(solution)/shard_map/ppermute | solution.py:34
  50.7 6.6 %collective-permute-start.12 = (bf16[1,272,128]{2,1,0:T(8,128)(2,1)S(1)}, bf16[1,272,128]{2,1,0:T(8,128)(2,1)S(1)}, u32[]{:S(2)}, u32[]{:S(2)}) collective-permute-start(bf16[1,272,128]{2,1,0:T(8,128)(2,1)S(1)} %get-tuple-element.42), channel_id=1, source_target_pairs={{0,4},{1,5},{2,6},{3,7},{4,0},{5,1},{6,2},{7,3},{8,12},{9,13},{10,... | collective-permute-start | bytes 208904 | tf_op jit(solution)/shard_map/ppermute | solution.py:34
  50.9 6.5 %collective-permute-start.17 = (bf16[1,272,128]{2,1,0:T(8,128)(2,1)S(1)}, bf16[1,272,128]{2,1,0:T(8,128)(2,1)S(1)}, u32[]{:S(2)}, u32[]{:S(2)}) collective-permute-start(bf16[1,272,128]{2,1,0:T(8,128)(2,1)S(1)} %get-tuple-element.48), channel_id=1, source_target_pairs={{0,8},{1,9},{2,10},{3,11},{4,12},{5,13},{6,14},{7,15},{8,0},{9,1},... | collective-permute-start | bytes 208904 | tf_op jit(solution)/shard_map/ppermute | solution.py:34
where the time goes:
time: 59.2 us; the launch traced here: 59 us
  Pallas kernels  25.9 us (44%)
  starting transfers between devices  22.7 us (38%)
  waiting for transfers between devices  9.05 us (15%)
  other arithmetic  0.9 us (2%)
    ppermute x17, starting transfers between devices, exchanged(): return lax.ppermute(value, SITES, [(i, i ^ mask) for i in range(size)])  19.9 us
    pallas_call x1, Pallas kernels, plane_items(): pl.pallas_call(functools.partial(plane_kernel, total_z, plane, scale), gr...  15.1 us
    ppermute x17, waiting for transfers between devices, exchanged(): return lax.ppermute(value, SITES, [(i, i ^ mask) for i in range(size)])  9.05 us
    pallas_call x2, Pallas kernels, layer_items(): pl.pallas_call(functools.partial(layer_kernel, core, scale), in_specs=[pl...  4.98 us
    pallas_call x1, Pallas kernels, mixed_perambulators(): pl.pallas_call(mix_kernel, grid_spec=pltpu.PrefetchScalarGridSpec(num_sca...  3.38 us
    ppermute x1, starting transfers between devices, shifted(): lax.ppermute(value, axis, [(i, (i + by) % size) for i in range(size)])  2.75 us
    pallas_call x1, Pallas kernels, diagrams(): pl.pallas_call(functools.partial(diagram_kernel, places), in_specs=[whole...  1.62 us
  transfers between devices with their start and end apart: 18, of which 5 were waited for; matrix products, arithmetic and copies ran while one was open for 2% of the time, Pallas kernels for 35%

commit v1 on v0

--- a/solution.py
+++ b/solution.py
@@ -452,38 +452,49 @@
             del self.entries[r]
 
 
-def mix_kernel(slot_ref, structure_ref, weight_ref, tau_ref, out_ref):
-    spins, _, nvec, width = tau_ref.shape[1:]
-    base = structure_ref[pl.program_id(0)] * spins * spins
-    weight = [[weight_ref[base + r * spins + s] for s in range(spins)] for r in range(spins)]
-
-    @pl.loop(0, 2 * nvec // ROWS)
-    def _(index):
-        part = index // (nvec // ROWS)
-        rows = pl.ds(pl.multiple_of(index % (nvec // ROWS) * ROWS, ROWS), ROWS)
-        tau = [tau_ref[0, s, part, rows, :].astype(jnp.float32) for s in range(spins)]
-        for r in range(spins):
-            mixed = weight[r][0] * tau[0]
-            for s in range(1, spins):
-                mixed = mixed + weight[r][s] * tau[s]
-            out_ref[0, r, part, rows, :] = mixed.astype(jnp.bfloat16)
+def mix_kernel(slot_ref, structure_ref, weight_ref, tau_in, out_ref, tau_ref, sems):
+    count, spins, parts, nvec, width = out_ref.shape
+
+    def copy(index, part):
+        return pltpu.make_async_copy(
+            tau_in.at[slot_ref[index], :, part], tau_ref.at[index, :, part], sems.at[index, part]
+        )
+
+    for index in range(count):
+        for part in range(parts):
+            copy(index, part).start()
+    for index in range(count):
+        base = structure_ref[index] * spins * spins
+        weight = [[weight_ref[base + r * spins + s] for s in range(spins)] for r in range(spins)]
+        for part in range(parts):
+            copy(index, part).wait()
+
+            @pl.loop(0, nvec // ROWS)
+            def _(step):
+                rows = pl.ds(pl.multiple_of(step * ROWS, ROWS), ROWS)
+                tau = [tau_ref[index, s, part, rows, :].astype(jnp.float32) for s in range(spins)]
+                for r in range(spins):
+                    mixed = weight[r][0] * tau[0]
+                    for s in range(1, spins):
+                        mixed = mixed + weight[r][s] * tau[s]
+                    out_ref[index, r, part, rows, :] = mixed.astype(jnp.bfloat16)
 
 
 def mixed_perambulators(slots, structures, weights, perambulators):
-    block = (1,) + perambulators.shape[1:]
-    count = slots.shape[0]
+    shape = (slots.shape[0],) + perambulators.shape[1:]
+    scalar = pl.BlockSpec(memory_space=pltpu.SMEM)
     return pl.pallas_call(
         mix_kernel,
-        grid_spec=pltpu.PrefetchScalarGridSpec(
-            num_scalar_prefetch=3,
-            grid=(count,),
-            in_specs=[pl.BlockSpec(block, lambda j, slot, *_: (slot[j], 0, 0, 0, 0))],
-            out_specs=pl.BlockSpec(block, lambda j, *_: (j, 0, 0, 0, 0)),
-        ),
-        out_shape=jax.ShapeDtypeStruct((count,) + perambulators.shape[1:], jnp.bfloat16),
+        in_specs=[scalar] * 3 + [pl.BlockSpec(memory_space=pltpu.HBM)],
+        out_specs=pl.BlockSpec(memory_space=pltpu.VMEM),
+        out_shape=jax.ShapeDtypeStruct(shape, jnp.bfloat16),
+        scratch_shapes=[
+            pltpu.VMEM(shape, jnp.bfloat16),
+            pltpu.SemaphoreType.DMA(shape[::2][:2]),
+        ],
         compiler_params=pltpu.CompilerParams(vmem_limit_bytes=8 * MIB),
         cost_estimate=pl.CostEstimate(
-            flops=8 * perambulators.size, bytes_accessed=4 * perambulators.size, transcendentals=0
+            flops=8 * math.prod(shape), bytes_accessed=4 * math.prod(shape), transcendentals=0
         ),
         name="mixed_perambulators",
     )(slots, structures, weights, in_hbm(perambulators))

time: 59.2 us -> 57.7 us (0.975); the launches traced: 59 us -> 58.6 us
  waiting for transfers between devices: 9.05 us -> 8.28 us
    ppermute x17, waiting for transfers between devices: 9.05 us -> 8.28 us  [exchanged(): return lax.ppermute(value, SITES, [(i, i ^ mask) for i in range(size)])]
    pallas_call x2, Pallas kernels: 4.98 us -> 5.75 us  [layer_items(): pl.pallas_call(functools.partial(layer_kernel, core, scale), in_specs=[pl...]
  transfers between devices with their start and end apart: 18 -> 18, of which waited for: 5 -> 5; matrix products, arithmetic and copies ran while one was open for 2% -> 2% of each run, Pallas kernels for 35% -> 36%
where the time goes in v1:
time: 57.7 us; the launch traced here: 58.6 us
  Pallas kernels  26.2 us (45%)
  starting transfers between devices  22.7 us (39%)
  waiting for transfers between devices  8.28 us (14%)
  other arithmetic  0.9 us (2%)
    ppermute x17, starting transfers between devices, exchanged(): return lax.ppermute(value, SITES, [(i, i ^ mask) for i in range(size)])  19.9 us
    pallas_call x1, Pallas kernels, plane_items(): pl.pallas_call(functools.partial(plane_kernel, total_z, plane, scale), gr...  15.1 us
    ppermute x17, waiting for transfers between devices, exchanged(): return lax.ppermute(value, SITES, [(i, i ^ mask) for i in range(size)])  8.28 us
    pallas_call x2, Pallas kernels, layer_items(): pl.pallas_call(functools.partial(layer_kernel, core, scale), in_specs=[pl...  5.75 us
    pallas_call x1, Pallas kernels, mixed_perambulators(): pl.pallas_call(mix_kernel, in_specs=[scalar] * 3 + [pl.BlockSpec(memory_s...  2.98 us
    ppermute x1, starting transfers between devices, shifted(): lax.ppermute(value, axis, [(i, (i + by) % size) for i in range(size)])  2.75 us
    pallas_call x1, Pallas kernels, diagrams(): pl.pallas_call(functools.partial(diagram_kernel, places), in_specs=[whole...  1.61 us
  transfers between devices with their start and end apart: 18, of which 5 were waited for; matrix products, arithmetic and copies ran while one was open for 2% of the time, Pallas kernels for 36%

profile of v1, /device:TPU:0, one launch (start us, length us, event | category | flops | bytes accessed | tf_op | source)
XLA Modules:
  0.0 58.6 jit_solution(17330584638875856370)
XLA Ops:
  0.0 2.4 %collective-permute-start = (s32[1,2,3]{2,1,0:T(2,128)}, s32[1,2,3]{2,1,0:T(2,128)S(1)}, u32[]{:S(2)}, u32[]{:S(2)}) collective-permute-start(s32[1,2,3]{2,1,0:T(2,128)} %bitcast.7), channel_id=1, source_target_pairs={{0,3},{1,2},{2,1},{3,0},{4,7},{5,6},{6,5},{7,4},{8,11},{9,10},{10,... | collective-permute-start | bytes 80 | tf_op jit(solution)/shard_map/ppermute | solution.py:34
  2.4 0.6 %collective-permute-start.1 = (s32[1,2,3]{2,1,0:T(2,128)}, s32[1,2,3]{2,1,0:T(2,128)S(1)}, u32[]{:S(2)}, u32[]{:S(2)}) collective-permute-start(s32[1,2,3]{2,1,0:T(2,128)} %bitcast.8), channel_id=1, source_target_pairs={{0,2},{1,3},{2,0},{3,1},{4,6},{5,7},{6,4},{7,5},{8,10},{9,11},{10,... | collective-permute-start | bytes 80 | tf_op jit(solution)/shard_map/ppermute | solution.py:34
  3.1 0.8 %collective-permute-done = s32[1,2,3]{2,1,0:T(2,128)S(1)} collective-permute-done((s32[1,2,3]{2,1,0:T(2,128)}, s32[1,2,3]{2,1,0:T(2,128)S(1)}, u32[]{:S(2)}, u32[]{:S(2)}) %collective-permute-start) | collective-permute-done | bytes 56 | tf_op jit(solution)/shard_map/ppermute | solution.py:34
  3.9 2.3 %collective-permute-done.1 = s32[1,2,3]{2,1,0:T(2,128)S(1)} collective-permute-done((s32[1,2,3]{2,1,0:T(2,128)}, s32[1,2,3]{2,1,0:T(2,128)S(1)}, u32[]{:S(2)}, u32[]{:S(2)}) %collective-permute-start.1) | collective-permute-done | bytes 56 | tf_op jit(solution)/shard_map/ppermute | solution.py:34
  6.2 2.7 %collective-permute-start.6 = (bf16[4,2,3,128,1,256]{5,3,2,1,0,4:T(8,128)(2,1)}, bf16[4,2,3,128,1,256]{5,3,2,1,0,4:T(8,128)(2,1)S(1)}, u32[]{:S(2)}, u32[]{:S(2)}) collective-permute-start(bf16[4,2,3,128,1,256]{5,3,2,1,0,4:T(8,128)(2,1)} %bitcast.11), channel_id=1, source_target_pairs={{0,15},{1,0},{2,1},{3,2},{4,3},{5,4},{6,5},{7,6},{8,7},{9,8},{10,9... | collective-permute-start | bytes 4718600 | tf_op jit(solution)/shard_map/ppermute | solution.py:25
  8.9 0.7 %pad_add_fusion = s32[4,2,3]{2,1,0:T(2,128)S(1)} fusion(s32[1,2,3]{2,1,0:T(2,128)S(1)} %collective-permute-done, s32[1,2,3]{2,1,0:T(2,128)S(1)} %collective-permute-done.1, s32[1,2,3]{2,1,0:T(2,128)S(1)} %collective-permute-done.2, s32[1,2,3]{2,1,0:T(2,128)} %bitcast.10), kind=kLoop, calls=%fused_computation.4 | loop fusion | flops 72 | bytes 192 | tf_op jit(solution)/shard_map/concatenate | solution.py:46
  9.6 1.4 %collective-permute-start.4 = (s32[4,2,3]{2,1,0:T(2,128)S(1)}, s32[4,2,3]{2,1,0:T(2,128)S(1)}, u32[]{:S(2)}, u32[]{:S(2)}) collective-permute-start(s32[4,2,3]{2,1,0:T(2,128)S(1)} %pad_add_fusion), channel_id=1, source_target_pairs={{0,8},{1,9},{2,10},{3,11},{4,12},{5,13},{6,14},{7,15},{8,0},{9,1},... | collective-permute-start | bytes 296 | tf_op jit(solution)/shard_map/ppermute | solution.py:34
  11.0 3.0 %collective-permute-start.5 = (s32[4,2,3]{2,1,0:T(2,128)S(1)}, s32[4,2,3]{2,1,0:T(2,128)S(1)}, u32[]{:S(2)}, u32[]{:S(2)}) collective-permute-start(s32[4,2,3]{2,1,0:T(2,128)S(1)} %pad_add_fusion), channel_id=1, source_target_pairs={{0,12},{1,13},{2,14},{3,15},{4,8},{5,9},{6,10},{7,11},{8,4},{9,5},... | collective-permute-start | bytes 296 | tf_op jit(solution)/shard_map/ppermute | solution.py:34
  14.0 15.1 %plane_items.1 = (bf16[4,4,3,272,128]{4,3,2,1,0:T(8,128)(2,1)S(1)}, f32[4,2,3,128,256]{4,3,2,1,0:T(8,128)S(1)}, f32[4,2,1,256]{3,2,1,0:T(1,128)S(1)}, f32[4,2,1,128]{3,2,1,0:T(1,128)S(1)}) custom-call(s32[1]{0:T(128)} %bitcast.1.position_ref, s32[4,3]{1,0:T(4,128)} %momenta_in.1, bf16[4,2,3,128,256]{4,3,2,1,0:T(8,128)(2,1)} %bitcast.12, ...), custom_call_target="tpu_custom_call" | custom-call | flops 3221225472 | bytes 4939776 | tf_op jit(solution)/shard_map/plane_items/pallas_call | solution.py:260
  29.2 3.3 %layer_items.3 = bf16[16,272,128]{2,1,0:T(8,128)(2,1)S(1)} custom-call(s32[16,2,3]{2,1,0:T(2,128)S(1)} %constant_dynamic-update-slice_fusion.rows_ref, bf16[4,4,3,272,128]{4,3,2,1,0:T(8,128)(2,1)S(1)} %get-tuple-element.32.item_ref, f32[4,2,3,128,256]{4,3,2,1,0:T(8,128)S(1)} %get-tuple-element.33.own_ref, bf16[4,2,3,128,256]{4,3,2,1,0:T(8,128)(2,1)S(1)} %bitcast.5, ...), custom_call_target="tpu_custom_call" | custom-call | flops 805306368 | bytes 1572864 | tf_op jit(solution)/shard_map/layer_items/pallas_call | solution.py:366
  32.6 2.5 %layer_items.2.refs_0_ = bf16[16,272,128]{2,1,0:T(8,128)(2,1)S(1)} custom-call(s32[16,2,3]{2,1,0:T(2,128)S(1)} %constant_dynamic-update-slice_fusion.rows_ref, bf16[4,4,3,272,128]{4,3,2,1,0:T(8,128)(2,1)S(1)} %get-tuple-element.32.item_ref, f32[4,2,3,128,256]{4,3,2,1,0:T(8,128)S(1)} %get-tuple-element.33.own_ref, bf16[4,2,3,128,256]{4,3,2,1,0:T(8,128)(2,1)S(1)} %bitcast.6, ...), custom_call_target="tpu_custom_call" | custom-call | flops 805306368 | bytes 1572864 | tf_op jit(solution)/shard_map/layer_items/pallas_call | solution.py:366
  35.1 0.2 collective-permute-done.7.refs_1_
  35.6 0.6 %collective-permute-start.14 = (bf16[2,272,128]{2,1,0:T(8,128)(2,1)S(1)}, bf16[2,272,128]{2,1,0:T(8,128)(2,1)S(1)}, u32[]{:S(2)}, u32[]{:S(2)}) collective-permute-start(bf16[2,272,128]{2,1,0:T(8,128)(2,1)S(1)} %get-tuple-element.46), channel_id=1, source_target_pairs={{0,4},{1,5},{2,6},{3,7},{4,0},{5,1},{6,2},{7,3},{8,12},{9,13},{10,... | collective-permute-start | bytes 417800 | tf_op jit(solution)/shard_map/ppermute | solution.py:34
  36.4 2.1 %collective-permute-start.8 = (bf16[2,272,128]{2,1,0:T(8,128)(2,1)S(1)}, bf16[2,272,128]{2,1,0:T(8,128)(2,1)S(1)}, u32[]{:S(2)}, u32[]{:S(2)}) collective-permute-start(bf16[2,272,128]{2,1,0:T(8,128)(2,1)S(1)} %get-tuple-element.38), channel_id=1, source_target_pairs={{0,2},{1,3},{2,0},{3,1},{4,6},{5,7},{6,4},{7,5},{8,10},{9,11},{10,... | collective-permute-start | bytes 417800 | tf_op jit(solution)/shard_map/ppermute | solution.py:34
  38.5 1.5 %collective-permute-start.13 = (bf16[2,272,128]{2,1,0:T(8,128)(2,1)S(1)}, bf16[2,272,128]{2,1,0:T(8,128)(2,1)S(1)}, u32[]{:S(2)}, u32[]{:S(2)}) collective-permute-start(bf16[2,272,128]{2,1,0:T(8,128)(2,1)S(1)} %get-tuple-element.44), channel_id=1, source_target_pairs={{0,4},{1,5},{2,6},{3,7},{4,0},{5,1},{6,2},{7,3},{8,12},{9,13},{10,... | collective-permute-start | bytes 417800 | tf_op jit(solution)/shard_map/ppermute | solution.py:34
  40.1 1.9 %collective-permute-done.9.refs_1_ = bf16[2,272,128]{2,1,0:T(8,128)(2,1)S(1)} collective-permute-done((bf16[2,272,128]{2,1,0:T(8,128)(2,1)S(1)}, bf16[2,272,128]{2,1,0:T(8,128)(2,1)S(1)}, u32[]{:S(2)}, u32[]{:S(2)}) %collective-permute-start.9) | collective-permute-done | bytes 139296 | tf_op jit(solution)/shard_map/ppermute | solution.py:34
  42.0 1.6 %collective-permute-start.10 = (bf16[1,272,128]{2,1,0:T(8,128)(2,1)S(1)}, bf16[1,272,128]{2,1,0:T(8,128)(2,1)S(1)}, u32[]{:S(2)}, u32[]{:S(2)}) collective-permute-start(bf16[1,272,128]{2,1,0:T(8,128)(2,1)S(1)} %added.12), channel_id=1, source_target_pairs={{0,8},{1,9},{2,10},{3,11},{4,12},{5,13},{6,14},{7,15},{8,0},{9,1},... | collective-permute-start | bytes 208904 | tf_op jit(solution)/shard_map/ppermute | solution.py:34
  43.7 0.6 %collective-permute-start.15 = (bf16[1,272,128]{2,1,0:T(8,128)(2,1)S(1)}, bf16[1,272,128]{2,1,0:T(8,128)(2,1)S(1)}, u32[]{:S(2)}, u32[]{:S(2)}) collective-permute-start(bf16[1,272,128]{2,1,0:T(8,128)(2,1)S(1)} %added.17), channel_id=1, source_target_pairs={{0,2},{1,3},{2,0},{3,1},{4,6},{5,7},{6,4},{7,5},{8,10},{9,11},{10,... | collective-permute-start | bytes 208904 | tf_op jit(solution)/shard_map/ppermute | solution.py:34
  44.6 1.6 %collective-permute-start.11 = (bf16[1,272,128]{2,1,0:T(8,128)(2,1)S(1)}, bf16[1,272,128]{2,1,0:T(8,128)(2,1)S(1)}, u32[]{:S(2)}, u32[]{:S(2)}) collective-permute-start(bf16[1,272,128]{2,1,0:T(8,128)(2,1)S(1)} %added.14), channel_id=1, source_target_pairs={{0,8},{1,9},{2,10},{3,11},{4,12},{5,13},{6,14},{7,15},{8,0},{9,1},... | collective-permute-start | bytes 208904 | tf_op jit(solution)/shard_map/ppermute | solution.py:34
  46.3 1.3 %collective-permute-start.16 = (bf16[1,272,128]{2,1,0:T(8,128)(2,1)S(1)}, bf16[1,272,128]{2,1,0:T(8,128)(2,1)S(1)}, u32[]{:S(2)}, u32[]{:S(2)}) collective-permute-start(bf16[1,272,128]{2,1,0:T(8,128)(2,1)S(1)} %added.19), channel_id=1, source_target_pairs={{0,2},{1,3},{2,0},{3,1},{4,6},{5,7},{6,4},{7,5},{8,10},{9,11},{10,... | collective-permute-start | bytes 208904 | tf_op jit(solution)/shard_map/ppermute | solution.py:34
  47.6 3.0 %collective-permute-done.10.refs_2_ = bf16[1,272,128]{2,1,0:T(8,128)(2,1)S(1)} collective-permute-done((bf16[1,272,128]{2,1,0:T(8,128)(2,1)S(1)}, bf16[1,272,128]{2,1,0:T(8,128)(2,1)S(1)}, u32[]{:S(2)}, u32[]{:S(2)}) %collective-permute-start.10) | collective-permute-done | bytes 69664 | tf_op jit(solution)/shard_map/ppermute | solution.py:34
  50.9 2.8 %collective-permute-start.17 = (bf16[1,272,128]{2,1,0:T(8,128)(2,1)S(1)}, bf16[1,272,128]{2,1,0:T(8,128)(2,1)S(1)}, u32[]{:S(2)}, u32[]{:S(2)}) collective-permute-start(bf16[1,272,128]{2,1,0:T(8,128)(2,1)S(1)} %get-tuple-element.48), channel_id=1, source_target_pairs={{0,8},{1,9},{2,10},{3,11},{4,12},{5,13},{6,14},{7,15},{8,0},{9,1},... | collective-permute-start | bytes 208904 | tf_op jit(solution)/shard_map/ppermute | solution.py:34
  53.9 3.0 %mixed_perambulators.1.refs_6_ = bf16[2,4,2,128,512]{4,3,2,1,0:T(8,128)(2,1)S(1)} custom-call(s32[2]{0:T(128)S(1)} %get-tuple-element.50.slot_ref, s32[2]{0:T(128)S(1)} %get-tuple-element.49.structure_ref, f32[256]{0:T(256)S(1)} %reshape.17.weight_ref, bf16[2,4,2,128,512]{4,3,2,1,0:T(8,128)(2,1)} %tau_in.1), custom_call_target="tpu_custom_call" | custom-call | flops 8388608 | bytes 4194304 | tf_op jit(solution)/shard_map/mixed_perambulators/pallas_call | solution.py:486
  57.0 1.6 %diagrams.1 = bf16[2,4,2,128,512]{4,3,2,1,0:T(8,128)(2,1)} custom-call(f32[1,272,128]{2,1,0:T(8,128)S(1)} %get-tuple-element.41.refs_0_, bf16[1,272,128]{2,1,0:T(8,128)(2,1)S(1)} %collective-permute-done.11.refs_1_, bf16[1,272,128]{2,1,0:T(8,128)(2,1)S(1)} %collective-permute-done.12.refs_2_, f32[1,272,128]{2,1,0:T(8,128)S(1)} %get-tuple-element.47.refs_3_, ...), custom_call_target="tpu_custom_call" | custom-call | flops 536870912 | bytes 4194304 | tf_op jit(solution)/shard_map/diagrams/pallas_call | solution.py:533
  (39 shorter events, 1.6 us)
Async XLA Ops:
  0.0 3.9 %collective-permute-start = (s32[1,2,3]{2,1,0:T(2,128)}, s32[1,2,3]{2,1,0:T(2,128)S(1)}, u32[]{:S(2)}, u32[]{:S(2)}) collective-permute-start(s32[1,2,3]{2,1,0:T(2,128)} %bitcast.7), channel_id=1, source_target_pairs={{0,3},{1,2},{2,1},{3,0},{4,7},{5,6},{6,5},{7,4},{8,11},{9,10},{10,... | collective-permute-start | bytes 80 | tf_op jit(solution)/shard_map/ppermute | solution.py:34
  2.4 3.8 %collective-permute-start.1 = (s32[1,2,3]{2,1,0:T(2,128)}, s32[1,2,3]{2,1,0:T(2,128)S(1)}, u32[]{:S(2)}, u32[]{:S(2)}) collective-permute-start(s32[1,2,3]{2,1,0:T(2,128)} %bitcast.8), channel_id=1, source_target_pairs={{0,2},{1,3},{2,0},{3,1},{4,6},{5,7},{6,4},{7,5},{8,10},{9,11},{10,... | collective-permute-start | bytes 80 | tf_op jit(solution)/shard_map/ppermute | solution.py:34
  3.0 3.2 %collective-permute-start.2 = (s32[1,2,3]{2,1,0:T(2,128)}, s32[1,2,3]{2,1,0:T(2,128)S(1)}, u32[]{:S(2)}, u32[]{:S(2)}) collective-permute-start(s32[1,2,3]{2,1,0:T(2,128)} %bitcast.9), channel_id=1, source_target_pairs={{0,1},{1,0},{2,3},{3,2},{4,5},{5,4},{6,7},{7,6},{8,9},{9,8},{10,11... | collective-permute-start | bytes 80 | tf_op jit(solution)/shard_map/ppermute | solution.py:34
  6.2 23.0 %collective-permute-start.6 = (bf16[4,2,3,128,1,256]{5,3,2,1,0,4:T(8,128)(2,1)}, bf16[4,2,3,128,1,256]{5,3,2,1,0,4:T(8,128)(2,1)S(1)}, u32[]{:S(2)}, u32[]{:S(2)}) collective-permute-start(bf16[4,2,3,128,1,256]{5,3,2,1,0,4:T(8,128)(2,1)} %bitcast.11), channel_id=1, source_target_pairs={{0,15},{1,0},{2,1},{3,2},{4,3},{5,4},{6,5},{7,6},{8,7},{9,8},{10,9... | collective-permute-start | bytes 4718600 | tf_op jit(solution)/shard_map/ppermute | solution.py:25
  9.6 19.5 %collective-permute-start.3 = (s32[4,2,3]{2,1,0:T(2,128)S(1)}, s32[4,2,3]{2,1,0:T(2,128)S(1)}, u32[]{:S(2)}, u32[]{:S(2)}) collective-permute-start(s32[4,2,3]{2,1,0:T(2,128)S(1)} %pad_add_fusion), channel_id=1, source_target_pairs={{0,4},{1,5},{2,6},{3,7},{4,0},{5,1},{6,2},{7,3},{8,12},{9,13},{10,... | collective-permute-start | bytes 296 | tf_op jit(solution)/shard_map/ppermute | solution.py:34
  9.6 19.6 %collective-permute-start.4 = (s32[4,2,3]{2,1,0:T(2,128)S(1)}, s32[4,2,3]{2,1,0:T(2,128)S(1)}, u32[]{:S(2)}, u32[]{:S(2)}) collective-permute-start(s32[4,2,3]{2,1,0:T(2,128)S(1)} %pad_add_fusion), channel_id=1, source_target_pairs={{0,8},{1,9},{2,10},{3,11},{4,12},{5,13},{6,14},{7,15},{8,0},{9,1},... | collective-permute-start | bytes 296 | tf_op jit(solution)/shard_map/ppermute | solution.py:34
  11.0 18.2 %collective-permute-start.5 = (s32[4,2,3]{2,1,0:T(2,128)S(1)}, s32[4,2,3]{2,1,0:T(2,128)S(1)}, u32[]{:S(2)}, u32[]{:S(2)}) collective-permute-start(s32[4,2,3]{2,1,0:T(2,128)S(1)} %pad_add_fusion), channel_id=1, source_target_pairs={{0,12},{1,13},{2,14},{3,15},{4,8},{5,9},{6,10},{7,11},{8,4},{9,5},... | collective-permute-start | bytes 296 | tf_op jit(solution)/shard_map/ppermute | solution.py:34
  32.5 2.8 %collective-permute-start.7 = (bf16[16,272,128]{2,1,0:T(8,128)(2,1)S(1)}, bf16[16,272,128]{2,1,0:T(8,128)(2,1)S(1)}, u32[]{:S(2)}, u32[]{:S(2)}) collective-permute-start(bf16[16,272,128]{2,1,0:T(8,128)(2,1)S(1)} %layer_items.3), channel_id=1, source_target_pairs={{0,1},{1,0},{2,3},{3,2},{4,5},{5,4},{6,7},{7,6},{8,9},{9,8},{10,11... | collective-permute-start | bytes 3342344 | tf_op jit(solution)/shard_map/ppermute | solution.py:34
  35.4 6.5 %collective-permute-start.9 = (bf16[2,272,128]{2,1,0:T(8,128)(2,1)S(1)}, bf16[2,272,128]{2,1,0:T(8,128)(2,1)S(1)}, u32[]{:S(2)}, u32[]{:S(2)}) collective-permute-start(bf16[2,272,128]{2,1,0:T(8,128)(2,1)S(1)} %get-tuple-element.40), channel_id=1, source_target_pairs={{0,2},{1,3},{2,0},{3,1},{4,6},{5,7},{6,4},{7,5},{8,10},{9,11},{10,... | collective-permute-start | bytes 417800 | tf_op jit(solution)/shard_map/ppermute | solution.py:34
  35.6 8.1 %collective-permute-start.14 = (bf16[2,272,128]{2,1,0:T(8,128)(2,1)S(1)}, bf16[2,272,128]{2,1,0:T(8,128)(2,1)S(1)}, u32[]{:S(2)}, u32[]{:S(2)}) collective-permute-start(bf16[2,272,128]{2,1,0:T(8,128)(2,1)S(1)} %get-tuple-element.46), channel_id=1, source_target_pairs={{0,4},{1,5},{2,6},{3,7},{4,0},{5,1},{6,2},{7,3},{8,12},{9,13},{10,... | collective-permute-start | bytes 417800 | tf_op jit(solution)/shard_map/ppermute | solution.py:34
  36.3 8.0 %copy-start.1 = (f32[16,4,4]{0,2,1:T(4,128)S(1)}, f32[16,4,4]{0,2,1:T(4,128)}, u32[]{:S(2)}) copy-start(f32[16,4,4]{0,2,1:T(4,128)} %param.9) | copy-start | bytes 3076
  36.4 17.4 %copy-start = (s32[2,3]{1,0:T(2,128)S(1)}, s32[2,3]{1,0:T(2,128)}, u32[]{:S(2)}) copy-start(s32[2,3]{1,0:T(2,128)} %param.11) | copy-start | bytes 76
  36.4 10.0 %collective-permute-start.8 = (bf16[2,272,128]{2,1,0:T(8,128)(2,1)S(1)}, bf16[2,272,128]{2,1,0:T(8,128)(2,1)S(1)}, u32[]{:S(2)}, u32[]{:S(2)}) collective-permute-start(bf16[2,272,128]{2,1,0:T(8,128)(2,1)S(1)} %get-tuple-element.38), channel_id=1, source_target_pairs={{0,2},{1,3},{2,0},{3,1},{4,6},{5,7},{6,4},{7,5},{8,10},{9,11},{10,... | collective-permute-start | bytes 417800 | tf_op jit(solution)/shard_map/ppermute | solution.py:34
  38.5 12.2 %collective-permute-start.13 = (bf16[2,272,128]{2,1,0:T(8,128)(2,1)S(1)}, bf16[2,272,128]{2,1,0:T(8,128)(2,1)S(1)}, u32[]{:S(2)}, u32[]{:S(2)}) collective-permute-start(bf16[2,272,128]{2,1,0:T(8,128)(2,1)S(1)} %get-tuple-element.44), channel_id=1, source_target_pairs={{0,4},{1,5},{2,6},{3,7},{4,0},{5,1},{6,2},{7,3},{8,12},{9,13},{10,... | collective-permute-start | bytes 417800 | tf_op jit(solution)/shard_map/ppermute | solution.py:34
  42.0 8.6 %collective-permute-start.10 = (bf16[1,272,128]{2,1,0:T(8,128)(2,1)S(1)}, bf16[1,272,128]{2,1,0:T(8,128)(2,1)S(1)}, u32[]{:S(2)}, u32[]{:S(2)}) collective-permute-start(bf16[1,272,128]{2,1,0:T(8,128)(2,1)S(1)} %added.12), channel_id=1, source_target_pairs={{0,8},{1,9},{2,10},{3,11},{4,12},{5,13},{6,14},{7,15},{8,0},{9,1},... | collective-permute-start | bytes 208904 | tf_op jit(solution)/shard_map/ppermute | solution.py:34
  43.7 7.1 %collective-permute-start.15 = (bf16[1,272,128]{2,1,0:T(8,128)(2,1)S(1)}, bf16[1,272,128]{2,1,0:T(8,128)(2,1)S(1)}, u32[]{:S(2)}, u32[]{:S(2)}) collective-permute-start(bf16[1,272,128]{2,1,0:T(8,128)(2,1)S(1)} %added.17), channel_id=1, source_target_pairs={{0,2},{1,3},{2,0},{3,1},{4,6},{5,7},{6,4},{7,5},{8,10},{9,11},{10,... | collective-permute-start | bytes 208904 | tf_op jit(solution)/shard_map/ppermute | solution.py:34
  44.6 12.3 %collective-permute-start.11 = (bf16[1,272,128]{2,1,0:T(8,128)(2,1)S(1)}, bf16[1,272,128]{2,1,0:T(8,128)(2,1)S(1)}, u32[]{:S(2)}, u32[]{:S(2)}) collective-permute-start(bf16[1,272,128]{2,1,0:T(8,128)(2,1)S(1)} %added.14), channel_id=1, source_target_pairs={{0,8},{1,9},{2,10},{3,11},{4,12},{5,13},{6,14},{7,15},{8,0},{9,1},... | collective-permute-start | bytes 208904 | tf_op jit(solution)/shard_map/ppermute | solution.py:34
  46.3 10.6 %collective-permute-start.16 = (bf16[1,272,128]{2,1,0:T(8,128)(2,1)S(1)}, bf16[1,272,128]{2,1,0:T(8,128)(2,1)S(1)}, u32[]{:S(2)}, u32[]{:S(2)}) collective-permute-start(bf16[1,272,128]{2,1,0:T(8,128)(2,1)S(1)} %added.19), channel_id=1, source_target_pairs={{0,2},{1,3},{2,0},{3,1},{4,6},{5,7},{6,4},{7,5},{8,10},{9,11},{10,... | collective-permute-start | bytes 208904 | tf_op jit(solution)/shard_map/ppermute | solution.py:34
  50.7 6.2 %collective-permute-start.12 = (bf16[1,272,128]{2,1,0:T(8,128)(2,1)S(1)}, bf16[1,272,128]{2,1,0:T(8,128)(2,1)S(1)}, u32[]{:S(2)}, u32[]{:S(2)}) collective-permute-start(bf16[1,272,128]{2,1,0:T(8,128)(2,1)S(1)} %get-tuple-element.42), channel_id=1, source_target_pairs={{0,4},{1,5},{2,6},{3,7},{4,0},{5,1},{6,2},{7,3},{8,12},{9,13},{10,... | collective-permute-start | bytes 208904 | tf_op jit(solution)/shard_map/ppermute | solution.py:34
  50.9 6.1 %collective-permute-start.17 = (bf16[1,272,128]{2,1,0:T(8,128)(2,1)S(1)}, bf16[1,272,128]{2,1,0:T(8,128)(2,1)S(1)}, u32[]{:S(2)}, u32[]{:S(2)}) collective-permute-start(bf16[1,272,128]{2,1,0:T(8,128)(2,1)S(1)} %get-tuple-element.48), channel_id=1, source_target_pairs={{0,8},{1,9},{2,10},{3,11},{4,12},{5,13},{6,14},{7,15},{8,0},{9,1},... | collective-permute-start | bytes 208904 | tf_op jit(solution)/shard_map/ppermute | solution.py:34

commit v2 on v0

--- a/solution.py
+++ b/solution.py
@@ -350,12 +350,18 @@
         listed_ref[found] = place
         found = found + (disp == NDISP - 1).astype(jnp.int32)
 
-    @pl.loop(0, lax.div(found + 1, 2))
+    def finish(places):
+        results = [bond(place, lhs_ref.at[index]) for index, place in enumerate(places)]
+        for place, (real, imag) in zip(places, results):
+            store_rounded(out_ref, (place,), real, imag)
+
+    @pl.loop(0, lax.div(found, 2))
     def _(pair):
-        both = [listed_ref[2 * pair], listed_ref[jnp.minimum(2 * pair + 1, found - 1)]]
-        results = [bond(place, lhs_ref.at[index]) for index, place in enumerate(both)]
-        for place, (real, imag) in zip(both, results):
-            store_rounded(out_ref, (place,), real, imag)
+        finish([listed_ref[2 * pair], listed_ref[2 * pair + 1]])
+
+    @pl.when(lax.rem(found, 2) == 1)
+    def _():
+        finish([listed_ref[found - 1]])
 
 
 def layer_items(core, rows, item, own, ahead, phase, turn, scale):
@@ -452,88 +458,84 @@
             del self.entries[r]
 
 
-def mix_kernel(slot_ref, structure_ref, weight_ref, tau_ref, out_ref):
-    spins, _, nvec, width = tau_ref.shape[1:]
-    base = structure_ref[pl.program_id(0)] * spins * spins
+def mix_kernel(index, slot_ref, structure_ref, weight_ref, tau_in, out_ref, tau_ref, sems):
+    spins, parts, nvec, width = out_ref.shape
+    copies = [
+        pltpu.make_async_copy(tau_in.at[slot_ref[index], :, part], tau_ref.at[:, part], sems.at[part])
+        for part in range(parts)
+    ]
+    for copy in copies:
+        copy.start()
+    base = structure_ref[index] * spins * spins
     weight = [[weight_ref[base + r * spins + s] for s in range(spins)] for r in range(spins)]
-
-    @pl.loop(0, 2 * nvec // ROWS)
-    def _(index):
-        part = index // (nvec // ROWS)
-        rows = pl.ds(pl.multiple_of(index % (nvec // ROWS) * ROWS, ROWS), ROWS)
-        tau = [tau_ref[0, s, part, rows, :].astype(jnp.float32) for s in range(spins)]
-        for r in range(spins):
-            mixed = weight[r][0] * tau[0]
-            for s in range(1, spins):
-                mixed = mixed + weight[r][s] * tau[s]
-            out_ref[0, r, part, rows, :] = mixed.astype(jnp.bfloat16)
-
-
-def mixed_perambulators(slots, structures, weights, perambulators):
-    block = (1,) + perambulators.shape[1:]
-    count = slots.shape[0]
+    for part in range(parts):
+        copies[part].wait()
+
+        @pl.loop(0, nvec // ROWS)
+        def _(step):
+            rows = pl.ds(pl.multiple_of(step * ROWS, ROWS), ROWS)
+            tau = [tau_ref[s, part, rows, :].astype(jnp.float32) for s in range(spins)]
+            for r in range(spins):
+                mixed = weight[r][0] * tau[0]
+                for s in range(1, spins):
+                    mixed = mixed + weight[r][s] * tau[s]
+                out_ref[r, part, rows, :] = mixed.astype(jnp.bfloat16)
+
+
+def mixed_perambulator(index, slots, structures, weights, perambulators):
+    shape = perambulators.shape[1:]
+    scalar = pl.BlockSpec(memory_space=pltpu.SMEM)
     return pl.pallas_call(
-        mix_kernel,
-        grid_spec=pltpu.PrefetchScalarGridSpec(
-            num_scalar_prefetch=3,
-            grid=(count,),
-            in_specs=[pl.BlockSpec(block, lambda j, slot, *_: (slot[j], 0, 0, 0, 0))],
-            out_specs=pl.BlockSpec(block, lambda j, *_: (j, 0, 0, 0, 0)),
-        ),
-        out_shape=jax.ShapeDtypeStruct((count,) + perambulators.shape[1:], jnp.bfloat16),
+        functools.partial(mix_kernel, index),
+        in_specs=[scalar] * 3 + [pl.BlockSpec(memory_space=pltpu.HBM)],
+        out_specs=pl.BlockSpec(memory_space=pltpu.VMEM),
+        out_shape=jax.ShapeDtypeStruct(shape, jnp.bfloat16),
+        scratch_shapes=[pltpu.VMEM(shape, jnp.bfloat16), pltpu.SemaphoreType.DMA(shape[1:2])],
         compiler_params=pltpu.CompilerParams(vmem_limit_bytes=8 * MIB),
         cost_estimate=pl.CostEstimate(
-            flops=8 * perambulators.size, bytes_accessed=4 * perambulators.size, transcendentals=0
+            flops=8 * math.prod(shape), bytes_accessed=4 * math.prod(shape), transcendentals=0
         ),
-        name="mixed_perambulators",
+        name="mixed_perambulator",
     )(slots, structures, weights, in_hbm(perambulators))
 
 
-def diagram_kernel(places, *refs):
-    tau_ref, out_ref, block_ref, sems = refs[-4:]
-    count, spins, _, nvec, width = tau_ref.shape
-
-    def copy(index, r):
-        return pltpu.make_async_copy(block_ref.at[index, r], out_ref.at[index, r], sems.at[index, r])
-
-    for index, entry in enumerate(places):
-        real, imag = restored(sum(refs[number][at].astype(jnp.float32) for number, at in entry))
-        square = jnp.concatenate(
-            [jnp.concatenate([real, -imag], 1), jnp.concatenate([imag, real], 1)], 0
-        ).astype(jnp.bfloat16)
-        for r in range(spins):
-            tau = tau_ref[index, r].reshape(2 * nvec, width)
-            block = jnp.dot(square, tau, preferred_element_type=jnp.float32)
-            block_ref[index, r] = block.astype(jnp.bfloat16).reshape(2, nvec, width)
-            copy(index, r).start()
-    for index in range(count):
-        for r in range(spins):
-            copy(index, r).wait()
-
-
-def diagrams(entries, tau):
-    count, spins, _, nvec, width = tau.shape
+def diagram_kernel(index, places, *refs):
+    tau_ref = refs[len(places)]
+    out_ref, block_ref, sems = refs[-3:]
+    spins, _, nvec, width = tau_ref.shape
+    real, imag = restored(sum(ref[at].astype(jnp.float32) for ref, at in zip(refs, places)))
+    square = jnp.concatenate(
+        [jnp.concatenate([real, -imag], 1), jnp.concatenate([imag, real], 1)], 0
+    ).astype(jnp.bfloat16)
+    copies = [
+        pltpu.make_async_copy(block_ref.at[r], out_ref.at[index, r], sems.at[r]) for r in range(spins)
+    ]
+    for r in range(spins):
+        tau = tau_ref[r].reshape(2 * nvec, width)
+        block = jnp.dot(square, tau, preferred_element_type=jnp.float32)
+        block_ref[r] = block.astype(jnp.bfloat16).reshape(2, nvec, width)
+        copies[r].start()
+    for copy in copies:
+        copy.wait()
+
+
+def diagram(index, count, entry, tau, before):
     whole = pl.BlockSpec(memory_space=pltpu.VMEM)
-    arrays = [array for entry in entries for array, _ in entry]
-    places = []
-    for entry in entries:
-        start = sum(len(one) for one in places)
-        places.append([(start + number, at) for number, (_, at) in enumerate(entry)])
+    large = pl.BlockSpec(memory_space=pltpu.HBM)
+    earlier = [] if before is None else [before]
     return pl.pallas_call(
-        functools.partial(diagram_kernel, places),
-        in_specs=[whole] * (len(arrays) + 1),
-        out_specs=pl.BlockSpec(memory_space=pltpu.HBM),
-        out_shape=jax.ShapeDtypeStruct(tau.shape, jnp.bfloat16),
-        scratch_shapes=[
-            pltpu.VMEM(tau.shape, jnp.bfloat16),
-            pltpu.SemaphoreType.DMA((count, spins)),
-        ],
+        functools.partial(diagram_kernel, index, [at for _, at in entry]),
+        in_specs=[whole] * (len(entry) + 1) + [large] * len(earlier),
+        out_specs=large,
+        out_shape=jax.ShapeDtypeStruct((count,) + tau.shape, jnp.bfloat16),
+        scratch_shapes=[pltpu.VMEM(tau.shape, jnp.bfloat16), pltpu.SemaphoreType.DMA(tau.shape[:1])],
+        input_output_aliases={len(entry) + 1: 0} if earlier else {},
         compiler_params=pltpu.CompilerParams(vmem_limit_bytes=8 * MIB),
         cost_estimate=pl.CostEstimate(
-            flops=8 * nvec * nvec * width * spins * count, bytes_accessed=4 * tau.size, transcendentals=0
+            flops=8 * tau.shape[2] * tau.size, bytes_accessed=4 * tau.size, transcendentals=0
         ),
-        name="diagrams",
-    )(*arrays, tau)
+        name="diagram",
+    )(*[array for array, _ in entry], tau, *earlier)
 
 
 def body(eigvecs, gauge_links, momenta, spin_mix, perambulators, contraction_list):
@@ -551,7 +553,11 @@
     links = gauge_links.reshape(slices, 3, 2, NCOL, NCOL, 1, width)
     item, own, phase, turn = plane_items(place, momenta, vectors, links, total_z, plane, scale)
     chosen = contraction_list[:, 2] - position * perambulators.shape[0]
-    tau = mixed_perambulators(chosen, contraction_list[:, 1], spin_mix.reshape(-1), perambulators)
+    weights = spin_mix.reshape(-1)
+    taus = [
+        mixed_perambulator(j, chosen, contraction_list[:, 1], weights, perambulators)
+        for j in range(contraction_list.shape[0])
+    ]
     ahead = jnp.concatenate([eigvecs[:, :, :, :, 1:, :], upper], 4).reshape(vectors.shape)
     send = layer_items(1, rows, item, own, ahead, phase, turn, scale)
     keep = layer_items(0, rows, item, own, ahead, phase, turn, scale)
@@ -567,10 +573,18 @@
     ]
     for step in range(bits - 1):
         messages = [chain.chunks(step) for chain in chains]
+        if step == bits - 2:
+            terms = chains[0].entries[messages[0][0][0]]
+            (array, at) = terms[-1]
+            array, taus[0] = lax.optimization_barrier((array, taus[0]))
+            terms[-1] = (array, at)
         for part in range(len(messages[0])):
             for chain, far in zip(chains, messages):
                 chain.send(step, far[part])
-    return diagrams([chain.entries[0] for chain in chains], tau)
+    out = None
+    for slot, chain in enumerate(chains):
+        out = diagram(slot, len(chains), chain.entries[0], taus[slot], out)
+    return out
 
 
 def solution(mesh):

time: 59.2 us -> 62.1 us (1.049)
  waiting for transfers between devices: 9.05 us -> 4.01 us
  Pallas kernels: 25.9 us -> 30.9 us
  local copies, waits for them, and re-layouts: 0.26 us -> 3.51 us
    ppermute x17, waiting for transfers between devices: 9.05 us -> 4.01 us  [exchanged(): return lax.ppermute(value, SITES, [(i, i ^ mask) for i in range(size)])]
    unnamed x8 -> x16, local copies, waits for them, and re-layouts: 0.14 us -> 3.39 us
    pallas_call x10, Pallas kernels: 0.74 us -> 3.27 us  [added(): pl.pallas_call(functools.partial(add_kernel, places), in_specs=[whole] *...]
    pallas_call x2 -> x4, Pallas kernels: 5 us -> 7.04 us  [the longest x2 4.57 us: mixed_perambulator(): pl.pallas_call(functools.partial(mix_kernel, index), in_specs=[scalar] *...]
  transfers between devices with their start and end apart: 18 -> 18, of which waited for: 5 -> 3; matrix products, arithmetic and copies ran while one was open for 2% -> 2% of each run, Pallas kernels for 35% -> 43%
where the time goes in v2:
time: 62.1 us; the launch traced here: 62.5 us
  Pallas kernels  30.9 us (50%)
  starting transfers between devices  22.9 us (37%)
  waiting for transfers between devices  4.01 us (6%)
  local copies, waits for them, and re-layouts  3.51 us (6%)
  other arithmetic  0.9 us (1%)
    ppermute x17, starting transfers between devices, exchanged(): return lax.ppermute(value, SITES, [(i, i ^ mask) for i in range(size)])  20.2 us
    pallas_call x1, Pallas kernels, plane_items(): pl.pallas_call(functools.partial(plane_kernel, total_z, plane, scale), gr...  15.1 us
    pallas_call x2, Pallas kernels, layer_items(): pl.pallas_call(functools.partial(layer_kernel, core, scale), in_specs=[pl...  5.46 us
    pallas_call x2, Pallas kernels, mixed_perambulator(): pl.pallas_call(functools.partial(mix_kernel, index), in_specs=[scalar] *...  4.57 us
    ppermute x17, waiting for transfers between devices, exchanged(): return lax.ppermute(value, SITES, [(i, i ^ mask) for i in range(size)])  4.01 us
    unnamed x16, local copies, waits for them, and re-layouts  3.39 us
    pallas_call x10, Pallas kernels, added(): pl.pallas_call(functools.partial(add_kernel, places), in_specs=[whole] *...  3.27 us
    ppermute x1, starting transfers between devices, shifted(): lax.ppermute(value, axis, [(i, (i + by) % size) for i in range(size)])  2.75 us
  transfers between devices with their start and end apart: 18, of which 3 were waited for; matrix products, arithmetic and copies ran while one was open for 2% of the time, Pallas kernels for 43%

profile of v2, /device:TPU:0, one launch (start us, length us, event | category | flops | bytes accessed | tf_op | source)
XLA Modules:
  0.0 62.5 jit_solution(5599830263427761264)
XLA Ops:
  0.0 2.4 %collective-permute-start = (s32[1,2,3]{2,1,0:T(2,128)}, s32[1,2,3]{2,1,0:T(2,128)S(1)}, u32[]{:S(2)}, u32[]{:S(2)}) collective-permute-start(s32[1,2,3]{2,1,0:T(2,128)} %bitcast.7), channel_id=1, source_target_pairs={{0,3},{1,2},{2,1},{3,0},{4,7},{5,6},{6,5},{7,4},{8,11},{9,10},{10,... | collective-permute-start | bytes 80 | tf_op jit(solution)/shard_map/ppermute | solution.py:34
  3.1 0.8 %collective-permute-done = s32[1,2,3]{2,1,0:T(2,128)S(1)} collective-permute-done((s32[1,2,3]{2,1,0:T(2,128)}, s32[1,2,3]{2,1,0:T(2,128)S(1)}, u32[]{:S(2)}, u32[]{:S(2)}) %collective-permute-start) | collective-permute-done | bytes 56 | tf_op jit(solution)/shard_map/ppermute | solution.py:34
  3.9 2.3 %collective-permute-done.1 = s32[1,2,3]{2,1,0:T(2,128)S(1)} collective-permute-done((s32[1,2,3]{2,1,0:T(2,128)}, s32[1,2,3]{2,1,0:T(2,128)S(1)}, u32[]{:S(2)}, u32[]{:S(2)}) %collective-permute-start.1) | collective-permute-done | bytes 56 | tf_op jit(solution)/shard_map/ppermute | solution.py:34
  6.2 2.7 %collective-permute-start.6 = (bf16[4,2,3,128,1,256]{5,3,2,1,0,4:T(8,128)(2,1)}, bf16[4,2,3,128,1,256]{5,3,2,1,0,4:T(8,128)(2,1)S(1)}, u32[]{:S(2)}, u32[]{:S(2)}) collective-permute-start(bf16[4,2,3,128,1,256]{5,3,2,1,0,4:T(8,128)(2,1)} %bitcast.11), channel_id=1, source_target_pairs={{0,15},{1,0},{2,1},{3,2},{4,3},{5,4},{6,5},{7,6},{8,7},{9,8},{10,9... | collective-permute-start | bytes 4718600 | tf_op jit(solution)/shard_map/ppermute | solution.py:25
  9.6 1.4 %collective-permute-start.4 = (s32[4,2,3]{2,1,0:T(2,128)S(1)}, s32[4,2,3]{2,1,0:T(2,128)S(1)}, u32[]{:S(2)}, u32[]{:S(2)}) collective-permute-start(s32[4,2,3]{2,1,0:T(2,128)S(1)} %pad_add_fusion), channel_id=1, source_target_pairs={{0,8},{1,9},{2,10},{3,11},{4,12},{5,13},{6,14},{7,15},{8,0},{9,1},... | collective-permute-start | bytes 296 | tf_op jit(solution)/shard_map/ppermute | solution.py:34
  11.0 3.0 %collective-permute-start.5 = (s32[4,2,3]{2,1,0:T(2,128)S(1)}, s32[4,2,3]{2,1,0:T(2,128)S(1)}, u32[]{:S(2)}, u32[]{:S(2)}) collective-permute-start(s32[4,2,3]{2,1,0:T(2,128)S(1)} %pad_add_fusion), channel_id=1, source_target_pairs={{0,12},{1,13},{2,14},{3,15},{4,8},{5,9},{6,10},{7,11},{8,4},{9,5},... | collective-permute-start | bytes 296 | tf_op jit(solution)/shard_map/ppermute | solution.py:34
  14.0 15.1 %plane_items.1 = (bf16[4,4,3,272,128]{4,3,2,1,0:T(8,128)(2,1)S(1)}, f32[4,2,3,128,256]{4,3,2,1,0:T(8,128)S(1)}, f32[4,2,1,256]{3,2,1,0:T(1,128)S(1)}, f32[4,2,1,128]{3,2,1,0:T(1,128)S(1)}) custom-call(s32[1]{0:T(128)} %bitcast.1.position_ref, s32[4,3]{1,0:T(4,128)} %momenta_in.1, bf16[4,2,3,128,256]{4,3,2,1,0:T(8,128)(2,1)} %bitcast.12, ...), custom_call_target="tpu_custom_call" | custom-call | flops 3221225472 | bytes 4939776 | tf_op jit(solution)/shard_map/plane_items/pallas_call | solution.py:260
  29.2 2.3 %layer_items.3 = bf16[16,272,128]{2,1,0:T(8,128)(2,1)S(1)} custom-call(s32[16,2,3]{2,1,0:T(2,128)S(1)} %constant_dynamic-update-slice_fusion.rows_ref, bf16[4,4,3,272,128]{4,3,2,1,0:T(8,128)(2,1)S(1)} %get-tuple-element.34.item_ref, f32[4,2,3,128,256]{4,3,2,1,0:T(8,128)S(1)} %get-tuple-element.35.own_ref, bf16[4,2,3,128,256]{4,3,2,1,0:T(8,128)(2,1)S(1)} %bitcast.5, ...), custom_call_target="tpu_custom_call" | custom-call | flops 805306368 | bytes 1572864 | tf_op jit(solution)/shard_map/layer_items/pallas_call | solution.py:372
  31.6 1.1 %copy-done = bf16[4,2,3,128,1,256]{5,3,2,1,0,4:T(8,128)(2,1)} copy-done((bf16[4,2,3,128,1,256]{5,3,2,1,0,4:T(8,128)(2,1)}, bf16[4,2,3,128,1,256]{5,3,2,1,0,4:T(8,128)(2,1)S(1)}, u32[]{:S(2)}) %copy-start) | copy-done | bytes 1572888
  32.7 1.4 %copy-done.1 = bf16[4,2,3,128,1,256]{5,3,2,1,0,4:T(8,128)(2,1)S(1)} copy-done((bf16[4,2,3,128,1,256]{5,3,2,1,0,4:T(8,128)(2,1)S(1)}, bf16[4,2,3,128,1,256]{5,3,2,1,0,4:T(8,128)(2,1)}, u32[]{:S(2)}) %copy-start.1) | copy-done | bytes 1572888
  34.1 3.2 %layer_items.2.refs_0_ = bf16[16,272,128]{2,1,0:T(8,128)(2,1)S(1)} custom-call(s32[16,2,3]{2,1,0:T(2,128)S(1)} %constant_dynamic-update-slice_fusion.rows_ref, bf16[4,4,3,272,128]{4,3,2,1,0:T(8,128)(2,1)S(1)} %get-tuple-element.34.item_ref, f32[4,2,3,128,256]{4,3,2,1,0:T(8,128)S(1)} %get-tuple-element.35.own_ref, bf16[4,2,3,128,256]{4,3,2,1,0:T(8,128)(2,1)S(1)} %bitcast.6, ...), custom_call_target="tpu_custom_call" | custom-call | flops 805306368 | bytes 1572864 | tf_op jit(solution)/shard_map/layer_items/pallas_call | solution.py:372
  37.3 0.7 %added.11 = (bf16[2,272,128]{2,1,0:T(8,128)(2,1)}, f32[2,272,128]{2,1,0:T(8,128)S(1)}) custom-call(bf16[16,272,128]{2,1,0:T(8,128)(2,1)S(1)} %layer_items.2.refs_0_, bf16[16,272,128]{2,1,0:T(8,128)(2,1)S(1)} %collective-permute-done.7.refs_1_), custom_call_target="tpu_custom_call" | custom-call | flops 278528 | bytes 1114112 | tf_op jit(solution)/shard_map/added/pallas_call | solution.py:416
  41.2 1.6 %collective-permute-start.13 = (bf16[2,272,128]{2,1,0:T(8,128)(2,1)}, bf16[2,272,128]{2,1,0:T(8,128)(2,1)S(1)}, u32[]{:S(2)}, u32[]{:S(2)}) collective-permute-start(bf16[2,272,128]{2,1,0:T(8,128)(2,1)} %get-tuple-element.46), channel_id=1, source_target_pairs={{0,2},{1,3},{2,0},{3,1},{4,6},{5,7},{6,4},{7,5},{8,10},{9,11},{10,... | collective-permute-start | bytes 417800 | tf_op jit(solution)/shard_map/ppermute | solution.py:34
  42.8 0.7 %added.10 = (bf16[2,272,128]{2,1,0:T(8,128)(2,1)}, f32[2,272,128]{2,1,0:T(8,128)S(1)}) custom-call(bf16[16,272,128]{2,1,0:T(8,128)(2,1)S(1)} %layer_items.2.refs_0_, bf16[16,272,128]{2,1,0:T(8,128)(2,1)S(1)} %collective-permute-done.7.refs_1_), custom_call_target="tpu_custom_call" | custom-call | flops 278528 | bytes 1114112 | tf_op jit(solution)/shard_map/added/pallas_call | solution.py:416
  43.5 1.5 %collective-permute-start.8 = (bf16[2,272,128]{2,1,0:T(8,128)(2,1)}, bf16[2,272,128]{2,1,0:T(8,128)(2,1)S(1)}, u32[]{:S(2)}, u32[]{:S(2)}) collective-permute-start(bf16[2,272,128]{2,1,0:T(8,128)(2,1)} %get-tuple-element.40), channel_id=1, source_target_pairs={{0,4},{1,5},{2,6},{3,7},{4,0},{5,1},{6,2},{7,3},{8,12},{9,13},{10,... | collective-permute-start | bytes 417800 | tf_op jit(solution)/shard_map/ppermute | solution.py:34
  45.1 0.9 %collective-permute-done.14.refs_1_ = bf16[2,272,128]{2,1,0:T(8,128)(2,1)S(1)} collective-permute-done((bf16[2,272,128]{2,1,0:T(8,128)(2,1)}, bf16[2,272,128]{2,1,0:T(8,128)(2,1)S(1)}, u32[]{:S(2)}, u32[]{:S(2)}) %collective-permute-start.14) | collective-permute-done | bytes 139296 | tf_op jit(solution)/shard_map/ppermute | solution.py:34
  46.1 2.2 %collective-permute-start.15 = (bf16[1,272,128]{2,1,0:T(8,128)(2,1)S(1)}, bf16[1,272,128]{2,1,0:T(8,128)(2,1)S(1)}, u32[]{:S(2)}, u32[]{:S(2)}) collective-permute-start(bf16[1,272,128]{2,1,0:T(8,128)(2,1)S(1)} %added.17), channel_id=1, source_target_pairs={{0,8},{1,9},{2,10},{3,11},{4,12},{5,13},{6,14},{7,15},{8,0},{9,1},... | collective-permute-start | bytes 208904 | tf_op jit(solution)/shard_map/ppermute | solution.py:34
  48.7 2.3 %mixed_perambulator.3.refs_3_ = bf16[4,2,128,512]{3,2,1,0:T(8,128)(2,1)S(1)} custom-call(s32[2]{0:T(128)S(1)} %get-tuple-element.54.slot_ref, s32[2]{0:T(128)S(1)} %get-tuple-element.53.structure_ref, f32[256]{0:T(256)S(1)} %reshape.17.weight_ref, bf16[2,4,2,128,512]{4,3,2,1,0:T(8,128)(2,1)} %tau_in.3), custom_call_target="tpu_custom_call" | custom-call | flops 4194304 | bytes 2097152 | tf_op jit(solution)/shard_map/mixed_perambulator/pallas_call | solution.py:488
  51.0 0.9 %collective-permute-start.16 = (bf16[1,272,128]{2,1,0:T(8,128)(2,1)S(1)}, bf16[1,272,128]{2,1,0:T(8,128)(2,1)S(1)}, u32[]{:S(2)}, u32[]{:S(2)}) collective-permute-start(bf16[1,272,128]{2,1,0:T(8,128)(2,1)S(1)} %added.19), channel_id=1, source_target_pairs={{0,8},{1,9},{2,10},{3,11},{4,12},{5,13},{6,14},{7,15},{8,0},{9,1},... | collective-permute-start | bytes 208904 | tf_op jit(solution)/shard_map/ppermute | solution.py:34
  52.0 1.9 %collective-permute-start.17 = (bf16[1,272,128]{2,1,0:T(8,128)(2,1)S(1)}, bf16[1,272,128]{2,1,0:T(8,128)(2,1)S(1)}, u32[]{:S(2)}, u32[]{:S(2)}) collective-permute-start(bf16[1,272,128]{2,1,0:T(8,128)(2,1)S(1)} %get-tuple-element.51), channel_id=1, source_target_pairs={{0,4},{1,5},{2,6},{3,7},{4,0},{5,1},{6,2},{7,3},{8,12},{9,13},{10,... | collective-permute-start | bytes 208904 | tf_op jit(solution)/shard_map/ppermute | solution.py:34
  54.4 3.3 %collective-permute-start.12 = (bf16[1,272,128]{2,1,0:T(8,128)(2,1)S(1)}, bf16[1,272,128]{2,1,0:T(8,128)(2,1)S(1)}, u32[]{:S(2)}, u32[]{:S(2)}) collective-permute-start(bf16[1,272,128]{2,1,0:T(8,128)(2,1)S(1)} %get-tuple-element.44), channel_id=1, source_target_pairs={{0,8},{1,9},{2,10},{3,11},{4,12},{5,13},{6,14},{7,15},{8,0},{9,1},... | collective-permute-start | bytes 208904 | tf_op jit(solution)/shard_map/ppermute | solution.py:34
  57.7 2.3 %mixed_perambulator.2.refs_3_ = bf16[4,2,128,512]{3,2,1,0:T(8,128)(2,1)S(1)} custom-call(s32[2]{0:T(128)S(1)} %get-tuple-element.54.slot_ref, s32[2]{0:T(128)S(1)} %get-tuple-element.53.structure_ref, f32[256]{0:T(256)S(1)} %reshape.17.weight_ref, bf16[2,4,2,128,512]{4,3,2,1,0:T(8,128)(2,1)} %tau_in.3), custom_call_target="tpu_custom_call" | custom-call | flops 4194304 | bytes 2097152 | tf_op jit(solution)/shard_map/mixed_perambulator/pallas_call | solution.py:488
  60.0 1.2 %diagram.2.refs_4_ = bf16[2,4,2,128,512]{4,3,2,1,0:T(8,128)(2,1)} custom-call(f32[1,272,128]{2,1,0:T(8,128)S(1)} %get-tuple-element.50.refs_0_, bf16[1,272,128]{2,1,0:T(8,128)(2,1)S(1)} %collective-permute-done.16.refs_1_, bf16[1,272,128]{2,1,0:T(8,128)(2,1)S(1)} %collective-permute-done.17.refs_2_, bf16[4,2,128,512]{3,2,1,0:T(8,128)(2,1)S(1)} %mixed_perambulator.3.refs_3_), custom_call_target="tpu_custom_call" | custom-call | flops 536870912 | bytes 2097152 | tf_op jit(solution)/shard_map/diagram/pallas_call | solution.py:526
  61.2 1.2 %diagram.3 = bf16[2,4,2,128,512]{4,3,2,1,0:T(8,128)(2,1)} custom-call(f32[1,272,128]{2,1,0:T(8,128)S(1)} %get-tuple-element.43.refs_0_, bf16[1,272,128]{2,1,0:T(8,128)(2,1)S(1)} %collective-permute-done.11.refs_1_, bf16[1,272,128]{2,1,0:T(8,128)(2,1)S(1)} %collective-permute-done.12.refs_2_, ...), custom_call_target="tpu_custom_call", output_to_operand_aliasing={{}: (4, {})} | custom-call | flops 536870912 | bytes 2097152 | tf_op jit(solution)/shard_map/diagram/pallas_call | solution.py:526
  (49 shorter events, 5.8 us)
Async XLA Ops:
  0.0 3.9 %collective-permute-start = (s32[1,2,3]{2,1,0:T(2,128)}, s32[1,2,3]{2,1,0:T(2,128)S(1)}, u32[]{:S(2)}, u32[]{:S(2)}) collective-permute-start(s32[1,2,3]{2,1,0:T(2,128)} %bitcast.7), channel_id=1, source_target_pairs={{0,3},{1,2},{2,1},{3,0},{4,7},{5,6},{6,5},{7,4},{8,11},{9,10},{10,... | collective-permute-start | bytes 80 | tf_op jit(solution)/shard_map/ppermute | solution.py:34
  2.4 3.8 %collective-permute-start.1 = (s32[1,2,3]{2,1,0:T(2,128)}, s32[1,2,3]{2,1,0:T(2,128)S(1)}, u32[]{:S(2)}, u32[]{:S(2)}) collective-permute-start(s32[1,2,3]{2,1,0:T(2,128)} %bitcast.8), channel_id=1, source_target_pairs={{0,2},{1,3},{2,0},{3,1},{4,6},{5,7},{6,4},{7,5},{8,10},{9,11},{10,... | collective-permute-start | bytes 80 | tf_op jit(solution)/shard_map/ppermute | solution.py:34
  3.0 3.2 %collective-permute-start.2 = (s32[1,2,3]{2,1,0:T(2,128)}, s32[1,2,3]{2,1,0:T(2,128)S(1)}, u32[]{:S(2)}, u32[]{:S(2)}) collective-permute-start(s32[1,2,3]{2,1,0:T(2,128)} %bitcast.9), channel_id=1, source_target_pairs={{0,1},{1,0},{2,3},{3,2},{4,5},{5,4},{6,7},{7,6},{8,9},{9,8},{10,11... | collective-permute-start | bytes 80 | tf_op jit(solution)/shard_map/ppermute | solution.py:34
  6.2 23.0 %collective-permute-start.6 = (bf16[4,2,3,128,1,256]{5,3,2,1,0,4:T(8,128)(2,1)}, bf16[4,2,3,128,1,256]{5,3,2,1,0,4:T(8,128)(2,1)S(1)}, u32[]{:S(2)}, u32[]{:S(2)}) collective-permute-start(bf16[4,2,3,128,1,256]{5,3,2,1,0,4:T(8,128)(2,1)} %bitcast.11), channel_id=1, source_target_pairs={{0,15},{1,0},{2,1},{3,2},{4,3},{5,4},{6,5},{7,6},{8,7},{9,8},{10,9... | collective-permute-start | bytes 4718600 | tf_op jit(solution)/shard_map/ppermute | solution.py:25
  9.6 19.5 %collective-permute-start.3 = (s32[4,2,3]{2,1,0:T(2,128)S(1)}, s32[4,2,3]{2,1,0:T(2,128)S(1)}, u32[]{:S(2)}, u32[]{:S(2)}) collective-permute-start(s32[4,2,3]{2,1,0:T(2,128)S(1)} %pad_add_fusion), channel_id=1, source_target_pairs={{0,4},{1,5},{2,6},{3,7},{4,0},{5,1},{6,2},{7,3},{8,12},{9,13},{10,... | collective-permute-start | bytes 296 | tf_op jit(solution)/shard_map/ppermute | solution.py:34
  9.6 19.6 %collective-permute-start.4 = (s32[4,2,3]{2,1,0:T(2,128)S(1)}, s32[4,2,3]{2,1,0:T(2,128)S(1)}, u32[]{:S(2)}, u32[]{:S(2)}) collective-permute-start(s32[4,2,3]{2,1,0:T(2,128)S(1)} %pad_add_fusion), channel_id=1, source_target_pairs={{0,8},{1,9},{2,10},{3,11},{4,12},{5,13},{6,14},{7,15},{8,0},{9,1},... | collective-permute-start | bytes 296 | tf_op jit(solution)/shard_map/ppermute | solution.py:34
  11.0 18.2 %collective-permute-start.5 = (s32[4,2,3]{2,1,0:T(2,128)S(1)}, s32[4,2,3]{2,1,0:T(2,128)S(1)}, u32[]{:S(2)}, u32[]{:S(2)}) collective-permute-start(s32[4,2,3]{2,1,0:T(2,128)S(1)} %pad_add_fusion), channel_id=1, source_target_pairs={{0,12},{1,13},{2,14},{3,15},{4,8},{5,9},{6,10},{7,11},{8,4},{9,5},... | collective-permute-start | bytes 296 | tf_op jit(solution)/shard_map/ppermute | solution.py:34
  31.5 1.1 %copy-start = (bf16[4,2,3,128,1,256]{5,3,2,1,0,4:T(8,128)(2,1)}, bf16[4,2,3,128,1,256]{5,3,2,1,0,4:T(8,128)(2,1)S(1)}, u32[]{:S(2)}) copy-start(bf16[4,2,3,128,1,256]{5,3,2,1,0,4:T(8,128)(2,1)S(1)} %collective-permute-done.6) | copy-start | bytes 4718596
  32.7 4.6 %collective-permute-start.7 = (bf16[16,272,128]{2,1,0:T(8,128)(2,1)S(1)}, bf16[16,272,128]{2,1,0:T(8,128)(2,1)S(1)}, u32[]{:S(2)}, u32[]{:S(2)}) collective-permute-start(bf16[16,272,128]{2,1,0:T(8,128)(2,1)S(1)} %layer_items.3), channel_id=1, source_target_pairs={{0,1},{1,0},{2,3},{3,2},{4,5},{5,4},{6,7},{7,6},{8,9},{9,8},{10,11... | collective-permute-start | bytes 3342344 | tf_op jit(solution)/shard_map/ppermute | solution.py:34
  32.7 1.4 %copy-start.1 = (bf16[4,2,3,128,1,256]{5,3,2,1,0,4:T(8,128)(2,1)S(1)}, bf16[4,2,3,128,1,256]{5,3,2,1,0,4:T(8,128)(2,1)}, u32[]{:S(2)}) copy-start(bf16[4,2,3,128,1,256]{5,3,2,1,0,4:T(8,128)(2,1)} %copy-done) | copy-start | bytes 4718596
  38.0 7.0 %collective-permute-start.9 = (bf16[2,272,128]{2,1,0:T(8,128)(2,1)}, bf16[2,272,128]{2,1,0:T(8,128)(2,1)S(1)}, u32[]{:S(2)}, u32[]{:S(2)}) collective-permute-start(bf16[2,272,128]{2,1,0:T(8,128)(2,1)} %get-tuple-element.42), channel_id=1, source_target_pairs={{0,4},{1,5},{2,6},{3,7},{4,0},{5,1},{6,2},{7,3},{8,12},{9,13},{10,... | collective-permute-start | bytes 417800 | tf_op jit(solution)/shard_map/ppermute | solution.py:34
  39.3 6.7 %collective-permute-start.14 = (bf16[2,272,128]{2,1,0:T(8,128)(2,1)}, bf16[2,272,128]{2,1,0:T(8,128)(2,1)S(1)}, u32[]{:S(2)}, u32[]{:S(2)}) collective-permute-start(bf16[2,272,128]{2,1,0:T(8,128)(2,1)} %get-tuple-element.48), channel_id=1, source_target_pairs={{0,2},{1,3},{2,0},{3,1},{4,6},{5,7},{6,4},{7,5},{8,10},{9,11},{10,... | collective-permute-start | bytes 417800 | tf_op jit(solution)/shard_map/ppermute | solution.py:34
  40.5 0.7 %copy-start.2 = (f32[2,272,128]{2,1,0:T(8,128)}, f32[2,272,128]{2,1,0:T(8,128)S(1)}, u32[]{:S(2)}) copy-start(f32[2,272,128]{2,1,0:T(8,128)S(1)} %get-tuple-element.45.refs_0_) | copy-start | bytes 835588
  41.2 7.0 %copy-start.4 = (s32[2,3]{1,0:T(2,128)S(1)}, s32[2,3]{1,0:T(2,128)}, u32[]{:S(2)}) copy-start(s32[2,3]{1,0:T(2,128)} %param.11) | copy-start | bytes 76
  41.2 7.3 %copy-start.5 = (f32[16,4,4]{0,2,1:T(4,128)S(1)}, f32[16,4,4]{0,2,1:T(4,128)}, u32[]{:S(2)}) copy-start(f32[16,4,4]{0,2,1:T(4,128)} %param.9) | copy-start | bytes 3076
  41.2 10.7 %collective-permute-start.13 = (bf16[2,272,128]{2,1,0:T(8,128)(2,1)}, bf16[2,272,128]{2,1,0:T(8,128)(2,1)S(1)}, u32[]{:S(2)}, u32[]{:S(2)}) collective-permute-start(bf16[2,272,128]{2,1,0:T(8,128)(2,1)} %get-tuple-element.46), channel_id=1, source_target_pairs={{0,2},{1,3},{2,0},{3,1},{4,6},{5,7},{6,4},{7,5},{8,10},{9,11},{10,... | collective-permute-start | bytes 417800 | tf_op jit(solution)/shard_map/ppermute | solution.py:34
  43.5 10.8 %collective-permute-start.8 = (bf16[2,272,128]{2,1,0:T(8,128)(2,1)}, bf16[2,272,128]{2,1,0:T(8,128)(2,1)S(1)}, u32[]{:S(2)}, u32[]{:S(2)}) collective-permute-start(bf16[2,272,128]{2,1,0:T(8,128)(2,1)} %get-tuple-element.40), channel_id=1, source_target_pairs={{0,4},{1,5},{2,6},{3,7},{4,0},{5,1},{6,2},{7,3},{8,12},{9,13},{10,... | collective-permute-start | bytes 417800 | tf_op jit(solution)/shard_map/ppermute | solution.py:34
  45.0 9.3 %collective-permute-start.10 = (bf16[1,272,128]{2,1,0:T(8,128)(2,1)S(1)}, bf16[1,272,128]{2,1,0:T(8,128)(2,1)S(1)}, u32[]{:S(2)}, u32[]{:S(2)}) collective-permute-start(bf16[1,272,128]{2,1,0:T(8,128)(2,1)S(1)} %added.12), channel_id=1, source_target_pairs={{0,2},{1,3},{2,0},{3,1},{4,6},{5,7},{6,4},{7,5},{8,10},{9,11},{10,... | collective-permute-start | bytes 208904 | tf_op jit(solution)/shard_map/ppermute | solution.py:34
  46.0 5.9 %copy-start.3 = (f32[2,272,128]{2,1,0:T(8,128)S(1)}, f32[2,272,128]{2,1,0:T(8,128)}, u32[]{:S(2)}) copy-start(f32[2,272,128]{2,1,0:T(8,128)} %copy-done.2) | copy-start | bytes 835588
  46.1 5.9 %collective-permute-start.15 = (bf16[1,272,128]{2,1,0:T(8,128)(2,1)S(1)}, bf16[1,272,128]{2,1,0:T(8,128)(2,1)S(1)}, u32[]{:S(2)}, u32[]{:S(2)}) collective-permute-start(bf16[1,272,128]{2,1,0:T(8,128)(2,1)S(1)} %added.17), channel_id=1, source_target_pairs={{0,8},{1,9},{2,10},{3,11},{4,12},{5,13},{6,14},{7,15},{8,0},{9,1},... | collective-permute-start | bytes 208904 | tf_op jit(solution)/shard_map/ppermute | solution.py:34
  51.0 8.9 %collective-permute-start.16 = (bf16[1,272,128]{2,1,0:T(8,128)(2,1)S(1)}, bf16[1,272,128]{2,1,0:T(8,128)(2,1)S(1)}, u32[]{:S(2)}, u32[]{:S(2)}) collective-permute-start(bf16[1,272,128]{2,1,0:T(8,128)(2,1)S(1)} %added.19), channel_id=1, source_target_pairs={{0,8},{1,9},{2,10},{3,11},{4,12},{5,13},{6,14},{7,15},{8,0},{9,1},... | collective-permute-start | bytes 208904 | tf_op jit(solution)/shard_map/ppermute | solution.py:34
  52.0 8.0 %collective-permute-start.17 = (bf16[1,272,128]{2,1,0:T(8,128)(2,1)S(1)}, bf16[1,272,128]{2,1,0:T(8,128)(2,1)S(1)}, u32[]{:S(2)}, u32[]{:S(2)}) collective-permute-start(bf16[1,272,128]{2,1,0:T(8,128)(2,1)S(1)} %get-tuple-element.51), channel_id=1, source_target_pairs={{0,4},{1,5},{2,6},{3,7},{4,0},{5,1},{6,2},{7,3},{8,12},{9,13},{10,... | collective-permute-start | bytes 208904 | tf_op jit(solution)/shard_map/ppermute | solution.py:34
  54.0 7.2 %collective-permute-start.11 = (bf16[1,272,128]{2,1,0:T(8,128)(2,1)S(1)}, bf16[1,272,128]{2,1,0:T(8,128)(2,1)S(1)}, u32[]{:S(2)}, u32[]{:S(2)}) collective-permute-start(bf16[1,272,128]{2,1,0:T(8,128)(2,1)S(1)} %added.14), channel_id=1, source_target_pairs={{0,2},{1,3},{2,0},{3,1},{4,6},{5,7},{6,4},{7,5},{8,10},{9,11},{10,... | collective-permute-start | bytes 208904 | tf_op jit(solution)/shard_map/ppermute | solution.py:34
  54.4 6.8 %collective-permute-start.12 = (bf16[1,272,128]{2,1,0:T(8,128)(2,1)S(1)}, bf16[1,272,128]{2,1,0:T(8,128)(2,1)S(1)}, u32[]{:S(2)}, u32[]{:S(2)}) collective-permute-start(bf16[1,272,128]{2,1,0:T(8,128)(2,1)S(1)} %get-tuple-element.44), channel_id=1, source_target_pairs={{0,8},{1,9},{2,10},{3,11},{4,12},{5,13},{6,14},{7,15},{8,0},{9,1},... | collective-permute-start | bytes 208904 | tf_op jit(solution)/shard_map/ppermute | solution.py:34

commit v3 on v1

--- a/solution.py
+++ b/solution.py
@@ -350,12 +350,18 @@
         listed_ref[found] = place
         found = found + (disp == NDISP - 1).astype(jnp.int32)
 
-    @pl.loop(0, lax.div(found + 1, 2))
+    def finish(places):
+        results = [bond(place, lhs_ref.at[index]) for index, place in enumerate(places)]
+        for place, (real, imag) in zip(places, results):
+            store_rounded(out_ref, (place,), real, imag)
+
+    @pl.loop(0, lax.div(found, 2))
     def _(pair):
-        both = [listed_ref[2 * pair], listed_ref[jnp.minimum(2 * pair + 1, found - 1)]]
-        results = [bond(place, lhs_ref.at[index]) for index, place in enumerate(both)]
-        for place, (real, imag) in zip(both, results):
-            store_rounded(out_ref, (place,), real, imag)
+        finish([listed_ref[2 * pair], listed_ref[2 * pair + 1]])
+
+    @pl.when(lax.rem(found, 2) == 1)
+    def _():
+        finish([listed_ref[found - 1]])
 
 
 def layer_items(core, rows, item, own, ahead, phase, turn, scale):

time: 57.7 us -> 57.4 us (level); the launches traced: 58.6 us -> 57.7 us
  Pallas kernels: 26.2 us -> 25.4 us
    pallas_call x2, Pallas kernels: 5.75 us -> 4.9 us  [layer_items(): pl.pallas_call(functools.partial(layer_kernel, core, scale), in_specs=[pl...]
  transfers between devices with their start and end apart: 18 -> 18, of which waited for: 5 -> 5; matrix products, arithmetic and copies ran while one was open for 2% -> 2% of each run, Pallas kernels for 36% -> 38%
where the time goes in v3:
time: 57.4 us; the launch traced here: 57.7 us
  Pallas kernels  25.4 us (44%)
  starting transfers between devices  22.3 us (39%)
  waiting for transfers between devices  8.63 us (15%)
  other arithmetic  0.9 us (2%)
    ppermute x17, starting transfers between devices, exchanged(): return lax.ppermute(value, SITES, [(i, i ^ mask) for i in range(size)])  19.6 us
    pallas_call x1, Pallas kernels, plane_items(): pl.pallas_call(functools.partial(plane_kernel, total_z, plane, scale), gr...  15.1 us
    ppermute x17, waiting for transfers between devices, exchanged(): return lax.ppermute(value, SITES, [(i, i ^ mask) for i in range(size)])  8.63 us
    pallas_call x2, Pallas kernels, layer_items(): pl.pallas_call(functools.partial(layer_kernel, core, scale), in_specs=[pl...  4.9 us
    pallas_call x1, Pallas kernels, mixed_perambulators(): pl.pallas_call(mix_kernel, in_specs=[scalar] * 3 + [pl.BlockSpec(memory_s...  2.98 us
    ppermute x1, starting transfers between devices, shifted(): lax.ppermute(value, axis, [(i, (i + by) % size) for i in range(size)])  2.75 us
    pallas_call x1, Pallas kernels, diagrams(): pl.pallas_call(functools.partial(diagram_kernel, places), in_specs=[whole...  1.61 us
  transfers between devices with their start and end apart: 18, of which 5 were waited for; matrix products, arithmetic and copies ran while one was open for 2% of the time, Pallas kernels for 38%

profile of v3, /device:TPU:0, one launch (start us, length us, event | category | flops | bytes accessed | tf_op | source)
XLA Modules:
  0.0 57.7 jit_solution(5200227723088881054)
XLA Ops:
  0.0 2.4 %collective-permute-start = (s32[1,2,3]{2,1,0:T(2,128)}, s32[1,2,3]{2,1,0:T(2,128)S(1)}, u32[]{:S(2)}, u32[]{:S(2)}) collective-permute-start(s32[1,2,3]{2,1,0:T(2,128)} %bitcast.7), channel_id=1, source_target_pairs={{0,3},{1,2},{2,1},{3,0},{4,7},{5,6},{6,5},{7,4},{8,11},{9,10},{10,... | collective-permute-start | bytes 80 | tf_op jit(solution)/shard_map/ppermute | solution.py:34
  2.4 0.6 %collective-permute-start.1 = (s32[1,2,3]{2,1,0:T(2,128)}, s32[1,2,3]{2,1,0:T(2,128)S(1)}, u32[]{:S(2)}, u32[]{:S(2)}) collective-permute-start(s32[1,2,3]{2,1,0:T(2,128)} %bitcast.8), channel_id=1, source_target_pairs={{0,2},{1,3},{2,0},{3,1},{4,6},{5,7},{6,4},{7,5},{8,10},{9,11},{10,... | collective-permute-start | bytes 80 | tf_op jit(solution)/shard_map/ppermute | solution.py:34
  3.1 0.8 %collective-permute-done = s32[1,2,3]{2,1,0:T(2,128)S(1)} collective-permute-done((s32[1,2,3]{2,1,0:T(2,128)}, s32[1,2,3]{2,1,0:T(2,128)S(1)}, u32[]{:S(2)}, u32[]{:S(2)}) %collective-permute-start) | collective-permute-done | bytes 56 | tf_op jit(solution)/shard_map/ppermute | solution.py:34
  3.9 2.3 %collective-permute-done.1 = s32[1,2,3]{2,1,0:T(2,128)S(1)} collective-permute-done((s32[1,2,3]{2,1,0:T(2,128)}, s32[1,2,3]{2,1,0:T(2,128)S(1)}, u32[]{:S(2)}, u32[]{:S(2)}) %collective-permute-start.1) | collective-permute-done | bytes 56 | tf_op jit(solution)/shard_map/ppermute | solution.py:34
  6.2 2.7 %collective-permute-start.6 = (bf16[4,2,3,128,1,256]{5,3,2,1,0,4:T(8,128)(2,1)}, bf16[4,2,3,128,1,256]{5,3,2,1,0,4:T(8,128)(2,1)S(1)}, u32[]{:S(2)}, u32[]{:S(2)}) collective-permute-start(bf16[4,2,3,128,1,256]{5,3,2,1,0,4:T(8,128)(2,1)} %bitcast.11), channel_id=1, source_target_pairs={{0,15},{1,0},{2,1},{3,2},{4,3},{5,4},{6,5},{7,6},{8,7},{9,8},{10,9... | collective-permute-start | bytes 4718600 | tf_op jit(solution)/shard_map/ppermute | solution.py:25
  8.9 0.7 %pad_add_fusion = s32[4,2,3]{2,1,0:T(2,128)S(1)} fusion(s32[1,2,3]{2,1,0:T(2,128)S(1)} %collective-permute-done, s32[1,2,3]{2,1,0:T(2,128)S(1)} %collective-permute-done.1, s32[1,2,3]{2,1,0:T(2,128)S(1)} %collective-permute-done.2, s32[1,2,3]{2,1,0:T(2,128)} %bitcast.10), kind=kLoop, calls=%fused_computation.4 | loop fusion | flops 72 | bytes 192 | tf_op jit(solution)/shard_map/concatenate | solution.py:46
  9.6 1.4 %collective-permute-start.4 = (s32[4,2,3]{2,1,0:T(2,128)S(1)}, s32[4,2,3]{2,1,0:T(2,128)S(1)}, u32[]{:S(2)}, u32[]{:S(2)}) collective-permute-start(s32[4,2,3]{2,1,0:T(2,128)S(1)} %pad_add_fusion), channel_id=1, source_target_pairs={{0,8},{1,9},{2,10},{3,11},{4,12},{5,13},{6,14},{7,15},{8,0},{9,1},... | collective-permute-start | bytes 296 | tf_op jit(solution)/shard_map/ppermute | solution.py:34
  11.0 3.0 %collective-permute-start.5 = (s32[4,2,3]{2,1,0:T(2,128)S(1)}, s32[4,2,3]{2,1,0:T(2,128)S(1)}, u32[]{:S(2)}, u32[]{:S(2)}) collective-permute-start(s32[4,2,3]{2,1,0:T(2,128)S(1)} %pad_add_fusion), channel_id=1, source_target_pairs={{0,12},{1,13},{2,14},{3,15},{4,8},{5,9},{6,10},{7,11},{8,4},{9,5},... | collective-permute-start | bytes 296 | tf_op jit(solution)/shard_map/ppermute | solution.py:34
  14.0 15.1 %plane_items.1 = (bf16[4,4,3,272,128]{4,3,2,1,0:T(8,128)(2,1)S(1)}, f32[4,2,3,128,256]{4,3,2,1,0:T(8,128)S(1)}, f32[4,2,1,256]{3,2,1,0:T(1,128)S(1)}, f32[4,2,1,128]{3,2,1,0:T(1,128)S(1)}) custom-call(s32[1]{0:T(128)} %bitcast.1.position_ref, s32[4,3]{1,0:T(4,128)} %momenta_in.1, bf16[4,2,3,128,256]{4,3,2,1,0:T(8,128)(2,1)} %bitcast.12, ...), custom_call_target="tpu_custom_call" | custom-call | flops 3221225472 | bytes 4939776 | tf_op jit(solution)/shard_map/plane_items/pallas_call | solution.py:260
  29.2 1.8 %layer_items.3 = bf16[16,272,128]{2,1,0:T(8,128)(2,1)S(1)} custom-call(s32[16,2,3]{2,1,0:T(2,128)S(1)} %constant_dynamic-update-slice_fusion.rows_ref, bf16[4,4,3,272,128]{4,3,2,1,0:T(8,128)(2,1)S(1)} %get-tuple-element.32.item_ref, f32[4,2,3,128,256]{4,3,2,1,0:T(8,128)S(1)} %get-tuple-element.33.own_ref, bf16[4,2,3,128,256]{4,3,2,1,0:T(8,128)(2,1)S(1)} %bitcast.5, ...), custom_call_target="tpu_custom_call" | custom-call | flops 805306368 | bytes 1572864 | tf_op jit(solution)/shard_map/layer_items/pallas_call | solution.py:372
  31.1 3.1 %layer_items.2.refs_0_ = bf16[16,272,128]{2,1,0:T(8,128)(2,1)S(1)} custom-call(s32[16,2,3]{2,1,0:T(2,128)S(1)} %constant_dynamic-update-slice_fusion.rows_ref, bf16[4,4,3,272,128]{4,3,2,1,0:T(8,128)(2,1)S(1)} %get-tuple-element.32.item_ref, f32[4,2,3,128,256]{4,3,2,1,0:T(8,128)S(1)} %get-tuple-element.33.own_ref, bf16[4,2,3,128,256]{4,3,2,1,0:T(8,128)(2,1)S(1)} %bitcast.6, ...), custom_call_target="tpu_custom_call" | custom-call | flops 805306368 | bytes 1572864 | tf_op jit(solution)/shard_map/layer_items/pallas_call | solution.py:372
  34.5 1.6 %collective-permute-start.14 = (bf16[2,272,128]{2,1,0:T(8,128)(2,1)S(1)}, bf16[2,272,128]{2,1,0:T(8,128)(2,1)S(1)}, u32[]{:S(2)}, u32[]{:S(2)}) collective-permute-start(bf16[2,272,128]{2,1,0:T(8,128)(2,1)S(1)} %get-tuple-element.46), channel_id=1, source_target_pairs={{0,4},{1,5},{2,6},{3,7},{4,0},{5,1},{6,2},{7,3},{8,12},{9,13},{10,... | collective-permute-start | bytes 417800 | tf_op jit(solution)/shard_map/ppermute | solution.py:34
  36.2 1.1 %collective-permute-start.8 = (bf16[2,272,128]{2,1,0:T(8,128)(2,1)S(1)}, bf16[2,272,128]{2,1,0:T(8,128)(2,1)S(1)}, u32[]{:S(2)}, u32[]{:S(2)}) collective-permute-start(bf16[2,272,128]{2,1,0:T(8,128)(2,1)S(1)} %get-tuple-element.38), channel_id=1, source_target_pairs={{0,2},{1,3},{2,0},{3,1},{4,6},{5,7},{6,4},{7,5},{8,10},{9,11},{10,... | collective-permute-start | bytes 417800 | tf_op jit(solution)/shard_map/ppermute | solution.py:34
  37.5 1.5 %collective-permute-start.13 = (bf16[2,272,128]{2,1,0:T(8,128)(2,1)S(1)}, bf16[2,272,128]{2,1,0:T(8,128)(2,1)S(1)}, u32[]{:S(2)}, u32[]{:S(2)}) collective-permute-start(bf16[2,272,128]{2,1,0:T(8,128)(2,1)S(1)} %get-tuple-element.44), channel_id=1, source_target_pairs={{0,4},{1,5},{2,6},{3,7},{4,0},{5,1},{6,2},{7,3},{8,12},{9,13},{10,... | collective-permute-start | bytes 417800 | tf_op jit(solution)/shard_map/ppermute | solution.py:34
  39.0 2.0 %collective-permute-done.9.refs_1_ = bf16[2,272,128]{2,1,0:T(8,128)(2,1)S(1)} collective-permute-done((bf16[2,272,128]{2,1,0:T(8,128)(2,1)S(1)}, bf16[2,272,128]{2,1,0:T(8,128)(2,1)S(1)}, u32[]{:S(2)}, u32[]{:S(2)}) %collective-permute-start.9) | collective-permute-done | bytes 139296 | tf_op jit(solution)/shard_map/ppermute | solution.py:34
  41.5 2.5 %collective-permute-start.15 = (bf16[1,272,128]{2,1,0:T(8,128)(2,1)S(1)}, bf16[1,272,128]{2,1,0:T(8,128)(2,1)S(1)}, u32[]{:S(2)}, u32[]{:S(2)}) collective-permute-start(bf16[1,272,128]{2,1,0:T(8,128)(2,1)S(1)} %added.17), channel_id=1, source_target_pairs={{0,2},{1,3},{2,0},{3,1},{4,6},{5,7},{6,4},{7,5},{8,10},{9,11},{10,... | collective-permute-start | bytes 208904 | tf_op jit(solution)/shard_map/ppermute | solution.py:34
  44.3 0.7 %collective-permute-start.11 = (bf16[1,272,128]{2,1,0:T(8,128)(2,1)S(1)}, bf16[1,272,128]{2,1,0:T(8,128)(2,1)S(1)}, u32[]{:S(2)}, u32[]{:S(2)}) collective-permute-start(bf16[1,272,128]{2,1,0:T(8,128)(2,1)S(1)} %added.14), channel_id=1, source_target_pairs={{0,8},{1,9},{2,10},{3,11},{4,12},{5,13},{6,14},{7,15},{8,0},{9,1},... | collective-permute-start | bytes 208904 | tf_op jit(solution)/shard_map/ppermute | solution.py:34
  45.0 2.1 %collective-permute-start.16 = (bf16[1,272,128]{2,1,0:T(8,128)(2,1)S(1)}, bf16[1,272,128]{2,1,0:T(8,128)(2,1)S(1)}, u32[]{:S(2)}, u32[]{:S(2)}) collective-permute-start(bf16[1,272,128]{2,1,0:T(8,128)(2,1)S(1)} %added.19), channel_id=1, source_target_pairs={{0,2},{1,3},{2,0},{3,1},{4,6},{5,7},{6,4},{7,5},{8,10},{9,11},{10,... | collective-permute-start | bytes 208904 | tf_op jit(solution)/shard_map/ppermute | solution.py:34
  47.1 1.4 %collective-permute-done.10.refs_2_ = bf16[1,272,128]{2,1,0:T(8,128)(2,1)S(1)} collective-permute-done((bf16[1,272,128]{2,1,0:T(8,128)(2,1)S(1)}, bf16[1,272,128]{2,1,0:T(8,128)(2,1)S(1)}, u32[]{:S(2)}, u32[]{:S(2)}) %collective-permute-start.10) | collective-permute-done | bytes 69664 | tf_op jit(solution)/shard_map/ppermute | solution.py:34
  48.5 1.5 %collective-permute-start.12 = (bf16[1,272,128]{2,1,0:T(8,128)(2,1)S(1)}, bf16[1,272,128]{2,1,0:T(8,128)(2,1)S(1)}, u32[]{:S(2)}, u32[]{:S(2)}) collective-permute-start(bf16[1,272,128]{2,1,0:T(8,128)(2,1)S(1)} %get-tuple-element.42), channel_id=1, source_target_pairs={{0,4},{1,5},{2,6},{3,7},{4,0},{5,1},{6,2},{7,3},{8,12},{9,13},{10,... | collective-permute-start | bytes 208904 | tf_op jit(solution)/shard_map/ppermute | solution.py:34
  50.0 0.6 %collective-permute-start.17 = (bf16[1,272,128]{2,1,0:T(8,128)(2,1)S(1)}, bf16[1,272,128]{2,1,0:T(8,128)(2,1)S(1)}, u32[]{:S(2)}, u32[]{:S(2)}) collective-permute-start(bf16[1,272,128]{2,1,0:T(8,128)(2,1)S(1)} %get-tuple-element.48), channel_id=1, source_target_pairs={{0,8},{1,9},{2,10},{3,11},{4,12},{5,13},{6,14},{7,15},{8,0},{9,1},... | collective-permute-start | bytes 208904 | tf_op jit(solution)/shard_map/ppermute | solution.py:34
  50.9 3.0 %mixed_perambulators.1.refs_6_ = bf16[2,4,2,128,512]{4,3,2,1,0:T(8,128)(2,1)S(1)} custom-call(s32[2]{0:T(128)S(1)} %get-tuple-element.50.slot_ref, s32[2]{0:T(128)S(1)} %get-tuple-element.49.structure_ref, f32[256]{0:T(256)S(1)} %reshape.17.weight_ref, bf16[2,4,2,128,512]{4,3,2,1,0:T(8,128)(2,1)} %tau_in.1), custom_call_target="tpu_custom_call" | custom-call | flops 8388608 | bytes 4194304 | tf_op jit(solution)/shard_map/mixed_perambulators/pallas_call | solution.py:492
  53.9 2.2 %collective-permute-done.17.refs_5_ = bf16[1,272,128]{2,1,0:T(8,128)(2,1)S(1)} collective-permute-done((bf16[1,272,128]{2,1,0:T(8,128)(2,1)S(1)}, bf16[1,272,128]{2,1,0:T(8,128)(2,1)S(1)}, u32[]{:S(2)}, u32[]{:S(2)}) %collective-permute-start.17) | collective-permute-done | bytes 69664 | tf_op jit(solution)/shard_map/ppermute | solution.py:34
  56.1 1.6 %diagrams.1 = bf16[2,4,2,128,512]{4,3,2,1,0:T(8,128)(2,1)} custom-call(f32[1,272,128]{2,1,0:T(8,128)S(1)} %get-tuple-element.41.refs_0_, bf16[1,272,128]{2,1,0:T(8,128)(2,1)S(1)} %collective-permute-done.11.refs_1_, bf16[1,272,128]{2,1,0:T(8,128)(2,1)S(1)} %collective-permute-done.12.refs_2_, f32[1,272,128]{2,1,0:T(8,128)S(1)} %get-tuple-element.47.refs_3_, ...), custom_call_target="tpu_custom_call" | custom-call | flops 536870912 | bytes 4194304 | tf_op jit(solution)/shard_map/diagrams/pallas_call | solution.py:539
  (39 shorter events, 1.9 us)
Async XLA Ops:
  0.0 3.9 %collective-permute-start = (s32[1,2,3]{2,1,0:T(2,128)}, s32[1,2,3]{2,1,0:T(2,128)S(1)}, u32[]{:S(2)}, u32[]{:S(2)}) collective-permute-start(s32[1,2,3]{2,1,0:T(2,128)} %bitcast.7), channel_id=1, source_target_pairs={{0,3},{1,2},{2,1},{3,0},{4,7},{5,6},{6,5},{7,4},{8,11},{9,10},{10,... | collective-permute-start | bytes 80 | tf_op jit(solution)/shard_map/ppermute | solution.py:34
  2.4 3.8 %collective-permute-start.1 = (s32[1,2,3]{2,1,0:T(2,128)}, s32[1,2,3]{2,1,0:T(2,128)S(1)}, u32[]{:S(2)}, u32[]{:S(2)}) collective-permute-start(s32[1,2,3]{2,1,0:T(2,128)} %bitcast.8), channel_id=1, source_target_pairs={{0,2},{1,3},{2,0},{3,1},{4,6},{5,7},{6,4},{7,5},{8,10},{9,11},{10,... | collective-permute-start | bytes 80 | tf_op jit(solution)/shard_map/ppermute | solution.py:34
  3.0 3.2 %collective-permute-start.2 = (s32[1,2,3]{2,1,0:T(2,128)}, s32[1,2,3]{2,1,0:T(2,128)S(1)}, u32[]{:S(2)}, u32[]{:S(2)}) collective-permute-start(s32[1,2,3]{2,1,0:T(2,128)} %bitcast.9), channel_id=1, source_target_pairs={{0,1},{1,0},{2,3},{3,2},{4,5},{5,4},{6,7},{7,6},{8,9},{9,8},{10,11... | collective-permute-start | bytes 80 | tf_op jit(solution)/shard_map/ppermute | solution.py:34
  6.2 23.0 %collective-permute-start.6 = (bf16[4,2,3,128,1,256]{5,3,2,1,0,4:T(8,128)(2,1)}, bf16[4,2,3,128,1,256]{5,3,2,1,0,4:T(8,128)(2,1)S(1)}, u32[]{:S(2)}, u32[]{:S(2)}) collective-permute-start(bf16[4,2,3,128,1,256]{5,3,2,1,0,4:T(8,128)(2,1)} %bitcast.11), channel_id=1, source_target_pairs={{0,15},{1,0},{2,1},{3,2},{4,3},{5,4},{6,5},{7,6},{8,7},{9,8},{10,9... | collective-permute-start | bytes 4718600 | tf_op jit(solution)/shard_map/ppermute | solution.py:25
  9.6 19.5 %collective-permute-start.3 = (s32[4,2,3]{2,1,0:T(2,128)S(1)}, s32[4,2,3]{2,1,0:T(2,128)S(1)}, u32[]{:S(2)}, u32[]{:S(2)}) collective-permute-start(s32[4,2,3]{2,1,0:T(2,128)S(1)} %pad_add_fusion), channel_id=1, source_target_pairs={{0,4},{1,5},{2,6},{3,7},{4,0},{5,1},{6,2},{7,3},{8,12},{9,13},{10,... | collective-permute-start | bytes 296 | tf_op jit(solution)/shard_map/ppermute | solution.py:34
  9.6 19.6 %collective-permute-start.4 = (s32[4,2,3]{2,1,0:T(2,128)S(1)}, s32[4,2,3]{2,1,0:T(2,128)S(1)}, u32[]{:S(2)}, u32[]{:S(2)}) collective-permute-start(s32[4,2,3]{2,1,0:T(2,128)S(1)} %pad_add_fusion), channel_id=1, source_target_pairs={{0,8},{1,9},{2,10},{3,11},{4,12},{5,13},{6,14},{7,15},{8,0},{9,1},... | collective-permute-start | bytes 296 | tf_op jit(solution)/shard_map/ppermute | solution.py:34
  11.0 18.2 %collective-permute-start.5 = (s32[4,2,3]{2,1,0:T(2,128)S(1)}, s32[4,2,3]{2,1,0:T(2,128)S(1)}, u32[]{:S(2)}, u32[]{:S(2)}) collective-permute-start(s32[4,2,3]{2,1,0:T(2,128)S(1)} %pad_add_fusion), channel_id=1, source_target_pairs={{0,12},{1,13},{2,14},{3,15},{4,8},{5,9},{6,10},{7,11},{8,4},{9,5},... | collective-permute-start | bytes 296 | tf_op jit(solution)/shard_map/ppermute | solution.py:34
  31.0 3.2 %collective-permute-start.7 = (bf16[16,272,128]{2,1,0:T(8,128)(2,1)S(1)}, bf16[16,272,128]{2,1,0:T(8,128)(2,1)S(1)}, u32[]{:S(2)}, u32[]{:S(2)}) collective-permute-start(bf16[16,272,128]{2,1,0:T(8,128)(2,1)S(1)} %layer_items.3), channel_id=1, source_target_pairs={{0,1},{1,0},{2,3},{3,2},{4,5},{5,4},{6,7},{7,6},{8,9},{9,8},{10,11... | collective-permute-start | bytes 3342344 | tf_op jit(solution)/shard_map/ppermute | solution.py:34
  34.4 6.6 %collective-permute-start.9 = (bf16[2,272,128]{2,1,0:T(8,128)(2,1)S(1)}, bf16[2,272,128]{2,1,0:T(8,128)(2,1)S(1)}, u32[]{:S(2)}, u32[]{:S(2)}) collective-permute-start(bf16[2,272,128]{2,1,0:T(8,128)(2,1)S(1)} %get-tuple-element.40), channel_id=1, source_target_pairs={{0,2},{1,3},{2,0},{3,1},{4,6},{5,7},{6,4},{7,5},{8,10},{9,11},{10,... | collective-permute-start | bytes 417800 | tf_op jit(solution)/shard_map/ppermute | solution.py:34
  34.5 6.9 %collective-permute-start.14 = (bf16[2,272,128]{2,1,0:T(8,128)(2,1)S(1)}, bf16[2,272,128]{2,1,0:T(8,128)(2,1)S(1)}, u32[]{:S(2)}, u32[]{:S(2)}) collective-permute-start(bf16[2,272,128]{2,1,0:T(8,128)(2,1)S(1)} %get-tuple-element.46), channel_id=1, source_target_pairs={{0,4},{1,5},{2,6},{3,7},{4,0},{5,1},{6,2},{7,3},{8,12},{9,13},{10,... | collective-permute-start | bytes 417800 | tf_op jit(solution)/shard_map/ppermute | solution.py:34
  36.2 7.8 %copy-start.1 = (f32[16,4,4]{0,2,1:T(4,128)S(1)}, f32[16,4,4]{0,2,1:T(4,128)}, u32[]{:S(2)}) copy-start(f32[16,4,4]{0,2,1:T(4,128)} %param.9) | copy-start | bytes 3076
  36.2 14.4 %copy-start = (s32[2,3]{1,0:T(2,128)S(1)}, s32[2,3]{1,0:T(2,128)}, u32[]{:S(2)}) copy-start(s32[2,3]{1,0:T(2,128)} %param.11) | copy-start | bytes 76
  36.2 8.7 %collective-permute-start.8 = (bf16[2,272,128]{2,1,0:T(8,128)(2,1)S(1)}, bf16[2,272,128]{2,1,0:T(8,128)(2,1)S(1)}, u32[]{:S(2)}, u32[]{:S(2)}) collective-permute-start(bf16[2,272,128]{2,1,0:T(8,128)(2,1)S(1)} %get-tuple-element.38), channel_id=1, source_target_pairs={{0,2},{1,3},{2,0},{3,1},{4,6},{5,7},{6,4},{7,5},{8,10},{9,11},{10,... | collective-permute-start | bytes 417800 | tf_op jit(solution)/shard_map/ppermute | solution.py:34
  37.5 12.5 %collective-permute-start.13 = (bf16[2,272,128]{2,1,0:T(8,128)(2,1)S(1)}, bf16[2,272,128]{2,1,0:T(8,128)(2,1)S(1)}, u32[]{:S(2)}, u32[]{:S(2)}) collective-permute-start(bf16[2,272,128]{2,1,0:T(8,128)(2,1)S(1)} %get-tuple-element.44), channel_id=1, source_target_pairs={{0,4},{1,5},{2,6},{3,7},{4,0},{5,1},{6,2},{7,3},{8,12},{9,13},{10,... | collective-permute-start | bytes 417800 | tf_op jit(solution)/shard_map/ppermute | solution.py:34
  41.0 7.4 %collective-permute-start.10 = (bf16[1,272,128]{2,1,0:T(8,128)(2,1)S(1)}, bf16[1,272,128]{2,1,0:T(8,128)(2,1)S(1)}, u32[]{:S(2)}, u32[]{:S(2)}) collective-permute-start(bf16[1,272,128]{2,1,0:T(8,128)(2,1)S(1)} %added.12), channel_id=1, source_target_pairs={{0,8},{1,9},{2,10},{3,11},{4,12},{5,13},{6,14},{7,15},{8,0},{9,1},... | collective-permute-start | bytes 208904 | tf_op jit(solution)/shard_map/ppermute | solution.py:34
  41.5 8.5 %collective-permute-start.15 = (bf16[1,272,128]{2,1,0:T(8,128)(2,1)S(1)}, bf16[1,272,128]{2,1,0:T(8,128)(2,1)S(1)}, u32[]{:S(2)}, u32[]{:S(2)}) collective-permute-start(bf16[1,272,128]{2,1,0:T(8,128)(2,1)S(1)} %added.17), channel_id=1, source_target_pairs={{0,2},{1,3},{2,0},{3,1},{4,6},{5,7},{6,4},{7,5},{8,10},{9,11},{10,... | collective-permute-start | bytes 208904 | tf_op jit(solution)/shard_map/ppermute | solution.py:34
  44.3 9.6 %collective-permute-start.11 = (bf16[1,272,128]{2,1,0:T(8,128)(2,1)S(1)}, bf16[1,272,128]{2,1,0:T(8,128)(2,1)S(1)}, u32[]{:S(2)}, u32[]{:S(2)}) collective-permute-start(bf16[1,272,128]{2,1,0:T(8,128)(2,1)S(1)} %added.14), channel_id=1, source_target_pairs={{0,8},{1,9},{2,10},{3,11},{4,12},{5,13},{6,14},{7,15},{8,0},{9,1},... | collective-permute-start | bytes 208904 | tf_op jit(solution)/shard_map/ppermute | solution.py:34
  45.0 8.9 %collective-permute-start.16 = (bf16[1,272,128]{2,1,0:T(8,128)(2,1)S(1)}, bf16[1,272,128]{2,1,0:T(8,128)(2,1)S(1)}, u32[]{:S(2)}, u32[]{:S(2)}) collective-permute-start(bf16[1,272,128]{2,1,0:T(8,128)(2,1)S(1)} %added.19), channel_id=1, source_target_pairs={{0,2},{1,3},{2,0},{3,1},{4,6},{5,7},{6,4},{7,5},{8,10},{9,11},{10,... | collective-permute-start | bytes 208904 | tf_op jit(solution)/shard_map/ppermute | solution.py:34
  48.5 5.4 %collective-permute-start.12 = (bf16[1,272,128]{2,1,0:T(8,128)(2,1)S(1)}, bf16[1,272,128]{2,1,0:T(8,128)(2,1)S(1)}, u32[]{:S(2)}, u32[]{:S(2)}) collective-permute-start(bf16[1,272,128]{2,1,0:T(8,128)(2,1)S(1)} %get-tuple-element.42), channel_id=1, source_target_pairs={{0,4},{1,5},{2,6},{3,7},{4,0},{5,1},{6,2},{7,3},{8,12},{9,13},{10,... | collective-permute-start | bytes 208904 | tf_op jit(solution)/shard_map/ppermute | solution.py:34
  50.0 6.0 %collective-permute-start.17 = (bf16[1,272,128]{2,1,0:T(8,128)(2,1)S(1)}, bf16[1,272,128]{2,1,0:T(8,128)(2,1)S(1)}, u32[]{:S(2)}, u32[]{:S(2)}) collective-permute-start(bf16[1,272,128]{2,1,0:T(8,128)(2,1)S(1)} %get-tuple-element.48), channel_id=1, source_target_pairs={{0,8},{1,9},{2,10},{3,11},{4,12},{5,13},{6,14},{7,15},{8,0},{9,1},... | collective-permute-start | bytes 208904 | tf_op jit(solution)/shard_map/ppermute | solution.py:34

commit v4 on v3

--- a/solution.py
+++ b/solution.py
@@ -474,10 +474,8 @@
         weight = [[weight_ref[base + r * spins + s] for s in range(spins)] for r in range(spins)]
         for part in range(parts):
             copy(index, part).wait()
-
-            @pl.loop(0, nvec // ROWS)
-            def _(step):
-                rows = pl.ds(pl.multiple_of(step * ROWS, ROWS), ROWS)
+            for start in range(0, nvec, ROWS):
+                rows = pl.ds(start, ROWS)
                 tau = [tau_ref[index, s, part, rows, :].astype(jnp.float32) for s in range(spins)]
                 for r in range(spins):
                     mixed = weight[r][0] * tau[0]

time: 57.4 us -> 56.6 us (0.986); the launches traced: 57.7 us -> 57.5 us
  no operation moved by 1% of the time
where the time goes in v4:
time: 56.6 us; the launch traced here: 57.5 us
  Pallas kernels  25.7 us (45%)
  starting transfers between devices  22.2 us (39%)
  waiting for transfers between devices  8.25 us (15%)
  other arithmetic  0.9 us (2%)
    ppermute x17, starting transfers between devices, exchanged(): return lax.ppermute(value, SITES, [(i, i ^ mask) for i in range(size)])  19.4 us
    pallas_call x1, Pallas kernels, plane_items(): pl.pallas_call(functools.partial(plane_kernel, total_z, plane, scale), gr...  15.1 us
    ppermute x17, waiting for transfers between devices, exchanged(): return lax.ppermute(value, SITES, [(i, i ^ mask) for i in range(size)])  8.25 us
    pallas_call x2, Pallas kernels, layer_items(): pl.pallas_call(functools.partial(layer_kernel, core, scale), in_specs=[pl...  5.43 us
    pallas_call x1, Pallas kernels, mixed_perambulators(): pl.pallas_call(mix_kernel, in_specs=[scalar] * 3 + [pl.BlockSpec(memory_s...  2.81 us
    ppermute x1, starting transfers between devices, shifted(): lax.ppermute(value, axis, [(i, (i + by) % size) for i in range(size)])  2.75 us
    pallas_call x1, Pallas kernels, diagrams(): pl.pallas_call(functools.partial(diagram_kernel, places), in_specs=[whole...  1.61 us
  transfers between devices with their start and end apart: 18, of which 5 were waited for; matrix products, arithmetic and copies ran while one was open for 2% of the time, Pallas kernels for 38%

profile of v4, /device:TPU:0, one launch (start us, length us, event | category | flops | bytes accessed | tf_op | source)
XLA Modules:
  0.0 57.5 jit_solution(11500528113066023171)
XLA Ops:
  0.0 2.4 %collective-permute-start = (s32[1,2,3]{2,1,0:T(2,128)}, s32[1,2,3]{2,1,0:T(2,128)S(1)}, u32[]{:S(2)}, u32[]{:S(2)}) collective-permute-start(s32[1,2,3]{2,1,0:T(2,128)} %bitcast.7), channel_id=1, source_target_pairs={{0,3},{1,2},{2,1},{3,0},{4,7},{5,6},{6,5},{7,4},{8,11},{9,10},{10,... | collective-permute-start | bytes 80 | tf_op jit(solution)/shard_map/ppermute | solution.py:34
  2.4 0.6 %collective-permute-start.1 = (s32[1,2,3]{2,1,0:T(2,128)}, s32[1,2,3]{2,1,0:T(2,128)S(1)}, u32[]{:S(2)}, u32[]{:S(2)}) collective-permute-start(s32[1,2,3]{2,1,0:T(2,128)} %bitcast.8), channel_id=1, source_target_pairs={{0,2},{1,3},{2,0},{3,1},{4,6},{5,7},{6,4},{7,5},{8,10},{9,11},{10,... | collective-permute-start | bytes 80 | tf_op jit(solution)/shard_map/ppermute | solution.py:34
  3.1 0.8 %collective-permute-done = s32[1,2,3]{2,1,0:T(2,128)S(1)} collective-permute-done((s32[1,2,3]{2,1,0:T(2,128)}, s32[1,2,3]{2,1,0:T(2,128)S(1)}, u32[]{:S(2)}, u32[]{:S(2)}) %collective-permute-start) | collective-permute-done | bytes 56 | tf_op jit(solution)/shard_map/ppermute | solution.py:34
  3.9 2.3 %collective-permute-done.1 = s32[1,2,3]{2,1,0:T(2,128)S(1)} collective-permute-done((s32[1,2,3]{2,1,0:T(2,128)}, s32[1,2,3]{2,1,0:T(2,128)S(1)}, u32[]{:S(2)}, u32[]{:S(2)}) %collective-permute-start.1) | collective-permute-done | bytes 56 | tf_op jit(solution)/shard_map/ppermute | solution.py:34
  6.2 2.7 %collective-permute-start.6 = (bf16[4,2,3,128,1,256]{5,3,2,1,0,4:T(8,128)(2,1)}, bf16[4,2,3,128,1,256]{5,3,2,1,0,4:T(8,128)(2,1)S(1)}, u32[]{:S(2)}, u32[]{:S(2)}) collective-permute-start(bf16[4,2,3,128,1,256]{5,3,2,1,0,4:T(8,128)(2,1)} %bitcast.11), channel_id=1, source_target_pairs={{0,15},{1,0},{2,1},{3,2},{4,3},{5,4},{6,5},{7,6},{8,7},{9,8},{10,9... | collective-permute-start | bytes 4718600 | tf_op jit(solution)/shard_map/ppermute | solution.py:25
  8.9 0.7 %pad_add_fusion = s32[4,2,3]{2,1,0:T(2,128)S(1)} fusion(s32[1,2,3]{2,1,0:T(2,128)S(1)} %collective-permute-done, s32[1,2,3]{2,1,0:T(2,128)S(1)} %collective-permute-done.1, s32[1,2,3]{2,1,0:T(2,128)S(1)} %collective-permute-done.2, s32[1,2,3]{2,1,0:T(2,128)} %bitcast.10), kind=kLoop, calls=%fused_computation.4 | loop fusion | flops 72 | bytes 192 | tf_op jit(solution)/shard_map/concatenate | solution.py:46
  9.6 1.4 %collective-permute-start.4 = (s32[4,2,3]{2,1,0:T(2,128)S(1)}, s32[4,2,3]{2,1,0:T(2,128)S(1)}, u32[]{:S(2)}, u32[]{:S(2)}) collective-permute-start(s32[4,2,3]{2,1,0:T(2,128)S(1)} %pad_add_fusion), channel_id=1, source_target_pairs={{0,8},{1,9},{2,10},{3,11},{4,12},{5,13},{6,14},{7,15},{8,0},{9,1},... | collective-permute-start | bytes 296 | tf_op jit(solution)/shard_map/ppermute | solution.py:34
  11.0 3.0 %collective-permute-start.5 = (s32[4,2,3]{2,1,0:T(2,128)S(1)}, s32[4,2,3]{2,1,0:T(2,128)S(1)}, u32[]{:S(2)}, u32[]{:S(2)}) collective-permute-start(s32[4,2,3]{2,1,0:T(2,128)S(1)} %pad_add_fusion), channel_id=1, source_target_pairs={{0,12},{1,13},{2,14},{3,15},{4,8},{5,9},{6,10},{7,11},{8,4},{9,5},... | collective-permute-start | bytes 296 | tf_op jit(solution)/shard_map/ppermute | solution.py:34
  14.0 15.1 %plane_items.1 = (bf16[4,4,3,272,128]{4,3,2,1,0:T(8,128)(2,1)S(1)}, f32[4,2,3,128,256]{4,3,2,1,0:T(8,128)S(1)}, f32[4,2,1,256]{3,2,1,0:T(1,128)S(1)}, f32[4,2,1,128]{3,2,1,0:T(1,128)S(1)}) custom-call(s32[1]{0:T(128)} %bitcast.1.position_ref, s32[4,3]{1,0:T(4,128)} %momenta_in.1, bf16[4,2,3,128,256]{4,3,2,1,0:T(8,128)(2,1)} %bitcast.12, ...), custom_call_target="tpu_custom_call" | custom-call | flops 3221225472 | bytes 4939776 | tf_op jit(solution)/shard_map/plane_items/pallas_call | solution.py:260
  29.2 2.3 %layer_items.3 = bf16[16,272,128]{2,1,0:T(8,128)(2,1)S(1)} custom-call(s32[16,2,3]{2,1,0:T(2,128)S(1)} %constant_dynamic-update-slice_fusion.rows_ref, bf16[4,4,3,272,128]{4,3,2,1,0:T(8,128)(2,1)S(1)} %get-tuple-element.32.item_ref, f32[4,2,3,128,256]{4,3,2,1,0:T(8,128)S(1)} %get-tuple-element.33.own_ref, bf16[4,2,3,128,256]{4,3,2,1,0:T(8,128)(2,1)S(1)} %bitcast.5, ...), custom_call_target="tpu_custom_call" | custom-call | flops 805306368 | bytes 1572864 | tf_op jit(solution)/shard_map/layer_items/pallas_call | solution.py:372
  31.6 3.1 %layer_items.2.refs_0_ = bf16[16,272,128]{2,1,0:T(8,128)(2,1)S(1)} custom-call(s32[16,2,3]{2,1,0:T(2,128)S(1)} %constant_dynamic-update-slice_fusion.rows_ref, bf16[4,4,3,272,128]{4,3,2,1,0:T(8,128)(2,1)S(1)} %get-tuple-element.32.item_ref, f32[4,2,3,128,256]{4,3,2,1,0:T(8,128)S(1)} %get-tuple-element.33.own_ref, bf16[4,2,3,128,256]{4,3,2,1,0:T(8,128)(2,1)S(1)} %bitcast.6, ...), custom_call_target="tpu_custom_call" | custom-call | flops 805306368 | bytes 1572864 | tf_op jit(solution)/shard_map/layer_items/pallas_call | solution.py:372
  35.1 1.0 %collective-permute-start.14 = (bf16[2,272,128]{2,1,0:T(8,128)(2,1)S(1)}, bf16[2,272,128]{2,1,0:T(8,128)(2,1)S(1)}, u32[]{:S(2)}, u32[]{:S(2)}) collective-permute-start(bf16[2,272,128]{2,1,0:T(8,128)(2,1)S(1)} %get-tuple-element.46), channel_id=1, source_target_pairs={{0,4},{1,5},{2,6},{3,7},{4,0},{5,1},{6,2},{7,3},{8,12},{9,13},{10,... | collective-permute-start | bytes 417800 | tf_op jit(solution)/shard_map/ppermute | solution.py:34
  36.2 1.7 %collective-permute-start.8 = (bf16[2,272,128]{2,1,0:T(8,128)(2,1)S(1)}, bf16[2,272,128]{2,1,0:T(8,128)(2,1)S(1)}, u32[]{:S(2)}, u32[]{:S(2)}) collective-permute-start(bf16[2,272,128]{2,1,0:T(8,128)(2,1)S(1)} %get-tuple-element.38), channel_id=1, source_target_pairs={{0,2},{1,3},{2,0},{3,1},{4,6},{5,7},{6,4},{7,5},{8,10},{9,11},{10,... | collective-permute-start | bytes 417800 | tf_op jit(solution)/shard_map/ppermute | solution.py:34
  38.0 1.6 %collective-permute-start.13 = (bf16[2,272,128]{2,1,0:T(8,128)(2,1)S(1)}, bf16[2,272,128]{2,1,0:T(8,128)(2,1)S(1)}, u32[]{:S(2)}, u32[]{:S(2)}) collective-permute-start(bf16[2,272,128]{2,1,0:T(8,128)(2,1)S(1)} %get-tuple-element.44), channel_id=1, source_target_pairs={{0,4},{1,5},{2,6},{3,7},{4,0},{5,1},{6,2},{7,3},{8,12},{9,13},{10,... | collective-permute-start | bytes 417800 | tf_op jit(solution)/shard_map/ppermute | solution.py:34
  39.6 2.0 %collective-permute-done.9.refs_1_ = bf16[2,272,128]{2,1,0:T(8,128)(2,1)S(1)} collective-permute-done((bf16[2,272,128]{2,1,0:T(8,128)(2,1)S(1)}, bf16[2,272,128]{2,1,0:T(8,128)(2,1)S(1)}, u32[]{:S(2)}, u32[]{:S(2)}) %collective-permute-start.9) | collective-permute-done | bytes 139296 | tf_op jit(solution)/shard_map/ppermute | solution.py:34
  41.6 0.3 collective-permute-start.10
  42.0 2.5 %collective-permute-start.15 = (bf16[1,272,128]{2,1,0:T(8,128)(2,1)S(1)}, bf16[1,272,128]{2,1,0:T(8,128)(2,1)S(1)}, u32[]{:S(2)}, u32[]{:S(2)}) collective-permute-start(bf16[1,272,128]{2,1,0:T(8,128)(2,1)S(1)} %added.17), channel_id=1, source_target_pairs={{0,2},{1,3},{2,0},{3,1},{4,6},{5,7},{6,4},{7,5},{8,10},{9,11},{10,... | collective-permute-start | bytes 208904 | tf_op jit(solution)/shard_map/ppermute | solution.py:34
  45.1 2.1 %collective-permute-start.16 = (bf16[1,272,128]{2,1,0:T(8,128)(2,1)S(1)}, bf16[1,272,128]{2,1,0:T(8,128)(2,1)S(1)}, u32[]{:S(2)}, u32[]{:S(2)}) collective-permute-start(bf16[1,272,128]{2,1,0:T(8,128)(2,1)S(1)} %added.19), channel_id=1, source_target_pairs={{0,2},{1,3},{2,0},{3,1},{4,6},{5,7},{6,4},{7,5},{8,10},{9,11},{10,... | collective-permute-start | bytes 208904 | tf_op jit(solution)/shard_map/ppermute | solution.py:34
  47.2 1.2 %collective-permute-done.10.refs_2_ = bf16[1,272,128]{2,1,0:T(8,128)(2,1)S(1)} collective-permute-done((bf16[1,272,128]{2,1,0:T(8,128)(2,1)S(1)}, bf16[1,272,128]{2,1,0:T(8,128)(2,1)S(1)}, u32[]{:S(2)}, u32[]{:S(2)}) %collective-permute-start.10) | collective-permute-done | bytes 69664 | tf_op jit(solution)/shard_map/ppermute | solution.py:34
  48.5 1.3 %collective-permute-start.12 = (bf16[1,272,128]{2,1,0:T(8,128)(2,1)S(1)}, bf16[1,272,128]{2,1,0:T(8,128)(2,1)S(1)}, u32[]{:S(2)}, u32[]{:S(2)}) collective-permute-start(bf16[1,272,128]{2,1,0:T(8,128)(2,1)S(1)} %get-tuple-element.42), channel_id=1, source_target_pairs={{0,4},{1,5},{2,6},{3,7},{4,0},{5,1},{6,2},{7,3},{8,12},{9,13},{10,... | collective-permute-start | bytes 208904 | tf_op jit(solution)/shard_map/ppermute | solution.py:34
  49.9 1.0 %collective-permute-start.17 = (bf16[1,272,128]{2,1,0:T(8,128)(2,1)S(1)}, bf16[1,272,128]{2,1,0:T(8,128)(2,1)S(1)}, u32[]{:S(2)}, u32[]{:S(2)}) collective-permute-start(bf16[1,272,128]{2,1,0:T(8,128)(2,1)S(1)} %get-tuple-element.48), channel_id=1, source_target_pairs={{0,8},{1,9},{2,10},{3,11},{4,12},{5,13},{6,14},{7,15},{8,0},{9,1},... | collective-permute-start | bytes 208904 | tf_op jit(solution)/shard_map/ppermute | solution.py:34
  51.1 2.8 %mixed_perambulators.1.refs_6_ = bf16[2,4,2,128,512]{4,3,2,1,0:T(8,128)(2,1)S(1)} custom-call(s32[2]{0:T(128)S(1)} %get-tuple-element.50.slot_ref, s32[2]{0:T(128)S(1)} %get-tuple-element.49.structure_ref, f32[256]{0:T(256)S(1)} %reshape.17.weight_ref, bf16[2,4,2,128,512]{4,3,2,1,0:T(8,128)(2,1)} %tau_in.1), custom_call_target="tpu_custom_call" | custom-call | flops 8388608 | bytes 4194304 | tf_op jit(solution)/shard_map/mixed_perambulators/pallas_call | solution.py:490
  54.0 1.9 %collective-permute-done.17.refs_5_ = bf16[1,272,128]{2,1,0:T(8,128)(2,1)S(1)} collective-permute-done((bf16[1,272,128]{2,1,0:T(8,128)(2,1)S(1)}, bf16[1,272,128]{2,1,0:T(8,128)(2,1)S(1)}, u32[]{:S(2)}, u32[]{:S(2)}) %collective-permute-start.17) | collective-permute-done | bytes 69664 | tf_op jit(solution)/shard_map/ppermute | solution.py:34
  55.9 1.6 %diagrams.1 = bf16[2,4,2,128,512]{4,3,2,1,0:T(8,128)(2,1)} custom-call(f32[1,272,128]{2,1,0:T(8,128)S(1)} %get-tuple-element.41.refs_0_, bf16[1,272,128]{2,1,0:T(8,128)(2,1)S(1)} %collective-permute-done.11.refs_1_, bf16[1,272,128]{2,1,0:T(8,128)(2,1)S(1)} %collective-permute-done.12.refs_2_, f32[1,272,128]{2,1,0:T(8,128)S(1)} %get-tuple-element.47.refs_3_, ...), custom_call_target="tpu_custom_call" | custom-call | flops 536870912 | bytes 4194304 | tf_op jit(solution)/shard_map/diagrams/pallas_call | solution.py:537
  (39 shorter events, 1.7 us)
Async XLA Ops:
  0.0 3.9 %collective-permute-start = (s32[1,2,3]{2,1,0:T(2,128)}, s32[1,2,3]{2,1,0:T(2,128)S(1)}, u32[]{:S(2)}, u32[]{:S(2)}) collective-permute-start(s32[1,2,3]{2,1,0:T(2,128)} %bitcast.7), channel_id=1, source_target_pairs={{0,3},{1,2},{2,1},{3,0},{4,7},{5,6},{6,5},{7,4},{8,11},{9,10},{10,... | collective-permute-start | bytes 80 | tf_op jit(solution)/shard_map/ppermute | solution.py:34
  2.4 3.8 %collective-permute-start.1 = (s32[1,2,3]{2,1,0:T(2,128)}, s32[1,2,3]{2,1,0:T(2,128)S(1)}, u32[]{:S(2)}, u32[]{:S(2)}) collective-permute-start(s32[1,2,3]{2,1,0:T(2,128)} %bitcast.8), channel_id=1, source_target_pairs={{0,2},{1,3},{2,0},{3,1},{4,6},{5,7},{6,4},{7,5},{8,10},{9,11},{10,... | collective-permute-start | bytes 80 | tf_op jit(solution)/shard_map/ppermute | solution.py:34
  3.0 3.2 %collective-permute-start.2 = (s32[1,2,3]{2,1,0:T(2,128)}, s32[1,2,3]{2,1,0:T(2,128)S(1)}, u32[]{:S(2)}, u32[]{:S(2)}) collective-permute-start(s32[1,2,3]{2,1,0:T(2,128)} %bitcast.9), channel_id=1, source_target_pairs={{0,1},{1,0},{2,3},{3,2},{4,5},{5,4},{6,7},{7,6},{8,9},{9,8},{10,11... | collective-permute-start | bytes 80 | tf_op jit(solution)/shard_map/ppermute | solution.py:34
  6.2 23.0 %collective-permute-start.6 = (bf16[4,2,3,128,1,256]{5,3,2,1,0,4:T(8,128)(2,1)}, bf16[4,2,3,128,1,256]{5,3,2,1,0,4:T(8,128)(2,1)S(1)}, u32[]{:S(2)}, u32[]{:S(2)}) collective-permute-start(bf16[4,2,3,128,1,256]{5,3,2,1,0,4:T(8,128)(2,1)} %bitcast.11), channel_id=1, source_target_pairs={{0,15},{1,0},{2,1},{3,2},{4,3},{5,4},{6,5},{7,6},{8,7},{9,8},{10,9... | collective-permute-start | bytes 4718600 | tf_op jit(solution)/shard_map/ppermute | solution.py:25
  9.6 19.5 %collective-permute-start.3 = (s32[4,2,3]{2,1,0:T(2,128)S(1)}, s32[4,2,3]{2,1,0:T(2,128)S(1)}, u32[]{:S(2)}, u32[]{:S(2)}) collective-permute-start(s32[4,2,3]{2,1,0:T(2,128)S(1)} %pad_add_fusion), channel_id=1, source_target_pairs={{0,4},{1,5},{2,6},{3,7},{4,0},{5,1},{6,2},{7,3},{8,12},{9,13},{10,... | collective-permute-start | bytes 296 | tf_op jit(solution)/shard_map/ppermute | solution.py:34
  9.6 19.6 %collective-permute-start.4 = (s32[4,2,3]{2,1,0:T(2,128)S(1)}, s32[4,2,3]{2,1,0:T(2,128)S(1)}, u32[]{:S(2)}, u32[]{:S(2)}) collective-permute-start(s32[4,2,3]{2,1,0:T(2,128)S(1)} %pad_add_fusion), channel_id=1, source_target_pairs={{0,8},{1,9},{2,10},{3,11},{4,12},{5,13},{6,14},{7,15},{8,0},{9,1},... | collective-permute-start | bytes 296 | tf_op jit(solution)/shard_map/ppermute | solution.py:34
  11.0 18.2 %collective-permute-start.5 = (s32[4,2,3]{2,1,0:T(2,128)S(1)}, s32[4,2,3]{2,1,0:T(2,128)S(1)}, u32[]{:S(2)}, u32[]{:S(2)}) collective-permute-start(s32[4,2,3]{2,1,0:T(2,128)S(1)} %pad_add_fusion), channel_id=1, source_target_pairs={{0,12},{1,13},{2,14},{3,15},{4,8},{5,9},{6,10},{7,11},{8,4},{9,5},... | collective-permute-start | bytes 296 | tf_op jit(solution)/shard_map/ppermute | solution.py:34
  31.6 3.2 %collective-permute-start.7 = (bf16[16,272,128]{2,1,0:T(8,128)(2,1)S(1)}, bf16[16,272,128]{2,1,0:T(8,128)(2,1)S(1)}, u32[]{:S(2)}, u32[]{:S(2)}) collective-permute-start(bf16[16,272,128]{2,1,0:T(8,128)(2,1)S(1)} %layer_items.3), channel_id=1, source_target_pairs={{0,1},{1,0},{2,3},{3,2},{4,5},{5,4},{6,7},{7,6},{8,9},{9,8},{10,11... | collective-permute-start | bytes 3342344 | tf_op jit(solution)/shard_map/ppermute | solution.py:34
  34.9 6.7 %collective-permute-start.9 = (bf16[2,272,128]{2,1,0:T(8,128)(2,1)S(1)}, bf16[2,272,128]{2,1,0:T(8,128)(2,1)S(1)}, u32[]{:S(2)}, u32[]{:S(2)}) collective-permute-start(bf16[2,272,128]{2,1,0:T(8,128)(2,1)S(1)} %get-tuple-element.40), channel_id=1, source_target_pairs={{0,2},{1,3},{2,0},{3,1},{4,6},{5,7},{6,4},{7,5},{8,10},{9,11},{10,... | collective-permute-start | bytes 417800 | tf_op jit(solution)/shard_map/ppermute | solution.py:34
  35.1 6.9 %collective-permute-start.14 = (bf16[2,272,128]{2,1,0:T(8,128)(2,1)S(1)}, bf16[2,272,128]{2,1,0:T(8,128)(2,1)S(1)}, u32[]{:S(2)}, u32[]{:S(2)}) collective-permute-start(bf16[2,272,128]{2,1,0:T(8,128)(2,1)S(1)} %get-tuple-element.46), channel_id=1, source_target_pairs={{0,4},{1,5},{2,6},{3,7},{4,0},{5,1},{6,2},{7,3},{8,12},{9,13},{10,... | collective-permute-start | bytes 417800 | tf_op jit(solution)/shard_map/ppermute | solution.py:34
  36.2 8.3 %copy-start.1 = (f32[16,4,4]{0,2,1:T(4,128)S(1)}, f32[16,4,4]{0,2,1:T(4,128)}, u32[]{:S(2)}) copy-start(f32[16,4,4]{0,2,1:T(4,128)} %param.9) | copy-start | bytes 3076
  36.2 14.7 %copy-start = (s32[2,3]{1,0:T(2,128)S(1)}, s32[2,3]{1,0:T(2,128)}, u32[]{:S(2)}) copy-start(s32[2,3]{1,0:T(2,128)} %param.11) | copy-start | bytes 76
  36.2 8.9 %collective-permute-start.8 = (bf16[2,272,128]{2,1,0:T(8,128)(2,1)S(1)}, bf16[2,272,128]{2,1,0:T(8,128)(2,1)S(1)}, u32[]{:S(2)}, u32[]{:S(2)}) collective-permute-start(bf16[2,272,128]{2,1,0:T(8,128)(2,1)S(1)} %get-tuple-element.38), channel_id=1, source_target_pairs={{0,2},{1,3},{2,0},{3,1},{4,6},{5,7},{6,4},{7,5},{8,10},{9,11},{10,... | collective-permute-start | bytes 417800 | tf_op jit(solution)/shard_map/ppermute | solution.py:34
  38.0 11.8 %collective-permute-start.13 = (bf16[2,272,128]{2,1,0:T(8,128)(2,1)S(1)}, bf16[2,272,128]{2,1,0:T(8,128)(2,1)S(1)}, u32[]{:S(2)}, u32[]{:S(2)}) collective-permute-start(bf16[2,272,128]{2,1,0:T(8,128)(2,1)S(1)} %get-tuple-element.44), channel_id=1, source_target_pairs={{0,4},{1,5},{2,6},{3,7},{4,0},{5,1},{6,2},{7,3},{8,12},{9,13},{10,... | collective-permute-start | bytes 417800 | tf_op jit(solution)/shard_map/ppermute | solution.py:34
  41.6 6.8 %collective-permute-start.10 = (bf16[1,272,128]{2,1,0:T(8,128)(2,1)S(1)}, bf16[1,272,128]{2,1,0:T(8,128)(2,1)S(1)}, u32[]{:S(2)}, u32[]{:S(2)}) collective-permute-start(bf16[1,272,128]{2,1,0:T(8,128)(2,1)S(1)} %added.12), channel_id=1, source_target_pairs={{0,8},{1,9},{2,10},{3,11},{4,12},{5,13},{6,14},{7,15},{8,0},{9,1},... | collective-permute-start | bytes 208904 | tf_op jit(solution)/shard_map/ppermute | solution.py:34
  42.0 7.8 %collective-permute-start.15 = (bf16[1,272,128]{2,1,0:T(8,128)(2,1)S(1)}, bf16[1,272,128]{2,1,0:T(8,128)(2,1)S(1)}, u32[]{:S(2)}, u32[]{:S(2)}) collective-permute-start(bf16[1,272,128]{2,1,0:T(8,128)(2,1)S(1)} %added.17), channel_id=1, source_target_pairs={{0,2},{1,3},{2,0},{3,1},{4,6},{5,7},{6,4},{7,5},{8,10},{9,11},{10,... | collective-permute-start | bytes 208904 | tf_op jit(solution)/shard_map/ppermute | solution.py:34
  44.8 9.2 %collective-permute-start.11 = (bf16[1,272,128]{2,1,0:T(8,128)(2,1)S(1)}, bf16[1,272,128]{2,1,0:T(8,128)(2,1)S(1)}, u32[]{:S(2)}, u32[]{:S(2)}) collective-permute-start(bf16[1,272,128]{2,1,0:T(8,128)(2,1)S(1)} %added.14), channel_id=1, source_target_pairs={{0,8},{1,9},{2,10},{3,11},{4,12},{5,13},{6,14},{7,15},{8,0},{9,1},... | collective-permute-start | bytes 208904 | tf_op jit(solution)/shard_map/ppermute | solution.py:34
  45.1 8.8 %collective-permute-start.16 = (bf16[1,272,128]{2,1,0:T(8,128)(2,1)S(1)}, bf16[1,272,128]{2,1,0:T(8,128)(2,1)S(1)}, u32[]{:S(2)}, u32[]{:S(2)}) collective-permute-start(bf16[1,272,128]{2,1,0:T(8,128)(2,1)S(1)} %added.19), channel_id=1, source_target_pairs={{0,2},{1,3},{2,0},{3,1},{4,6},{5,7},{6,4},{7,5},{8,10},{9,11},{10,... | collective-permute-start | bytes 208904 | tf_op jit(solution)/shard_map/ppermute | solution.py:34
  48.5 5.5 %collective-permute-start.12 = (bf16[1,272,128]{2,1,0:T(8,128)(2,1)S(1)}, bf16[1,272,128]{2,1,0:T(8,128)(2,1)S(1)}, u32[]{:S(2)}, u32[]{:S(2)}) collective-permute-start(bf16[1,272,128]{2,1,0:T(8,128)(2,1)S(1)} %get-tuple-element.42), channel_id=1, source_target_pairs={{0,4},{1,5},{2,6},{3,7},{4,0},{5,1},{6,2},{7,3},{8,12},{9,13},{10,... | collective-permute-start | bytes 208904 | tf_op jit(solution)/shard_map/ppermute | solution.py:34
  49.9 6.0 %collective-permute-start.17 = (bf16[1,272,128]{2,1,0:T(8,128)(2,1)S(1)}, bf16[1,272,128]{2,1,0:T(8,128)(2,1)S(1)}, u32[]{:S(2)}, u32[]{:S(2)}) collective-permute-start(bf16[1,272,128]{2,1,0:T(8,128)(2,1)S(1)} %get-tuple-element.48), channel_id=1, source_target_pairs={{0,8},{1,9},{2,10},{3,11},{4,12},{5,13},{6,14},{7,15},{8,0},{9,1},... | collective-permute-start | bytes 208904 | tf_op jit(solution)/shard_map/ppermute | solution.py:34

commit v5 on v4

--- a/solution.py
+++ b/solution.py
@@ -461,27 +461,31 @@
 def mix_kernel(slot_ref, structure_ref, weight_ref, tau_in, out_ref, tau_ref, sems):
     count, spins, parts, nvec, width = out_ref.shape
 
-    def copy(index, part):
+    half = nvec // 2
+
+    def copy(index, part, piece):
+        rows = pl.ds(piece * half, half)
         return pltpu.make_async_copy(
-            tau_in.at[slot_ref[index], :, part], tau_ref.at[index, :, part], sems.at[index, part]
+            tau_in.at[slot_ref[index], :, part, rows],
+            tau_ref.at[index, :, part, rows],
+            sems.at[index, part, piece],
         )
 
-    for index in range(count):
-        for part in range(parts):
-            copy(index, part).start()
-    for index in range(count):
+    pieces = [(index, part, piece) for index in range(count) for part in range(parts) for piece in range(2)]
+    for place in pieces:
+        copy(*place).start()
+    for index, part, piece in pieces:
         base = structure_ref[index] * spins * spins
         weight = [[weight_ref[base + r * spins + s] for s in range(spins)] for r in range(spins)]
-        for part in range(parts):
-            copy(index, part).wait()
-            for start in range(0, nvec, ROWS):
-                rows = pl.ds(start, ROWS)
-                tau = [tau_ref[index, s, part, rows, :].astype(jnp.float32) for s in range(spins)]
-                for r in range(spins):
-                    mixed = weight[r][0] * tau[0]
-                    for s in range(1, spins):
-                        mixed = mixed + weight[r][s] * tau[s]
-                    out_ref[index, r, part, rows, :] = mixed.astype(jnp.bfloat16)
+        copy(index, part, piece).wait()
+        for start in range(piece * half, (piece + 1) * half, ROWS):
+            rows = pl.ds(start, ROWS)
+            tau = [tau_ref[index, s, part, rows, :].astype(jnp.float32) for s in range(spins)]
+            for r in range(spins):
+                mixed = weight[r][0] * tau[0]
+                for s in range(1, spins):
+                    mixed = mixed + weight[r][s] * tau[s]
+                out_ref[index, r, part, rows, :] = mixed.astype(jnp.bfloat16)
 
 
 def mixed_perambulators(slots, structures, weights, perambulators):
@@ -494,7 +498,7 @@
         out_shape=jax.ShapeDtypeStruct(shape, jnp.bfloat16),
         scratch_shapes=[
             pltpu.VMEM(shape, jnp.bfloat16),
-            pltpu.SemaphoreType.DMA(shape[::2][:2]),
+            pltpu.SemaphoreType.DMA(shape[::2][:2] + (2,)),
         ],
         compiler_params=pltpu.CompilerParams(vmem_limit_bytes=8 * MIB),
         cost_estimate=pl.CostEstimate(

time: 56.6 us -> 59 us (1.042); the launches traced: 57.5 us -> 57.9 us
  no operation moved by 1% of the time
where the time goes in v5:
time: 59 us; the launch traced here: 57.9 us
  Pallas kernels  26 us (44%)
  starting transfers between devices  22.4 us (38%)
  waiting for transfers between devices  8.22 us (14%)
  other arithmetic  0.9 us (2%)
    ppermute x17, starting transfers between devices, exchanged(): return lax.ppermute(value, SITES, [(i, i ^ mask) for i in range(size)])  19.6 us
    pallas_call x1, Pallas kernels, plane_items(): pl.pallas_call(functools.partial(plane_kernel, total_z, plane, scale), gr...  15.1 us
    ppermute x17, waiting for transfers between devices, exchanged(): return lax.ppermute(value, SITES, [(i, i ^ mask) for i in range(size)])  8.22 us
    pallas_call x2, Pallas kernels, layer_items(): pl.pallas_call(functools.partial(layer_kernel, core, scale), in_specs=[pl...  5.71 us
    pallas_call x1, Pallas kernels, mixed_perambulators(): pl.pallas_call(mix_kernel, in_specs=[scalar] * 3 + [pl.BlockSpec(memory_s...  2.79 us
    ppermute x1, starting transfers between devices, shifted(): lax.ppermute(value, axis, [(i, (i + by) % size) for i in range(size)])  2.75 us
    pallas_call x1, Pallas kernels, diagrams(): pl.pallas_call(functools.partial(diagram_kernel, places), in_specs=[whole...  1.61 us
  transfers between devices with their start and end apart: 18, of which 5 were waited for; matrix products, arithmetic and copies ran while one was open for 2% of the time, Pallas kernels for 38%

profile of v5, /device:TPU:0, one launch (start us, length us, event | category | flops | bytes accessed | tf_op | source)
XLA Modules:
  0.0 57.9 jit_solution(9849156079367359453)
XLA Ops:
  0.0 2.4 %collective-permute-start = (s32[1,2,3]{2,1,0:T(2,128)}, s32[1,2,3]{2,1,0:T(2,128)S(1)}, u32[]{:S(2)}, u32[]{:S(2)}) collective-permute-start(s32[1,2,3]{2,1,0:T(2,128)} %bitcast.7), channel_id=1, source_target_pairs={{0,3},{1,2},{2,1},{3,0},{4,7},{5,6},{6,5},{7,4},{8,11},{9,10},{10,... | collective-permute-start | bytes 80 | tf_op jit(solution)/shard_map/ppermute | solution.py:34
  2.4 0.6 %collective-permute-start.1 = (s32[1,2,3]{2,1,0:T(2,128)}, s32[1,2,3]{2,1,0:T(2,128)S(1)}, u32[]{:S(2)}, u32[]{:S(2)}) collective-permute-start(s32[1,2,3]{2,1,0:T(2,128)} %bitcast.8), channel_id=1, source_target_pairs={{0,2},{1,3},{2,0},{3,1},{4,6},{5,7},{6,4},{7,5},{8,10},{9,11},{10,... | collective-permute-start | bytes 80 | tf_op jit(solution)/shard_map/ppermute | solution.py:34
  3.1 0.8 %collective-permute-done = s32[1,2,3]{2,1,0:T(2,128)S(1)} collective-permute-done((s32[1,2,3]{2,1,0:T(2,128)}, s32[1,2,3]{2,1,0:T(2,128)S(1)}, u32[]{:S(2)}, u32[]{:S(2)}) %collective-permute-start) | collective-permute-done | bytes 56 | tf_op jit(solution)/shard_map/ppermute | solution.py:34
  3.9 2.3 %collective-permute-done.1 = s32[1,2,3]{2,1,0:T(2,128)S(1)} collective-permute-done((s32[1,2,3]{2,1,0:T(2,128)}, s32[1,2,3]{2,1,0:T(2,128)S(1)}, u32[]{:S(2)}, u32[]{:S(2)}) %collective-permute-start.1) | collective-permute-done | bytes 56 | tf_op jit(solution)/shard_map/ppermute | solution.py:34
  6.2 2.7 %collective-permute-start.6 = (bf16[4,2,3,128,1,256]{5,3,2,1,0,4:T(8,128)(2,1)}, bf16[4,2,3,128,1,256]{5,3,2,1,0,4:T(8,128)(2,1)S(1)}, u32[]{:S(2)}, u32[]{:S(2)}) collective-permute-start(bf16[4,2,3,128,1,256]{5,3,2,1,0,4:T(8,128)(2,1)} %bitcast.11), channel_id=1, source_target_pairs={{0,15},{1,0},{2,1},{3,2},{4,3},{5,4},{6,5},{7,6},{8,7},{9,8},{10,9... | collective-permute-start | bytes 4718600 | tf_op jit(solution)/shard_map/ppermute | solution.py:25
  8.9 0.7 %pad_add_fusion = s32[4,2,3]{2,1,0:T(2,128)S(1)} fusion(s32[1,2,3]{2,1,0:T(2,128)S(1)} %collective-permute-done, s32[1,2,3]{2,1,0:T(2,128)S(1)} %collective-permute-done.1, s32[1,2,3]{2,1,0:T(2,128)S(1)} %collective-permute-done.2, s32[1,2,3]{2,1,0:T(2,128)} %bitcast.10), kind=kLoop, calls=%fused_computation.4 | loop fusion | flops 72 | bytes 192 | tf_op jit(solution)/shard_map/concatenate | solution.py:46
  9.6 1.4 %collective-permute-start.4 = (s32[4,2,3]{2,1,0:T(2,128)S(1)}, s32[4,2,3]{2,1,0:T(2,128)S(1)}, u32[]{:S(2)}, u32[]{:S(2)}) collective-permute-start(s32[4,2,3]{2,1,0:T(2,128)S(1)} %pad_add_fusion), channel_id=1, source_target_pairs={{0,8},{1,9},{2,10},{3,11},{4,12},{5,13},{6,14},{7,15},{8,0},{9,1},... | collective-permute-start | bytes 296 | tf_op jit(solution)/shard_map/ppermute | solution.py:34
  11.0 3.0 %collective-permute-start.5 = (s32[4,2,3]{2,1,0:T(2,128)S(1)}, s32[4,2,3]{2,1,0:T(2,128)S(1)}, u32[]{:S(2)}, u32[]{:S(2)}) collective-permute-start(s32[4,2,3]{2,1,0:T(2,128)S(1)} %pad_add_fusion), channel_id=1, source_target_pairs={{0,12},{1,13},{2,14},{3,15},{4,8},{5,9},{6,10},{7,11},{8,4},{9,5},... | collective-permute-start | bytes 296 | tf_op jit(solution)/shard_map/ppermute | solution.py:34
  14.0 15.1 %plane_items.1 = (bf16[4,4,3,272,128]{4,3,2,1,0:T(8,128)(2,1)S(1)}, f32[4,2,3,128,256]{4,3,2,1,0:T(8,128)S(1)}, f32[4,2,1,256]{3,2,1,0:T(1,128)S(1)}, f32[4,2,1,128]{3,2,1,0:T(1,128)S(1)}) custom-call(s32[1]{0:T(128)} %bitcast.1.position_ref, s32[4,3]{1,0:T(4,128)} %momenta_in.1, bf16[4,2,3,128,256]{4,3,2,1,0:T(8,128)(2,1)} %bitcast.12, ...), custom_call_target="tpu_custom_call" | custom-call | flops 3221225472 | bytes 4939776 | tf_op jit(solution)/shard_map/plane_items/pallas_call | solution.py:260
  29.2 2.3 %layer_items.3 = bf16[16,272,128]{2,1,0:T(8,128)(2,1)S(1)} custom-call(s32[16,2,3]{2,1,0:T(2,128)S(1)} %constant_dynamic-update-slice_fusion.rows_ref, bf16[4,4,3,272,128]{4,3,2,1,0:T(8,128)(2,1)S(1)} %get-tuple-element.32.item_ref, f32[4,2,3,128,256]{4,3,2,1,0:T(8,128)S(1)} %get-tuple-element.33.own_ref, bf16[4,2,3,128,256]{4,3,2,1,0:T(8,128)(2,1)S(1)} %bitcast.5, ...), custom_call_target="tpu_custom_call" | custom-call | flops 805306368 | bytes 1572864 | tf_op jit(solution)/shard_map/layer_items/pallas_call | solution.py:372
  31.6 3.4 %layer_items.2.refs_0_ = bf16[16,272,128]{2,1,0:T(8,128)(2,1)S(1)} custom-call(s32[16,2,3]{2,1,0:T(2,128)S(1)} %constant_dynamic-update-slice_fusion.rows_ref, bf16[4,4,3,272,128]{4,3,2,1,0:T(8,128)(2,1)S(1)} %get-tuple-element.32.item_ref, f32[4,2,3,128,256]{4,3,2,1,0:T(8,128)S(1)} %get-tuple-element.33.own_ref, bf16[4,2,3,128,256]{4,3,2,1,0:T(8,128)(2,1)S(1)} %bitcast.6, ...), custom_call_target="tpu_custom_call" | custom-call | flops 805306368 | bytes 1572864 | tf_op jit(solution)/shard_map/layer_items/pallas_call | solution.py:372
  35.4 1.3 %collective-permute-start.14 = (bf16[2,272,128]{2,1,0:T(8,128)(2,1)S(1)}, bf16[2,272,128]{2,1,0:T(8,128)(2,1)S(1)}, u32[]{:S(2)}, u32[]{:S(2)}) collective-permute-start(bf16[2,272,128]{2,1,0:T(8,128)(2,1)S(1)} %get-tuple-element.46), channel_id=1, source_target_pairs={{0,4},{1,5},{2,6},{3,7},{4,0},{5,1},{6,2},{7,3},{8,12},{9,13},{10,... | collective-permute-start | bytes 417800 | tf_op jit(solution)/shard_map/ppermute | solution.py:34
  36.8 1.4 %collective-permute-start.8 = (bf16[2,272,128]{2,1,0:T(8,128)(2,1)S(1)}, bf16[2,272,128]{2,1,0:T(8,128)(2,1)S(1)}, u32[]{:S(2)}, u32[]{:S(2)}) collective-permute-start(bf16[2,272,128]{2,1,0:T(8,128)(2,1)S(1)} %get-tuple-element.38), channel_id=1, source_target_pairs={{0,2},{1,3},{2,0},{3,1},{4,6},{5,7},{6,4},{7,5},{8,10},{9,11},{10,... | collective-permute-start | bytes 417800 | tf_op jit(solution)/shard_map/ppermute | solution.py:34
  38.3 1.6 %collective-permute-start.13 = (bf16[2,272,128]{2,1,0:T(8,128)(2,1)S(1)}, bf16[2,272,128]{2,1,0:T(8,128)(2,1)S(1)}, u32[]{:S(2)}, u32[]{:S(2)}) collective-permute-start(bf16[2,272,128]{2,1,0:T(8,128)(2,1)S(1)} %get-tuple-element.44), channel_id=1, source_target_pairs={{0,4},{1,5},{2,6},{3,7},{4,0},{5,1},{6,2},{7,3},{8,12},{9,13},{10,... | collective-permute-start | bytes 417800 | tf_op jit(solution)/shard_map/ppermute | solution.py:34
  39.9 1.9 %collective-permute-done.9.refs_1_ = bf16[2,272,128]{2,1,0:T(8,128)(2,1)S(1)} collective-permute-done((bf16[2,272,128]{2,1,0:T(8,128)(2,1)S(1)}, bf16[2,272,128]{2,1,0:T(8,128)(2,1)S(1)}, u32[]{:S(2)}, u32[]{:S(2)}) %collective-permute-start.9) | collective-permute-done | bytes 139296 | tf_op jit(solution)/shard_map/ppermute | solution.py:34
  42.1 2.5 %collective-permute-start.15 = (bf16[1,272,128]{2,1,0:T(8,128)(2,1)S(1)}, bf16[1,272,128]{2,1,0:T(8,128)(2,1)S(1)}, u32[]{:S(2)}, u32[]{:S(2)}) collective-permute-start(bf16[1,272,128]{2,1,0:T(8,128)(2,1)S(1)} %added.17), channel_id=1, source_target_pairs={{0,2},{1,3},{2,0},{3,1},{4,6},{5,7},{6,4},{7,5},{8,10},{9,11},{10,... | collective-permute-start | bytes 208904 | tf_op jit(solution)/shard_map/ppermute | solution.py:34
  44.8 0.7 %collective-permute-start.11 = (bf16[1,272,128]{2,1,0:T(8,128)(2,1)S(1)}, bf16[1,272,128]{2,1,0:T(8,128)(2,1)S(1)}, u32[]{:S(2)}, u32[]{:S(2)}) collective-permute-start(bf16[1,272,128]{2,1,0:T(8,128)(2,1)S(1)} %added.14), channel_id=1, source_target_pairs={{0,8},{1,9},{2,10},{3,11},{4,12},{5,13},{6,14},{7,15},{8,0},{9,1},... | collective-permute-start | bytes 208904 | tf_op jit(solution)/shard_map/ppermute | solution.py:34
  45.6 2.1 %collective-permute-start.16 = (bf16[1,272,128]{2,1,0:T(8,128)(2,1)S(1)}, bf16[1,272,128]{2,1,0:T(8,128)(2,1)S(1)}, u32[]{:S(2)}, u32[]{:S(2)}) collective-permute-start(bf16[1,272,128]{2,1,0:T(8,128)(2,1)S(1)} %added.19), channel_id=1, source_target_pairs={{0,2},{1,3},{2,0},{3,1},{4,6},{5,7},{6,4},{7,5},{8,10},{9,11},{10,... | collective-permute-start | bytes 208904 | tf_op jit(solution)/shard_map/ppermute | solution.py:34
  47.7 1.0 %collective-permute-done.10.refs_2_ = bf16[1,272,128]{2,1,0:T(8,128)(2,1)S(1)} collective-permute-done((bf16[1,272,128]{2,1,0:T(8,128)(2,1)S(1)}, bf16[1,272,128]{2,1,0:T(8,128)(2,1)S(1)}, u32[]{:S(2)}, u32[]{:S(2)}) %collective-permute-start.10) | collective-permute-done | bytes 69664 | tf_op jit(solution)/shard_map/ppermute | solution.py:34
  48.7 1.5 %collective-permute-start.12 = (bf16[1,272,128]{2,1,0:T(8,128)(2,1)S(1)}, bf16[1,272,128]{2,1,0:T(8,128)(2,1)S(1)}, u32[]{:S(2)}, u32[]{:S(2)}) collective-permute-start(bf16[1,272,128]{2,1,0:T(8,128)(2,1)S(1)} %get-tuple-element.42), channel_id=1, source_target_pairs={{0,4},{1,5},{2,6},{3,7},{4,0},{5,1},{6,2},{7,3},{8,12},{9,13},{10,... | collective-permute-start | bytes 208904 | tf_op jit(solution)/shard_map/ppermute | solution.py:34
  50.3 0.8 %collective-permute-start.17 = (bf16[1,272,128]{2,1,0:T(8,128)(2,1)S(1)}, bf16[1,272,128]{2,1,0:T(8,128)(2,1)S(1)}, u32[]{:S(2)}, u32[]{:S(2)}) collective-permute-start(bf16[1,272,128]{2,1,0:T(8,128)(2,1)S(1)} %get-tuple-element.48), channel_id=1, source_target_pairs={{0,8},{1,9},{2,10},{3,11},{4,12},{5,13},{6,14},{7,15},{8,0},{9,1},... | collective-permute-start | bytes 208904 | tf_op jit(solution)/shard_map/ppermute | solution.py:34
  51.3 2.8 %mixed_perambulators.1.refs_6_ = bf16[2,4,2,128,512]{4,3,2,1,0:T(8,128)(2,1)S(1)} custom-call(s32[2]{0:T(128)S(1)} %get-tuple-element.50.slot_ref, s32[2]{0:T(128)S(1)} %get-tuple-element.49.structure_ref, f32[256]{0:T(256)S(1)} %reshape.17.weight_ref, bf16[2,4,2,128,512]{4,3,2,1,0:T(8,128)(2,1)} %tau_in.1), custom_call_target="tpu_custom_call" | custom-call | flops 8388608 | bytes 4194304 | tf_op jit(solution)/shard_map/mixed_perambulators/pallas_call | solution.py:494
  54.1 2.2 %collective-permute-done.17.refs_5_ = bf16[1,272,128]{2,1,0:T(8,128)(2,1)S(1)} collective-permute-done((bf16[1,272,128]{2,1,0:T(8,128)(2,1)S(1)}, bf16[1,272,128]{2,1,0:T(8,128)(2,1)S(1)}, u32[]{:S(2)}, u32[]{:S(2)}) %collective-permute-start.17) | collective-permute-done | bytes 69664 | tf_op jit(solution)/shard_map/ppermute | solution.py:34
  56.3 1.6 %diagrams.1 = bf16[2,4,2,128,512]{4,3,2,1,0:T(8,128)(2,1)} custom-call(f32[1,272,128]{2,1,0:T(8,128)S(1)} %get-tuple-element.41.refs_0_, bf16[1,272,128]{2,1,0:T(8,128)(2,1)S(1)} %collective-permute-done.11.refs_1_, bf16[1,272,128]{2,1,0:T(8,128)(2,1)S(1)} %collective-permute-done.12.refs_2_, f32[1,272,128]{2,1,0:T(8,128)S(1)} %get-tuple-element.47.refs_3_, ...), custom_call_target="tpu_custom_call" | custom-call | flops 536870912 | bytes 4194304 | tf_op jit(solution)/shard_map/diagrams/pallas_call | solution.py:541
  (39 shorter events, 1.7 us)
Async XLA Ops:
  0.0 3.9 %collective-permute-start = (s32[1,2,3]{2,1,0:T(2,128)}, s32[1,2,3]{2,1,0:T(2,128)S(1)}, u32[]{:S(2)}, u32[]{:S(2)}) collective-permute-start(s32[1,2,3]{2,1,0:T(2,128)} %bitcast.7), channel_id=1, source_target_pairs={{0,3},{1,2},{2,1},{3,0},{4,7},{5,6},{6,5},{7,4},{8,11},{9,10},{10,... | collective-permute-start | bytes 80 | tf_op jit(solution)/shard_map/ppermute | solution.py:34
  2.4 3.8 %collective-permute-start.1 = (s32[1,2,3]{2,1,0:T(2,128)}, s32[1,2,3]{2,1,0:T(2,128)S(1)}, u32[]{:S(2)}, u32[]{:S(2)}) collective-permute-start(s32[1,2,3]{2,1,0:T(2,128)} %bitcast.8), channel_id=1, source_target_pairs={{0,2},{1,3},{2,0},{3,1},{4,6},{5,7},{6,4},{7,5},{8,10},{9,11},{10,... | collective-permute-start | bytes 80 | tf_op jit(solution)/shard_map/ppermute | solution.py:34
  3.0 3.2 %collective-permute-start.2 = (s32[1,2,3]{2,1,0:T(2,128)}, s32[1,2,3]{2,1,0:T(2,128)S(1)}, u32[]{:S(2)}, u32[]{:S(2)}) collective-permute-start(s32[1,2,3]{2,1,0:T(2,128)} %bitcast.9), channel_id=1, source_target_pairs={{0,1},{1,0},{2,3},{3,2},{4,5},{5,4},{6,7},{7,6},{8,9},{9,8},{10,11... | collective-permute-start | bytes 80 | tf_op jit(solution)/shard_map/ppermute | solution.py:34
  6.2 23.0 %collective-permute-start.6 = (bf16[4,2,3,128,1,256]{5,3,2,1,0,4:T(8,128)(2,1)}, bf16[4,2,3,128,1,256]{5,3,2,1,0,4:T(8,128)(2,1)S(1)}, u32[]{:S(2)}, u32[]{:S(2)}) collective-permute-start(bf16[4,2,3,128,1,256]{5,3,2,1,0,4:T(8,128)(2,1)} %bitcast.11), channel_id=1, source_target_pairs={{0,15},{1,0},{2,1},{3,2},{4,3},{5,4},{6,5},{7,6},{8,7},{9,8},{10,9... | collective-permute-start | bytes 4718600 | tf_op jit(solution)/shard_map/ppermute | solution.py:25
  9.6 19.5 %collective-permute-start.3 = (s32[4,2,3]{2,1,0:T(2,128)S(1)}, s32[4,2,3]{2,1,0:T(2,128)S(1)}, u32[]{:S(2)}, u32[]{:S(2)}) collective-permute-start(s32[4,2,3]{2,1,0:T(2,128)S(1)} %pad_add_fusion), channel_id=1, source_target_pairs={{0,4},{1,5},{2,6},{3,7},{4,0},{5,1},{6,2},{7,3},{8,12},{9,13},{10,... | collective-permute-start | bytes 296 | tf_op jit(solution)/shard_map/ppermute | solution.py:34
  9.6 19.6 %collective-permute-start.4 = (s32[4,2,3]{2,1,0:T(2,128)S(1)}, s32[4,2,3]{2,1,0:T(2,128)S(1)}, u32[]{:S(2)}, u32[]{:S(2)}) collective-permute-start(s32[4,2,3]{2,1,0:T(2,128)S(1)} %pad_add_fusion), channel_id=1, source_target_pairs={{0,8},{1,9},{2,10},{3,11},{4,12},{5,13},{6,14},{7,15},{8,0},{9,1},... | collective-permute-start | bytes 296 | tf_op jit(solution)/shard_map/ppermute | solution.py:34
  11.0 18.2 %collective-permute-start.5 = (s32[4,2,3]{2,1,0:T(2,128)S(1)}, s32[4,2,3]{2,1,0:T(2,128)S(1)}, u32[]{:S(2)}, u32[]{:S(2)}) collective-permute-start(s32[4,2,3]{2,1,0:T(2,128)S(1)} %pad_add_fusion), channel_id=1, source_target_pairs={{0,12},{1,13},{2,14},{3,15},{4,8},{5,9},{6,10},{7,11},{8,4},{9,5},... | collective-permute-start | bytes 296 | tf_op jit(solution)/shard_map/ppermute | solution.py:34
  31.6 3.5 %collective-permute-start.7 = (bf16[16,272,128]{2,1,0:T(8,128)(2,1)S(1)}, bf16[16,272,128]{2,1,0:T(8,128)(2,1)S(1)}, u32[]{:S(2)}, u32[]{:S(2)}) collective-permute-start(bf16[16,272,128]{2,1,0:T(8,128)(2,1)S(1)} %layer_items.3), channel_id=1, source_target_pairs={{0,1},{1,0},{2,3},{3,2},{4,5},{5,4},{6,7},{7,6},{8,9},{9,8},{10,11... | collective-permute-start | bytes 3342344 | tf_op jit(solution)/shard_map/ppermute | solution.py:34
  35.2 6.6 %collective-permute-start.9 = (bf16[2,272,128]{2,1,0:T(8,128)(2,1)S(1)}, bf16[2,272,128]{2,1,0:T(8,128)(2,1)S(1)}, u32[]{:S(2)}, u32[]{:S(2)}) collective-permute-start(bf16[2,272,128]{2,1,0:T(8,128)(2,1)S(1)} %get-tuple-element.40), channel_id=1, source_target_pairs={{0,2},{1,3},{2,0},{3,1},{4,6},{5,7},{6,4},{7,5},{8,10},{9,11},{10,... | collective-permute-start | bytes 417800 | tf_op jit(solution)/shard_map/ppermute | solution.py:34
  35.4 6.7 %collective-permute-start.14 = (bf16[2,272,128]{2,1,0:T(8,128)(2,1)S(1)}, bf16[2,272,128]{2,1,0:T(8,128)(2,1)S(1)}, u32[]{:S(2)}, u32[]{:S(2)}) collective-permute-start(bf16[2,272,128]{2,1,0:T(8,128)(2,1)S(1)} %get-tuple-element.46), channel_id=1, source_target_pairs={{0,4},{1,5},{2,6},{3,7},{4,0},{5,1},{6,2},{7,3},{8,12},{9,13},{10,... | collective-permute-start | bytes 417800 | tf_op jit(solution)/shard_map/ppermute | solution.py:34
  36.8 7.8 %copy-start.1 = (f32[16,4,4]{0,2,1:T(4,128)S(1)}, f32[16,4,4]{0,2,1:T(4,128)}, u32[]{:S(2)}) copy-start(f32[16,4,4]{0,2,1:T(4,128)} %param.9) | copy-start | bytes 3076
  36.8 14.3 %copy-start = (s32[2,3]{1,0:T(2,128)S(1)}, s32[2,3]{1,0:T(2,128)}, u32[]{:S(2)}) copy-start(s32[2,3]{1,0:T(2,128)} %param.11) | copy-start | bytes 76
  36.8 8.8 %collective-permute-start.8 = (bf16[2,272,128]{2,1,0:T(8,128)(2,1)S(1)}, bf16[2,272,128]{2,1,0:T(8,128)(2,1)S(1)}, u32[]{:S(2)}, u32[]{:S(2)}) collective-permute-start(bf16[2,272,128]{2,1,0:T(8,128)(2,1)S(1)} %get-tuple-element.38), channel_id=1, source_target_pairs={{0,2},{1,3},{2,0},{3,1},{4,6},{5,7},{6,4},{7,5},{8,10},{9,11},{10,... | collective-permute-start | bytes 417800 | tf_op jit(solution)/shard_map/ppermute | solution.py:34
  38.3 11.9 %collective-permute-start.13 = (bf16[2,272,128]{2,1,0:T(8,128)(2,1)S(1)}, bf16[2,272,128]{2,1,0:T(8,128)(2,1)S(1)}, u32[]{:S(2)}, u32[]{:S(2)}) collective-permute-start(bf16[2,272,128]{2,1,0:T(8,128)(2,1)S(1)} %get-tuple-element.44), channel_id=1, source_target_pairs={{0,4},{1,5},{2,6},{3,7},{4,0},{5,1},{6,2},{7,3},{8,12},{9,13},{10,... | collective-permute-start | bytes 417800 | tf_op jit(solution)/shard_map/ppermute | solution.py:34
  41.8 6.9 %collective-permute-start.10 = (bf16[1,272,128]{2,1,0:T(8,128)(2,1)S(1)}, bf16[1,272,128]{2,1,0:T(8,128)(2,1)S(1)}, u32[]{:S(2)}, u32[]{:S(2)}) collective-permute-start(bf16[1,272,128]{2,1,0:T(8,128)(2,1)S(1)} %added.12), channel_id=1, source_target_pairs={{0,8},{1,9},{2,10},{3,11},{4,12},{5,13},{6,14},{7,15},{8,0},{9,1},... | collective-permute-start | bytes 208904 | tf_op jit(solution)/shard_map/ppermute | solution.py:34
  42.1 8.2 %collective-permute-start.15 = (bf16[1,272,128]{2,1,0:T(8,128)(2,1)S(1)}, bf16[1,272,128]{2,1,0:T(8,128)(2,1)S(1)}, u32[]{:S(2)}, u32[]{:S(2)}) collective-permute-start(bf16[1,272,128]{2,1,0:T(8,128)(2,1)S(1)} %added.17), channel_id=1, source_target_pairs={{0,2},{1,3},{2,0},{3,1},{4,6},{5,7},{6,4},{7,5},{8,10},{9,11},{10,... | collective-permute-start | bytes 208904 | tf_op jit(solution)/shard_map/ppermute | solution.py:34
  44.8 9.3 %collective-permute-start.11 = (bf16[1,272,128]{2,1,0:T(8,128)(2,1)S(1)}, bf16[1,272,128]{2,1,0:T(8,128)(2,1)S(1)}, u32[]{:S(2)}, u32[]{:S(2)}) collective-permute-start(bf16[1,272,128]{2,1,0:T(8,128)(2,1)S(1)} %added.14), channel_id=1, source_target_pairs={{0,8},{1,9},{2,10},{3,11},{4,12},{5,13},{6,14},{7,15},{8,0},{9,1},... | collective-permute-start | bytes 208904 | tf_op jit(solution)/shard_map/ppermute | solution.py:34
  45.6 8.5 %collective-permute-start.16 = (bf16[1,272,128]{2,1,0:T(8,128)(2,1)S(1)}, bf16[1,272,128]{2,1,0:T(8,128)(2,1)S(1)}, u32[]{:S(2)}, u32[]{:S(2)}) collective-permute-start(bf16[1,272,128]{2,1,0:T(8,128)(2,1)S(1)} %added.19), channel_id=1, source_target_pairs={{0,2},{1,3},{2,0},{3,1},{4,6},{5,7},{6,4},{7,5},{8,10},{9,11},{10,... | collective-permute-start | bytes 208904 | tf_op jit(solution)/shard_map/ppermute | solution.py:34
  48.7 5.4 %collective-permute-start.12 = (bf16[1,272,128]{2,1,0:T(8,128)(2,1)S(1)}, bf16[1,272,128]{2,1,0:T(8,128)(2,1)S(1)}, u32[]{:S(2)}, u32[]{:S(2)}) collective-permute-start(bf16[1,272,128]{2,1,0:T(8,128)(2,1)S(1)} %get-tuple-element.42), channel_id=1, source_target_pairs={{0,4},{1,5},{2,6},{3,7},{4,0},{5,1},{6,2},{7,3},{8,12},{9,13},{10,... | collective-permute-start | bytes 208904 | tf_op jit(solution)/shard_map/ppermute | solution.py:34
  50.3 6.0 %collective-permute-start.17 = (bf16[1,272,128]{2,1,0:T(8,128)(2,1)S(1)}, bf16[1,272,128]{2,1,0:T(8,128)(2,1)S(1)}, u32[]{:S(2)}, u32[]{:S(2)}) collective-permute-start(bf16[1,272,128]{2,1,0:T(8,128)(2,1)S(1)} %get-tuple-element.48), channel_id=1, source_target_pairs={{0,8},{1,9},{2,10},{3,11},{4,12},{5,13},{6,14},{7,15},{8,0},{9,1},... | collective-permute-start | bytes 208904 | tf_op jit(solution)/shard_map/ppermute | solution.py:34
